TPU v7x, 32 devices: a whole 2x2x4 slice. The times are simulated.
32 devices in a mesh: din: 4 (over z), dout: 8 (over y, x, core).
Axes of the slice: x: 2, y: 2, z: 4, core: 2. Of those that a mesh axis runs over, the one named last changes fastest.
Arguments:
- inputs: bfloat16 [2048, 8192], P('dout', 'din'), may hold values from -6 to 6
- cotangent: bfloat16 [2048, 28672], P('din', 'dout'), may hold values from -6 to 6
- codes: int32 [2, 1024, 28672], P(None, 'din', 'dout'), may hold values from 0 to 255
- codebooks: float32 [2, 256, 8], replicated, may hold values from -6 to 6
- scales: float32 [28672], P('dout'), may hold values from 0.5 to 2
- book_mean: float32 [2, 256, 8], replicated, may hold values from -3 to 3
- book_var: float32 [2, 256, 8], replicated, may hold values from 0.1 to 1
- scale_mean: float32 [28672], P('dout'), may hold values from -3 to 3
- scale_var: float32 [28672], P('dout'), may hold values from 0.1 to 1
Outputs:
- grad_input: bfloat16 [2048, 8192], P('dout', 'din')
- book_grad: float32 [2, 256, 8], replicated
- new_books: float32 [2, 256, 8], replicated
- new_book_mean: float32 [2, 256, 8], replicated
- new_book_var: float32 [2, 256, 8], replicated
- new_scales: float32 [28672], P('dout')
- new_scale_mean: float32 [28672], P('dout')
- new_scale_var: float32 [28672], P('dout')
Inputs may be any that keep to these rules, and one draw needn't show every extreme that they name: codes[b, g, o] names the entry of codebook b used for input features 8 * g to 8 * g + 7 of output o.
All inputs are finite; a program needn't handle non-finite values.
Results may differ from a plain program's by a relative error of at most 0.0057.
Values may be sent and summed in bfloat16 or wider, within the bound.
No kernel may reach another device: no remote copies, remote signals or barrier semaphores. Data moves between devices by JAX's collectives and lax.ppermute only.
A program may use at most 128 MiB of HBM per device.

v0:
```python
import math

import jax
import jax.numpy as jnp
from jax import lax
from jax.sharding import PartitionSpec as P

DIN = 8192
DOUT = 28672
KCODE = 256
BOOKS = 2
GROUP = 8
TOKENS = 2048


beta_one = 0.9
beta_two = 0.999
adam_rate = 0.01
adam_eps = 1e-08
corr_one = 1.0 - 0.9**10
corr_two = 1.0 - 0.999**10


def adam_step(param, mean_old, var_old, gradient):
    mean_new = beta_one * mean_old + (1.0 - beta_one) * gradient
    var_new = beta_two * var_old + (1.0 - beta_two) * gradient * gradient
    update = mean_new / corr_one / (jnp.sqrt(var_new / corr_two) + adam_eps)
    return (param - adam_rate * update, mean_new, var_new)


def local(inputs, cotangent, codes, codebooks, scales, book_mean, book_var, scale_mean, scale_var):
    norm_factor = 1.0 / (2.0 * DOUT) ** 0.5
    loss_scale = (TOKENS * DIN / 4096.0) ** 0.5
    coef = scales * norm_factor
    groups_dev = codes.shape[1]
    outs_dev = codes.shape[2]
    gy_full = lax.all_gather(cotangent, "din", axis=0, tiled=True)
    x_full = lax.all_gather(inputs, "dout", axis=0, tiled=True)
    grad_w = lax.dot_general(
        x_full, gy_full, (((0,), (0,)), ((), ())), preferred_element_type=jnp.float32
    )
    grad_three = grad_w.reshape(groups_dev, GROUP, outs_dev)
    scaled = (grad_three * coef).astype(jnp.bfloat16)
    books_bf = codebooks.astype(jnp.bfloat16)
    code_iota = lax.iota(jnp.int32, KCODE)[:, None, None]
    scale_local = jnp.zeros((outs_dev,), jnp.float32)
    grad_local = jnp.zeros((BOOKS, KCODE, GROUP), jnp.float32)
    scale_total = scale_local
    grad_total = grad_local
    block_groups = math.gcd(4, groups_dev)

    def decode_block(turn_index, state_tuple):
        weight_tile, scale_run, grad_run = state_tuple
        local_first = turn_index * block_groups
        global_first = 0 + local_first
        code_block = lax.dynamic_slice_in_dim(codes, global_first, block_groups, 1)
        grad_block = lax.dynamic_slice_in_dim(grad_three, global_first, block_groups, 0)
        scaled_block = lax.dynamic_slice_in_dim(scaled, global_first, block_groups, 0)
        decoded = jnp.zeros((block_groups, GROUP, outs_dev), jnp.float32)
        book_terms = []
        for which_book in range(BOOKS):
            onehot = (code_block[which_book][None] == code_iota).astype(jnp.bfloat16)
            decoded = decoded + jnp.einsum(
                "kj,kgo->gjo", books_bf[which_book], onehot, preferred_element_type=jnp.float32
            )
            book_terms.append(
                jnp.einsum("kgo,gjo->kj", onehot, scaled_block, preferred_element_type=jnp.float32)
            )
        weight_new = (decoded * coef).astype(jnp.bfloat16)
        weight_tile = lax.dynamic_update_slice_in_dim(weight_tile, weight_new, local_first, 0)
        scale_run = scale_run + jnp.sum(decoded * grad_block, axis=(0, 1))
        grad_run = grad_run + jnp.stack(book_terms)
        return (weight_tile, scale_run, grad_run)

    start_state = (jnp.zeros((groups_dev, GROUP, outs_dev), jnp.bfloat16), scale_total, grad_total)
    weight_tile, scale_total, grad_total = lax.fori_loop(
        0, groups_dev // block_groups, decode_block, start_state
    )
    weight_flat = weight_tile.reshape(groups_dev * GROUP, outs_dev)
    grad_rows = lax.psum_scatter(
        lax.dot_general(
            gy_full, weight_flat, (((1,), (1,)), ((), ())), preferred_element_type=jnp.float32
        ),
        "dout",
        scatter_dimension=0,
        tiled=True,
    )
    grad_input = grad_rows.astype(jnp.bfloat16)
    scale_sums = lax.psum(scale_total, "din")
    grad_sums = lax.psum(grad_total, ("din", "dout"))
    book_grad = grad_sums / loss_scale
    scale_grad = scale_sums * norm_factor / loss_scale
    new_books, new_book_mean, new_book_var = adam_step(codebooks, book_mean, book_var, book_grad)
    new_scales, new_scale_mean, new_scale_var = adam_step(scales, scale_mean, scale_var, scale_grad)
    return (
        grad_input,
        book_grad,
        new_books,
        new_book_mean,
        new_book_var,
        new_scales,
        new_scale_mean,
        new_scale_var,
    )


def solution(mesh):
    in_specs = (
        P("dout", "din"),
        P("din", "dout"),
        P(None, "din", "dout"),
        P(),
        P("dout"),
        P(),
        P(),
        P("dout"),
        P("dout"),
    )
    out_specs = (P("dout", "din"), P(), P(), P(), P(), P("dout"), P("dout"), P("dout"))
    return jax.shard_map(local, mesh=mesh, in_specs=in_specs, out_specs=out_specs, check_vma=False)
```

profile of v0, /device:TPU:0, one launch (start us, length us, event | category | flops | bytes accessed | tf_op | source)
XLA Modules:
  0.0 1414.8 jit_solution(3301019142504448202)
XLA Ops:
  10.2 56.9 %all-gather.3.cloned.1.call-done = bf16[2048,2048]{1,0:T(8,128)(2,1)} async-done(((bf16[256,2048]{1,0:T(8,128)(2,1)}), bf16[2048,2048]{1,0:T(8,128)(2,1)}) %all-gather.3.cloned.1.call-update) | async-done | bytes 8388624 | tf_op jit(solution)/shard_map/all_gather | solution.py:38
  67.0 254.1 %all-gather.5.cloned.1.call-done = bf16[2048,3584]{1,0:T(8,128)(2,1)} async-done(((bf16[512,3584]{1,0:T(8,128)(2,1)}), bf16[2048,3584]{1,0:T(8,128)(2,1)}) %all-gather.5.cloned.1.call-update) | async-done | bytes 14680080 | tf_op jit(solution)/shard_map/all_gather | solution.py:37
  321.1 38.8 %multiply_convert_fusion.1 = (bf16[256,8,3584]{2,1,0:T(8,128)(2,1)}, f32[256,8,3584]{2,1,0:T(8,128)}) fusion(f32[3584]{0:T(1024)S(1)} %broadcast_multiply_fusion.1, bf16[2048,2048]{1,0:T(8,128)(2,1)} %all-gather.3.cloned.1.call-done, bf16[2048,3584]{1,0:T(8,128)(2,1)} %all-gather.5.cloned.1.call-done), kind=kOutput, calls=%fused_computation.30 | convolution fusion | flops 30079451136 | bytes 67123200 | tf_op jit(solution)/shard_map/dot_general | solution.py:39
  359.9 6.1 broadcast_in_dim.14
  366.1 886.0 %while.19 = (s32[]{:T(128)}, bf16[256,8,3584]{2,1,0:T(8,128)(2,1)}, f32[3584]{0:T(1024)S(1)}, f32[2,256,8]{1,2,0:T(8,128)S(1)}, s32[2,256,3584]{2,1,0:T(8,128)},...) while((s32[]{:T(128)}, bf16[256,8,3584]{2,1,0:T(8,128)(2,1)}, ...), condition=%wide.region_2.0_spmd.clone.clone, body=%wide.region_0.0_spmd.clone.clone.sunk | while | flops 250150400 | bytes 3588330 | solution.py:76
  394.8 3.2 fusion.44
  422.4 3.2 fusion.44
  436.3 3.2 fusion.44
  450.1 3.2 fusion.44
  464.0 3.2 fusion.44
  491.7 3.2 fusion.44
  505.5 3.2 fusion.44
  533.2 3.2 fusion.44
  560.9 3.2 fusion.44
  630.1 3.2 fusion.44
  671.6 3.2 fusion.44
  699.3 3.2 fusion.44
  713.2 3.2 fusion.44
  727.0 3.2 fusion.44
  796.2 3.2 fusion.44
  1252.1 38.4 %fusion.25 = f32[2048,2048]{0,1:T(8,128)} fusion(bf16[2048,3584]{1,0:T(8,128)(2,1)} %all-gather.5.cloned.1.call-done, bf16[256,8,3584]{2,1,0:T(8,128)(2,1)} %get-tuple-element.182), kind=kOutput, calls=%fused_computation.34 | convolution fusion | flops 30064771072 | bytes 46137344 | tf_op jit(solution)/shard_map/dot_general | solution.py:81
  1290.6 38.6 %psum.14 = f32[2,256,8]{1,2,0:T(8,128)S(1)} all-reduce(f32[2,256,8]{1,2,0:T(8,128)S(1)} %get-tuple-element.183), channel_id=1, replica_groups=mesh['din'=4,'dout'=8] {'din','dout'}, use_global_device_ids=true, to_apply=%region_4.0 | all-reduce | flops 4096 | bytes 32768 | tf_op jit(solution)/shard_map/psum | solution.py:90
  1329.3 17.6 %psum.15 = f32[3584]{0:T(1024)S(1)} all-reduce(f32[3584]{0:T(1024)S(1)} %get-tuple-element.184), channel_id=1, replica_groups=mesh['din'=4,'dout'=8] {'din'}, use_global_device_ids=true, to_apply=%region_5.0 | all-reduce | flops 3584 | bytes 28672 | tf_op jit(solution)/shard_map/psum | solution.py:89
  1348.2 57.0 %reduce-scatter.2.cloned.1.call-done = f32[256,2048]{0,1:T(8,128)} async-done(((f32[2048,2048]{0,1:T(8,128)}), f32[256,2048]{0,1:T(8,128)}) %reduce-scatter.2.cloned.1.call-update) | async-done | bytes 2097168 | tf_op jit(solution)/shard_map/reduce_scatter | solution.py:80
  (523 shorter events, 842.9 us)
Async XLA Ops:
  7.2 59.8 %all-gather.3.cloned.1.call-start = ((), (), s32[]{:S(2)}) async-start(), calls=%async_computation.1 | async-start | bytes 9437184 | tf_op jit(solution)/shard_map/all_gather | solution.py:38
  7.9 313.2 %all-gather.5.cloned.1.call-start = ((), (), s32[]{:S(2)}) async-start(), calls=%async_computation.2 | async-start | bytes 18350080 | tf_op jit(solution)/shard_map/all_gather | solution.py:37
  8.6 1396.5 %reduce-scatter.2.cloned.1.call-start = ((), (), s32[]{:S(2)}) async-start(), calls=%async_computation.3 | async-start | bytes 18874368 | tf_op jit(solution)/shard_map/reduce_scatter | solution.py:80
  1290.5 56.3 %copy-start = (f32[3584]{0:T(1024)S(1)}, f32[3584]{0:T(1024)}, u32[]{:S(2)}) copy-start(f32[3584]{0:T(1024)} %param.15) | copy-start | bytes 43012
  1290.5 56.3 %copy-start.2 = (f32[3584]{0:T(1024)S(1)}, f32[3584]{0:T(1024)}, u32[]{:S(2)}) copy-start(f32[3584]{0:T(1024)} %param.18) | copy-start | bytes 43012
  1290.6 56.3 %copy-start.3 = (f32[3584]{0:T(1024)S(1)}, f32[3584]{0:T(1024)}, u32[]{:S(2)}) copy-start(f32[3584]{0:T(1024)} %param.19) | copy-start | bytes 43012
  1290.6 57.0 %copy-start.1 = (f32[2,256,8]{1,2,0:T(8,128)S(1)}, f32[2,256,8]{1,2,0:T(8,128)}, u32[]{:S(2)}) copy-start(f32[2,256,8]{1,2,0:T(8,128)} %param.14) | copy-start | bytes 49156
  1290.6 57.0 %copy-start.4 = (f32[2,256,8]{1,2,0:T(8,128)S(1)}, f32[2,256,8]{1,2,0:T(8,128)}, u32[]{:S(2)}) copy-start(f32[2,256,8]{1,2,0:T(8,128)} %param.16) | copy-start | bytes 49156
  1290.6 56.9 %copy-start.5 = (f32[2,256,8]{1,2,0:T(8,128)S(1)}, f32[2,256,8]{1,2,0:T(8,128)}, u32[]{:S(2)}) copy-start(f32[2,256,8]{1,2,0:T(8,128)} %param.17) | copy-start | bytes 49156
Sparse Core Ops, SparseCore 0:
  9.9 57.0 all-gather.2
  68.6 252.4 all-gather.4
  1290.7 114.3 reduce-scatter.1
where the time goes:
time: 1420 us; the launch traced here: 1410 us
  matrix products  825 us (58%)
  waiting for transfers between devices  369 us (26%)
  other arithmetic  76.8 us (5%)
  local copies, waits for them, and re-layouts  70.5 us (5%)
  blocking collectives  56.2 us (4%)
    dot_general x128, matrix products, decode_block(): jnp.einsum('kgo,gjo->kj', onehot, scaled_block, preferred_element_type=jn...  410 us
    dot_general x128, matrix products, decode_block(): jnp.einsum('kj,kgo->gjo', books_bf[which_book], onehot, preferred_element...  338 us
    all_gather x1, waiting for transfers between devices, local(): gy_full = lax.all_gather(cotangent, 'din', axis=0, tiled=True)  254 us
    reduce_sum x64, other arithmetic, decode_block(): scale_run = scale_run + jnp.sum(decoded * grad_block, axis=(0, 1))  71.5 us
    eq x64, local copies, waits for them, and re-layouts, decode_block(): onehot = (code_block[which_book][None] == code_iota).astype(jnp.bfloat16)  62.9 us
    reduce_scatter x1, waiting for transfers between devices, local(): lax.psum_scatter(lax.dot_general(gy_full, weight_flat, (((1,), (1,)), (()...  57 us
    all_gather x1, waiting for transfers between devices, local(): x_full = lax.all_gather(inputs, 'dout', axis=0, tiled=True)  56.9 us
    dot_general x1, matrix products, local(): lax.dot_general(x_full, gy_full, (((0,), (0,)), ((), ())), preferred_elem...  38.8 us
  transfers between devices with their start and end apart: 3, of which 3 were waited for; matrix products, arithmetic and copies ran while one was open for 0% of the time, Pallas kernels for 0%

commit v1 on v0

v1 whole, which is shorter than its diff:
```python
import functools
import math

import jax
import jax.numpy as jnp
from jax import lax
from jax.experimental import pallas as pl
from jax.experimental.pallas import tpu as pltpu
from jax.sharding import PartitionSpec as P

DIN = 8192
DOUT = 28672
KCODE = 256
BOOKS = 2
GROUP = 8
TOKENS = 2048

LANES = 128
LOW = 8
HIGH = KCODE // LOW
VMEM = 56 * 1024 * 1024

beta_one = 0.9
beta_two = 0.999
adam_rate = 0.01
adam_eps = 1e-08
corr_one = 1.0 - 0.9**10
corr_two = 1.0 - 0.999**10


def adam_step(param, mean_old, var_old, gradient):
    mean_new = beta_one * mean_old + (1.0 - beta_one) * gradient
    var_new = beta_two * var_old + (1.0 - beta_two) * gradient * gradient
    update = mean_new / corr_one / (jnp.sqrt(var_new / corr_two) + adam_eps)
    return (param - adam_rate * update, mean_new, var_new)


def split_columns(outs):
    unit = 2 * LANES if outs % (2 * LANES) == 0 else LANES
    units = outs // unit
    last = max(1, units // 7)
    rest = units - last
    pieces = min(3, rest)
    widths = [rest // pieces + (1 if i < rest % pieces else 0) for i in range(pieces)]
    return [w * unit for w in widths if w] + [last * unit]


def largest_tile(size, limit):
    for tile in range(min(size, limit), 0, -1):
        if size % tile == 0 and tile % 8 == 0:
            return tile
    return size


def decode_kernel(tile_groups, width, first, codes_ref, table_ref, coef_ref, weight_ref):
    @pl.loop(0, tile_groups // 8)
    def _(i):
        start = pl.multiple_of(i * 8, 8)
        for q in range(width // LANES):
            cols = pl.ds(q * LANES, LANES)
            code = [codes_ref[b, pl.ds(start, 8), cols] for b in range(BOOKS)]
            coef = jnp.broadcast_to(coef_ref[:, cols], (8, LANES))
            rows = []
            for g in range(8):
                total = None
                for b in range(BOOKS):
                    c = jnp.broadcast_to(code[b][g : g + 1], (8, LANES))
                    low = c & (LANES - 1)
                    value = None
                    for part in range(KCODE // LANES):
                        got = jnp.take_along_axis(
                            table_ref[b, part], low, axis=1, mode="promise_in_bounds"
                        )
                        value = got if part == 0 else jnp.where(c < part * LANES, value, got)
                    total = value if total is None else total + value
                rows.append(total * coef)
            weight_ref[pl.ds(pl.multiple_of(i * 64, 64), 64), cols] = jnp.concatenate(
                rows, axis=0
            ).astype(jnp.bfloat16)


def decode(codes, table, coef, first, width):
    groups = codes.shape[1]
    tile_groups = largest_tile(groups, 64)
    unit = math.gcd(math.gcd(first, width), 512)
    return pl.pallas_call(
        functools.partial(decode_kernel, tile_groups, unit, first),
        grid=(width // unit, groups // tile_groups),
        in_specs=[
            pl.BlockSpec((BOOKS, tile_groups, unit), lambda o, f: (0, f, first // unit + o)),
            pl.BlockSpec(table.shape, lambda o, f: (0, 0, 0, 0)),
            pl.BlockSpec((1, unit), lambda o, f: (0, first // unit + o)),
        ],
        out_specs=pl.BlockSpec((tile_groups * GROUP, unit), lambda o, f: (f, o)),
        out_shape=jax.ShapeDtypeStruct((groups * GROUP, width), jnp.bfloat16),
        compiler_params=pltpu.CompilerParams(vmem_limit_bytes=VMEM),
        cost_estimate=pl.CostEstimate(
            flops=groups * GROUP * width * 6400, bytes_accessed=groups * width * 24, transcendentals=0
        ),
        name="decode_weights",
    )(codes, table, coef)


def piece_places(n, rows):
    places = []
    for d in range(1, (n - 1) // 2 + 1):
        places += [(-d, 0, rows), (d, 0, rows)]
    if n % 2 == 0:
        places += [(-(n // 2), 0, rows // 2), (n // 2, rows // 2, rows - rows // 2)]
    return places


def ring_pieces(own, n):
    forward = [(a, (a + 1) % n) for a in range(n)]
    backward = [((a + 1) % n, a) for a in range(n)]
    rows = own.shape[0]
    left = right = own
    pieces = []
    for _ in range(1, (n - 1) // 2 + 1):
        left = lax.ppermute(left, "din", forward)
        right = lax.ppermute(right, "din", backward)
        pieces += [left, right]
    if n % 2 == 0:
        pieces += [
            lax.ppermute(left[: rows // 2], "din", forward),
            lax.ppermute(right[rows // 2 :], "din", backward),
        ]
    return pieces


def place_pieces(me, n, rows, pieces, out_ref):
    for piece, (shift, skip, count) in zip(pieces, [(0, 0, rows)] + piece_places(n, rows)):
        chunk = lax.rem(me + shift + 2 * n, n)
        out_ref[pl.ds(pl.multiple_of(chunk * rows + skip, 16), count), :] = piece[...]


def histogram_terms(codes, scaled, width):
    spread = jnp.broadcast_to(codes[:, None, :], (8, GROUP, width)).reshape(8 * GROUP, width)
    low = (spread & (LOW - 1)).astype(jnp.bfloat16)
    zero = jnp.bfloat16(0)
    left = jnp.concatenate([jnp.where(low == jnp.bfloat16(v), scaled, zero) for v in range(LOW)], axis=0)
    iota = lax.broadcasted_iota(jnp.int32, (HIGH, width), 0).astype(jnp.bfloat16)
    hits = []
    for g in range(8):
        high = jnp.broadcast_to(codes[g : g + 1] >> 3, (16, width)).astype(jnp.bfloat16)
        for m in range(HIGH // 16):
            hits.append(jnp.where(high == iota[m * 16 : (m + 1) * 16], jnp.bfloat16(1), zero))
    return left, jnp.concatenate(hits, axis=0)


def gradient_kernel(n, tile, width, blocks, count, me_ref, codes_ref, x_ref, weight_ref, coef_ref, *refs):
    pieces, (cot_ref, book_ref, scale_ref, total_ref) = refs[:count], refs[count:]
    step = pl.program_id(0)

    @pl.when(step == 0)
    def _():
        total_ref[...] = jnp.zeros_like(total_ref)
        scale_ref[...] = jnp.zeros_like(scale_ref)
        place_pieces(me_ref[0], n, pieces[0].shape[0], pieces, cot_ref)

    x = jnp.concatenate([x_ref[e] for e in range(blocks)], axis=1) if blocks > 1 else x_ref[0]
    grads = jnp.dot(x, cot_ref[...], preferred_element_type=jnp.float32)
    scale = jnp.zeros((GROUP, width), jnp.float32)
    left, right = [[] for _ in range(BOOKS)], [[] for _ in range(BOOKS)]
    for i in range(tile // 64):
        grad = grads[i * 64 : (i + 1) * 64]
        scaled = (grad * coef_ref[...]).astype(jnp.bfloat16)
        product = grad * weight_ref[i * 64 : (i + 1) * 64, :].astype(jnp.float32)
        scale = scale + jnp.sum(product.reshape(8, GROUP, width), axis=0)
        for b in range(BOOKS):
            masked, hits = histogram_terms(codes_ref[b, i * 8 : (i + 1) * 8, :], scaled, width)
            left[b].append(masked)
            right[b].append(hits)
    scale_ref[...] += scale
    for b in range(BOOKS):
        total_ref[b] += lax.dot_general(
            jnp.concatenate(left[b], axis=1),
            jnp.concatenate(right[b], axis=1),
            (((1,), (1,)), ((), ())),
            preferred_element_type=jnp.float32,
        )

    @pl.when(step == pl.num_programs(0) - 1)
    def _():
        shape = (GROUP, 8 * HIGH)
        column = lax.broadcasted_iota(jnp.int32, shape, 1) // HIGH
        for b in range(BOOKS):
            for v in range(LOW):
                part = jnp.zeros(shape, jnp.float32)
                for g in range(8):
                    block = total_ref[b, pl.ds((v * 8 + g) * GROUP, GROUP), :]
                    part = part + jnp.where(column == g, block, 0.0)
                book_ref[b, pl.ds(v * GROUP, GROUP), :] = part


def gradients(me, n, codes, x, pieces, weights, coef, first, width):
    groups = codes.shape[1]
    blocks, features, tokens_block = x.shape
    tile_groups = largest_tile(groups, 32)
    tile = tile_groups * GROUP
    tokens = blocks * tokens_block
    place = first // width
    if first % width:
        codes = lax.slice_in_dim(codes, first, first + width, axis=2)
        coef = lax.slice_in_dim(coef, first, first + width, axis=1)
        place = 0
    once = pl.Buffered(1)
    return pl.pallas_call(
        functools.partial(gradient_kernel, n, tile, width, blocks, len(pieces)),
        grid=(groups // tile_groups,),
        in_specs=[
            pl.BlockSpec(memory_space=pltpu.SMEM),
            pl.BlockSpec((BOOKS, tile_groups, width), lambda f: (0, f, place)),
            pl.BlockSpec((blocks, tile, tokens_block), lambda f: (0, f, 0)),
            pl.BlockSpec((tile, width), lambda f: (f, 0)),
            pl.BlockSpec((1, width), lambda f: (0, place)),
        ]
        + [pl.BlockSpec(p.shape, lambda f: (0, 0), pipeline_mode=once) for p in pieces],
        out_specs=[
            pl.BlockSpec((tokens, width), lambda f: (0, 0), pipeline_mode=once),
            pl.BlockSpec((BOOKS, LOW * GROUP, 8 * HIGH), lambda f: (0, 0, 0)),
            pl.BlockSpec((GROUP, width), lambda f: (0, 0)),
        ],
        out_shape=[
            jax.ShapeDtypeStruct((tokens, width), jnp.bfloat16),
            jax.ShapeDtypeStruct((BOOKS, LOW * GROUP, 8 * HIGH), jnp.float32),
            jax.ShapeDtypeStruct((GROUP, width), jnp.float32),
        ],
        scratch_shapes=[pltpu.VMEM((BOOKS, LOW * 8 * GROUP, 8 * HIGH), jnp.float32)],
        compiler_params=pltpu.CompilerParams(vmem_limit_bytes=VMEM),
        cost_estimate=pl.CostEstimate(
            flops=3 * 2 * tokens * features * width,
            bytes_accessed=2 * (tokens + 2 * features) * width,
            transcendentals=0,
        ),
        name="weight_gradients",
    )(me, codes, x, weights, coef, *pieces)


def input_gradient_kernel(count, refs):
    left = jnp.concatenate([refs[s][...] for s in range(count)], axis=1)
    right = jnp.concatenate([refs[count + s][...] for s in range(count)], axis=1)
    return lax.dot_general(left, right, (((1,), (1,)), ((), ())), preferred_element_type=jnp.float32)


def early_kernel(count, *refs):
    refs[-1][...] = input_gradient_kernel(count, refs)


def early_input_gradient(cots, weights):
    tokens, features = cots[0].shape[0], weights[0].shape[0]
    tile_t, tile_f = largest_tile(tokens, 512), largest_tile(features, 1024)
    width = sum(c.shape[1] for c in cots)
    return pl.pallas_call(
        functools.partial(early_kernel, len(cots)),
        grid=(features // tile_f, tokens // tile_t),
        in_specs=[pl.BlockSpec((tile_t, c.shape[1]), lambda f, t: (t, 0)) for c in cots]
        + [pl.BlockSpec((tile_f, w.shape[1]), lambda f, t: (f, 0)) for w in weights],
        out_specs=pl.BlockSpec((tile_t, tile_f), lambda f, t: (t, f)),
        out_shape=jax.ShapeDtypeStruct((tokens, features), jnp.float32),
        compiler_params=pltpu.CompilerParams(vmem_limit_bytes=VMEM),
        cost_estimate=pl.CostEstimate(
            flops=2 * tokens * features * width,
            bytes_accessed=4 * tokens * features + 2 * (tokens + features) * width,
            transcendentals=0,
        ),
        name="early_input_gradient",
    )(*cots, *weights)


def last_kernel(n, rows, block, count, me_ref, early_ref, weight_ref, *refs):
    pieces, (out_ref, cot_ref) = refs[:count], refs[count:]

    @pl.when(pl.program_id(0) == 0)
    def _():
        place_pieces(me_ref[0], n, rows, pieces, cot_ref)

    start = pl.multiple_of((2 * pl.program_id(0) + me_ref[1]) * block, 16)
    part = lax.dot_general(
        cot_ref[pl.ds(start, block), :], weight_ref[...], (((1,), (1,)), ((), ())), preferred_element_type=jnp.float32
    )
    out_ref[...] = (early_ref[...] + part).astype(out_ref.dtype)


def last_input_gradient(me, n, block, pieces, weights, early, dtype):
    rows, width = pieces[0].shape
    tokens, features = early.shape
    once = pl.Buffered(1)
    half = tokens // (2 * block)
    return pl.pallas_call(
        functools.partial(last_kernel, n, rows, block, len(pieces)),
        grid_spec=pltpu.PrefetchScalarGridSpec(
            num_scalar_prefetch=1,
            grid=(half,),
            in_specs=[
                pl.BlockSpec((block, features), lambda t, who: (2 * t + who[1], 0)),
                pl.BlockSpec((features, width), lambda t, who: (0, 0), pipeline_mode=once),
            ]
            + [pl.BlockSpec(p.shape, lambda t, who: (0, 0), pipeline_mode=once) for p in pieces],
            out_specs=pl.BlockSpec((block, features), lambda t, who: (t, 0)),
            scratch_shapes=[pltpu.VMEM((tokens, width), jnp.bfloat16)],
        ),
        out_shape=jax.ShapeDtypeStruct((tokens // 2, features), dtype),
        compiler_params=pltpu.CompilerParams(vmem_limit_bytes=VMEM),
        cost_estimate=pl.CostEstimate(
            flops=tokens * features * width, bytes_accessed=3 * tokens * features, transcendentals=0
        ),
        name="last_input_gradient",
    )(me, early, weights, *pieces)


def halving_scatter(keep, got, size):
    me = lax.axis_index("dout")
    bits = size.bit_length() - 1
    tokens, features = keep.shape
    total = keep + got.astype(jnp.float32)
    if bits == 1:
        return total.astype(jnp.bfloat16)
    parts = total.reshape((2,) * (bits - 1) + (2 * tokens // size, features))

    def exchange(part, axis, bit):
        mine = (me >> bit) & 1
        held = lax.dynamic_index_in_dim(part, mine, axis, keepdims=False)
        give = lax.dynamic_index_in_dim(part, 1 - mine, axis, keepdims=False).astype(jnp.bfloat16)
        came = lax.ppermute(give, "dout", [(a, a ^ (1 << bit)) for a in range(size)])
        return held + came.astype(jnp.float32)

    half = features // 2
    one, two = parts[..., :half], parts[..., half:]
    order = list(range(1, bits))
    for step in range(bits - 1):
        up, down = order[step], order[bits - 2 - step]
        left_one = [b for b in reversed(order) if b not in order[:step]]
        left_two = [b for b in reversed(order) if b not in order[bits - 1 - step :]]
        one = exchange(one, left_one.index(up), up)
        two = exchange(two, left_two.index(down), down)
    return jnp.concatenate([one, two], axis=-1).astype(jnp.bfloat16)


def butterfly_sum(value, axis, size):
    if size & (size - 1):
        return lax.psum(value, axis)
    bit = 1
    while bit < size:
        value = value + lax.ppermute(value, axis, [(a, a ^ bit) for a in range(size)])
        bit *= 2
    return value


def local(n_din, n_dout, inputs, cotangent, codes, codebooks, scales, book_mean, book_var, scale_mean, scale_var):
    norm_factor = 1.0 / (2.0 * DOUT) ** 0.5
    loss_scale = (TOKENS * DIN / 4096.0) ** 0.5
    coef = scales * norm_factor
    outs = codes.shape[2]
    me = lax.axis_index("din").astype(jnp.int32).reshape(1)

    if inputs.shape[0] % LANES == 0:
        x = lax.all_gather(inputs.T, "dout", axis=0)
    else:
        x = lax.all_gather(inputs, "dout", axis=0, tiled=True).T[None]

    table = codebooks.astype(jnp.bfloat16).astype(jnp.float32).transpose(0, 2, 1)
    table = table.reshape(BOOKS, GROUP, KCODE // LANES, LANES).transpose(0, 2, 1, 3)
    coef_row = coef.reshape(1, outs)

    widths = split_columns(outs)
    firsts = [sum(widths[:i]) for i in range(len(widths))]
    weights, gathered = [], []
    for s, (first, width) in enumerate(zip(firsts, widths)):
        own = lax.slice_in_dim(cotangent, first, first + width, axis=1)
        if s >= 2 and n_din > 1:
            own, _ = lax.optimization_barrier((own, gathered[s - 2][1]))
        gathered.append([own] + ring_pieces(own, n_din))
        weights.append(decode(codes, table, coef_row, first, width))

    books, scale_parts, cots = [], [], []

    def run_gradients(s, after):
        row = coef_row if after is None else lax.optimization_barrier((coef_row, after))[0]
        cot, book, scale = gradients(me, n_din, codes, x, gathered[s], weights[s], row, firsts[s], widths[s])
        books.append(book)
        scale_parts.append(scale)
        cots.append(cot)

    final = len(widths) - 1
    for s in range(final):
        run_gradients(s, scale_parts[-1] if scale_parts else None)
    early = early_input_gradient(cots, weights[:final])
    block = inputs.shape[0]
    if n_dout > 1 and n_dout & (n_dout - 1) == 0:
        core = lax.axis_index("dout").astype(jnp.int32) & 1
        both_me = [jnp.stack([me[0], 1 - core]), jnp.stack([me[0], core])]
        give = last_input_gradient(both_me[0], n_din, block, gathered[final], weights[final], early, jnp.bfloat16)
        got = lax.ppermute(give, "dout", [(a, a ^ 1) for a in range(n_dout)])
        keep = last_input_gradient(both_me[1], n_din, block, gathered[final], weights[final], early, jnp.float32)
        run_gradients(final, keep[:1, :LANES])
        grad_input = halving_scatter(keep, got, n_dout)
    else:
        run_gradients(final, early[:1, :LANES])
        rows = early_input_gradient(cots, weights)
        grad_input = lax.psum_scatter(rows, "dout", scatter_dimension=0, tiled=True).astype(jnp.bfloat16)

    book = sum(books[1:], books[0]).reshape(BOOKS, LOW, GROUP, 8, HIGH).sum(axis=3)
    book = book.transpose(0, 3, 1, 2).reshape(BOOKS * KCODE * GROUP)
    scale_total = jnp.concatenate([jnp.sum(part, axis=0) for part in scale_parts]) / coef
    both = butterfly_sum(jnp.concatenate([book, scale_total]), "din", n_din)
    grad_sums = butterfly_sum(both[: book.shape[0]], "dout", n_dout).reshape(BOOKS, KCODE, GROUP)
    scale_sums = both[book.shape[0] :]

    book_grad = grad_sums / loss_scale
    scale_grad = scale_sums * norm_factor / loss_scale
    new_books, new_book_mean, new_book_var = adam_step(codebooks, book_mean, book_var, book_grad)
    new_scales, new_scale_mean, new_scale_var = adam_step(scales, scale_mean, scale_var, scale_grad)
    return (
        grad_input,
        book_grad,
        new_books,
        new_book_mean,
        new_book_var,
        new_scales,
        new_scale_mean,
        new_scale_var,
    )


def solution(mesh):
    in_specs = (
        P("dout", "din"),
        P("din", "dout"),
        P(None, "din", "dout"),
        P(),
        P("dout"),
        P(),
        P(),
        P("dout"),
        P("dout"),
    )
    out_specs = (P("dout", "din"), P(), P(), P(), P(), P("dout"), P("dout"), P("dout"))
    body = functools.partial(local, mesh.shape["din"], mesh.shape["dout"])
    return jax.shard_map(body, mesh=mesh, in_specs=in_specs, out_specs=out_specs, check_vma=False)
```

time: 1420 us -> 468 us (0.33)
  matrix products: 825 us -> 0 us
  waiting for transfers between devices: 369 us -> 58.1 us
  Pallas kernels: 0 us -> 266 us
  starting transfers between devices: 0.11 us -> 69.6 us
  other arithmetic: 76.8 us -> 17.4 us
  blocking collectives: 56.2 us -> 0 us
  local copies, waits for them, and re-layouts: 70.5 us -> 40.5 us
    dot_general x258 -> x0, matrix products: 825 us -> none  [the longest x128 410 us: decode_block(): jnp.einsum('kgo,gjo->kj', onehot, scaled_block, preferred_element_type=jn...]
    all_gather x2 -> x1, waiting for transfers between devices: 311 us -> 0.02 us  [local(): x = lax.all_gather(inputs.T, 'dout', axis=0)]
    pallas_call x0 -> x11, Pallas kernels: none -> 266 us  [the longest x4 119 us: gradients(): pl.pallas_call(functools.partial(gradient_kernel, n, tile, width, blocks,...]
    reduce_sum x64 -> x5, other arithmetic: 71.5 us -> 0.93 us  [the longest x4 0.78 us: local(): jnp.sum(part, axis=0)]
    ppermute x0 -> x26, starting transfers between devices: none -> 69.5 us  [the longest x4 24.7 us: ring_pieces(): lax.ppermute(right[rows // 2:], 'din', backward)]
    eq x64 -> x0, local copies, waits for them, and re-layouts: 62.9 us -> none  [decode_block(): onehot = (code_block[which_book][None] == code_iota).astype(jnp.bfloat16)]
    ppermute x0 -> x26, waiting for transfers between devices: none -> 57.4 us  [the longest x4 29.2 us: ring_pieces(): left = lax.ppermute(left, 'din', forward)]
    reduce_scatter x1 -> x0, waiting for transfers between devices: 57 us -> none  [local(): lax.psum_scatter(lax.dot_general(gy_full, weight_flat, (((1,), (1,)), (()...]
  transfers between devices with their start and end apart: 3 -> 27, of which waited for: 3 -> 8; matrix products, arithmetic and copies ran while one was open for 0% -> 9% of each run, Pallas kernels for 0% -> 55%
where the time goes in v1:
time: 468 us; the launch traced here: 467 us
  Pallas kernels  266 us (57%)
  starting transfers between devices  69.6 us (15%)
  waiting for transfers between devices  58.1 us (12%)
  local copies, waits for them, and re-layouts  40.5 us (9%)
  other arithmetic  17.4 us (4%)
  between operations  14.5 us (3%)
    pallas_call x4, Pallas kernels, gradients(): pl.pallas_call(functools.partial(gradient_kernel, n, tile, width, blocks,...  119 us
    pallas_call x4, Pallas kernels, decode(): pl.pallas_call(functools.partial(decode_kernel, tile_groups, unit, first)...  93.8 us
    pallas_call x1, Pallas kernels, early_input_gradient(): pl.pallas_call(functools.partial(early_kernel, len(cots)), grid=(features...  34.2 us
    ppermute x4, waiting for transfers between devices, ring_pieces(): left = lax.ppermute(left, 'din', forward)  29.2 us
    ppermute x4, starting transfers between devices, ring_pieces(): lax.ppermute(right[rows // 2:], 'din', backward)  24.7 us
    ppermute x4, starting transfers between devices, ring_pieces(): left = lax.ppermute(left, 'din', forward)  24.1 us
    pallas_call x2, Pallas kernels, last_input_gradient(): pl.pallas_call(functools.partial(last_kernel, n, rows, block, len(pieces)...  19.9 us
    ppermute x5, waiting for transfers between devices, butterfly_sum(): lax.ppermute(value, axis, [(a, a ^ bit) for a in range(size)])  19.1 us
  transfers between devices with their start and end apart: 27, of which 8 were waited for; matrix products, arithmetic and copies ran while one was open for 9% of the time, Pallas kernels for 55%

profile of v1, /device:TPU:0, one launch (start us, length us, event | category | flops | bytes accessed | tf_op | source)
XLA Modules:
  0.0 466.5 jit_solution(5170849629206874072)
XLA Ops:
  16.5 3.8 collective-permute-start.5
  22.8 26.5 %decode_weights.4.weight_ref.refs_3_ = bf16[2048,1024]{1,0:T(8,128)(2,1)} custom-call(s32[2,256,3584]{2,1,0:T(8,128)} %codes_ref.15, f32[2,2,8,128]{3,2,1,0:T(8,128)} %convert_bitcast_fusion.table_ref, f32[1,3584]{1,0:T(1,128)} %reshape.45.coef_ref), custom_call_target="tpu_custom_call" | custom-call | flops 13421772800 | bytes 6291456 | tf_op jit(solution)/shard_map/decode_weights/pallas_call | solution.py:86
  49.3 26.6 %decode_weights.5.weight_ref.refs_4_ = bf16[2048,1024]{1,0:T(8,128)(2,1)} custom-call(s32[2,256,3584]{2,1,0:T(8,128)} %codes_ref.15, f32[2,2,8,128]{3,2,1,0:T(8,128)} %convert_bitcast_fusion.table_ref, f32[1,3584]{1,0:T(1,128)} %reshape.45.coef_ref), custom_call_target="tpu_custom_call" | custom-call | flops 13421772800 | bytes 6291456 | tf_op jit(solution)/shard_map/decode_weights/pallas_call | solution.py:86
  76.0 3.8 collective-permute-start.9
  79.8 6.0 %collective-permute-done.4.refs_1_ = bf16[512,1024]{1,0:T(8,128)(2,1)} collective-permute-done((bf16[512,1024]{1,0:T(8,128)(2,1)}, bf16[512,1024]{1,0:T(8,128)(2,1)}, u32[]{:S(2)}, u32[]{:S(2)}) %collective-permute-start.4) | collective-permute-done | bytes 1048608 | tf_op jit(solution)/shard_map/ppermute | solution.py:120
  85.8 21.0 %collective-permute-start.12 = (bf16[512,512]{1,0:T(8,128)(2,1)S(1)}, bf16[512,512]{1,0:T(8,128)(2,1)S(1)}, u32[]{:S(2)}, u32[]{:S(2)}) collective-permute-start(bf16[512,512]{1,0:T(8,128)(2,1)S(1)} %slice.58.refs_0_), channel_id=1, source_target_pairs={{0,8},{8,16},{16,24},{24,0},{1,9},{9,17},{17,25},{25,1},{2,10},{10... | collective-permute-start | bytes 1572872 | tf_op jit(solution)/shard_map/ppermute | solution.py:120
  106.9 26.6 %decode_weights.6.weight_ref.refs_5_ = bf16[2048,1024]{1,0:T(8,128)(2,1)} custom-call(s32[2,256,3584]{2,1,0:T(8,128)} %codes_ref.15, f32[2,2,8,128]{3,2,1,0:T(8,128)} %convert_bitcast_fusion.table_ref, f32[1,3584]{1,0:T(1,128)} %reshape.45.coef_ref), custom_call_target="tpu_custom_call" | custom-call | flops 13421772800 | bytes 6291456 | tf_op jit(solution)/shard_map/decode_weights/pallas_call | solution.py:86
  141.2 23.2 %collective-permute-done.12.refs_1_ = bf16[512,512]{1,0:T(8,128)(2,1)S(1)} collective-permute-done((bf16[512,512]{1,0:T(8,128)(2,1)S(1)}, bf16[512,512]{1,0:T(8,128)(2,1)S(1)}, u32[]{:S(2)}, u32[]{:S(2)}) %collective-permute-start.12) | collective-permute-done | bytes 524320 | tf_op jit(solution)/shard_map/ppermute | solution.py:120
  164.5 13.1 %collective-permute-start.3 = (bf16[256,1024]{1,0:T(8,128)(2,1)}, bf16[256,1024]{1,0:T(8,128)(2,1)}, u32[]{:S(2)}, u32[]{:S(2)}) collective-permute-start(bf16[256,1024]{1,0:T(8,128)(2,1)} %slice.66), channel_id=1, source_target_pairs={{8,0},{16,8},{24,16},{0,24},{9,1},{17,9},{25,17},{1,25},{10,2},{18... | collective-permute-start | bytes 1572872 | tf_op jit(solution)/shard_map/ppermute | solution.py:126
  177.6 14.1 %decode_weights.7.weight_ref = bf16[2048,512]{1,0:T(8,128)(2,1)} custom-call(s32[2,256,3584]{2,1,0:T(8,128)} %codes_ref.15, f32[2,2,8,128]{3,2,1,0:T(8,128)} %convert_bitcast_fusion.table_ref, f32[1,3584]{1,0:T(1,128)} %reshape.45.coef_ref), custom_call_target="tpu_custom_call" | custom-call | flops 6710886400 | bytes 3145728 | tf_op jit(solution)/shard_map/decode_weights/pallas_call | solution.py:86
  201.5 12.0 %copy.39 = bf16[16384,256]{1,0:T(8,128)(2,1)} copy(bf16[16384,256]{0,1:T(8,128)(2,1)} %all-gather.3.cloned.1.call-done) | data formatting | bytes 16777216 | tf_op jit(solution)/shard_map/all_gather | solution.py:358
  213.6 3.9 collective-permute-start.15
  217.4 33.1 %weight_gradients.4 = (bf16[2048,1024]{1,0:T(8,128)(2,1)}, f32[2,64,256]{2,1,0:T(8,128)}, f32[8,1024]{1,0:T(8,128)}) custom-call(s32[1]{0:T(128)} %bitcast.me_ref, s32[2,256,3584]{2,1,0:T(8,128)} %codes_ref.15, bf16[8,2048,256]{2,1,0:T(8,128)(2,1)} %bitcast.36, bf16[2048,1024]{1,0:T(8,128)(2,1)} %decode_weights.4.weight_ref.refs_3_, ...), custom_call_target="tpu_custom_call" | custom-call | flops 25769803776 | bytes 12582912 | tf_op jit(solution)/shard_map/weight_gradients/pallas_call | solution.py:208
  250.6 4.0 collective-permute-start.11
  254.6 33.1 %weight_gradients.5 = (bf16[2048,1024]{1,0:T(8,128)(2,1)}, f32[2,64,256]{2,1,0:T(8,128)}, f32[8,1024]{1,0:T(8,128)}) custom-call(s32[1]{0:T(128)} %bitcast.me_ref, s32[2,256,3584]{2,1,0:T(8,128)} %codes_ref.15, bf16[8,2048,256]{2,1,0:T(8,128)(2,1)} %bitcast.37, bf16[2048,1024]{1,0:T(8,128)(2,1)} %decode_weights.5.weight_ref.refs_4_, ...), custom_call_target="tpu_custom_call" | custom-call | flops 25769803776 | bytes 12582912 | tf_op jit(solution)/shard_map/weight_gradients/pallas_call | solution.py:208
  289.4 33.1 %weight_gradients.6 = (bf16[2048,1024]{1,0:T(8,128)(2,1)}, f32[2,64,256]{2,1,0:T(8,128)}, f32[8,1024]{1,0:T(8,128)}) custom-call(s32[1]{0:T(128)} %bitcast.me_ref, s32[2,256,3584]{2,1,0:T(8,128)} %codes_ref.15, bf16[8,2048,256]{2,1,0:T(8,128)(2,1)} %bitcast.38, bf16[2048,1024]{1,0:T(8,128)(2,1)} %decode_weights.6.weight_ref.refs_5_, ...), custom_call_target="tpu_custom_call" | custom-call | flops 25769803776 | bytes 12582912 | tf_op jit(solution)/shard_map/weight_gradients/pallas_call | solution.py:208
  322.5 34.2 %early_input_gradient.1.early_ref = f32[2048,2048]{1,0:T(8,128)} custom-call(bf16[2048,1024]{1,0:T(8,128)(2,1)} %get-tuple-element.23.refs_0_, bf16[2048,1024]{1,0:T(8,128)(2,1)} %get-tuple-element.26.refs_1_, bf16[2048,1024]{1,0:T(8,128)(2,1)} %get-tuple-element.30.refs_2_, bf16[2048,1024]{1,0:T(8,128)(2,1)} %decode_weights.4.weight_ref.refs_3_, ...), custom_call_target="tpu_custom_call" | custom-call | flops 25769803776 | bytes 41943040 | tf_op jit(solution)/shard_map/early_input_gradient/pallas_call | solution.py:254
  358.1 9.4 %last_input_gradient.3 = bf16[1024,2048]{1,0:T(8,128)(2,1)} custom-call(s32[2]{0:T(128)} %pad_add_fusion.1.me_ref, f32[2048,2048]{1,0:T(8,128)} %early_input_gradient.1.early_ref, bf16[2048,512]{1,0:T(8,128)(2,1)} %decode_weights.7.weight_ref, bf16[512,512]{1,0:T(8,128)(2,1)} %copy-done.3, bf16[512,512]{1,0:T(8,128)(2,1)} %copy-done.4, ...), custom_call_target="tpu_custom_call" | custom-call | flops 2147483648 | bytes 12582912 | tf_op jit(solution)/shard_map/last_input_gradient/pallas_call | solution.py:290
  368.1 19.2 %weight_gradients.7 = (bf16[2048,512]{1,0:T(8,128)(2,1)}, f32[2,64,256]{2,1,0:T(8,128)}, f32[8,512]{1,0:T(8,128)}) custom-call(s32[1]{0:T(128)} %bitcast.me_ref, s32[2,256,3584]{2,1,0:T(8,128)} %codes_ref.15, bf16[8,2048,256]{2,1,0:T(8,128)(2,1)} %bitcast.39, bf16[2048,512]{1,0:T(8,128)(2,1)} %decode_weights.7.weight_ref, f32[1,3584]{1,0:T(1,128)} %reshape.45.coef_ref, ...), custom_call_target="tpu_custom_call" | custom-call | flops 12884901888 | bytes 6291456 | tf_op jit(solution)/shard_map/weight_gradients/pallas_call | solution.py:208
  388.1 10.5 %last_input_gradient.2 = f32[1024,2048]{1,0:T(8,128)} custom-call(s32[2]{0:T(128)} %pad_add_fusion.me_ref, f32[2048,2048]{1,0:T(8,128)} %early_input_gradient.1.early_ref, bf16[2048,512]{1,0:T(8,128)(2,1)} %decode_weights.7.weight_ref, bf16[512,512]{1,0:T(8,128)(2,1)} %copy-done.3, bf16[512,512]{1,0:T(8,128)(2,1)} %copy-done.4, bf16[512,512]{1,0:T(8,128)(2,1)} %copy-done.5, ...), custom_call_target="tpu_custom_call" | custom-call | flops 2147483648 | bytes 12582912 | tf_op jit(solution)/shard_map/last_input_gradient/pallas_call | solution.py:290
  398.7 5.8 %convert_add_fusion = f32[1024,2048]{1,0:T(8,128)S(1)} fusion(f32[1024,2048]{1,0:T(8,128)} %last_input_gradient.2, bf16[1024,2048]{1,0:T(8,128)(2,1)} %collective-permute-done.16), kind=kLoop, calls=%fused_computation | loop fusion | flops 4194304 | bytes 20971520 | tf_op jit(solution)/shard_map/add | solution.py:316
  415.9 4.8 %collective-permute-done.22 = f32[7680]{0:T(1024)S(1)} collective-permute-done((f32[7680]{0:T(1024)S(1)}, f32[7680]{0:T(1024)S(1)}, u32[]{:S(2)}, u32[]{:S(2)}) %collective-permute-start.22) | collective-permute-done | bytes 30752 | tf_op jit(solution)/shard_map/ppermute | solution.py:345
  423.2 12.5 %collective-permute-done.24 = f32[4096]{0:T(1024)S(1)} collective-permute-done((f32[4096]{0:T(1024)S(1)}, f32[4096]{0:T(1024)S(1)}, u32[]{:S(2)}, u32[]{:S(2)}) %collective-permute-start.24) | collective-permute-done | bytes 16416 | tf_op jit(solution)/shard_map/ppermute | solution.py:345
  447.0 7.2 %collective-permute-done.18 = bf16[256,1024]{1,0:T(8,128)(2,1)} collective-permute-done((bf16[256,1024]{1,0:T(8,128)(2,1)}, bf16[256,1024]{1,0:T(8,128)(2,1)}, u32[]{:S(2)}, u32[]{:S(2)}) %collective-permute-start.18) | collective-permute-done | bytes 524320 | tf_op jit(solution)/shard_map/ppermute | solution.py:325
  (152 shorter events, 64.2 us)
Async XLA Ops:
  7.2 194.4 %all-gather.3.cloned.1.call-start = ((), (), s32[]{:S(2)}) async-start(), calls=%async_computation | async-start | bytes 9437184 | tf_op jit(solution)/shard_map/all_gather | solution.py:358
  11.4 64.5 %collective-permute-start = (bf16[512,1024]{1,0:T(8,128)(2,1)}, bf16[512,1024]{1,0:T(8,128)(2,1)S(1)}, u32[]{:S(2)}, u32[]{:S(2)}) collective-permute-start(bf16[512,1024]{1,0:T(8,128)(2,1)} %get-tuple-element.72.refs_0_), channel_id=1, source_target_pairs={{0,8},{8,16},{16,24},{24,0},{1,9},{9,17},{17,25},{25,1},{2,10},{10... | collective-permute-start | bytes 3145736 | tf_op jit(solution)/shard_map/ppermute | solution.py:120
  14.5 121.5 %collective-permute-start.1 = (bf16[512,1024]{1,0:T(8,128)(2,1)}, bf16[512,1024]{1,0:T(8,128)(2,1)}, u32[]{:S(2)}, u32[]{:S(2)}) collective-permute-start(bf16[512,1024]{1,0:T(8,128)(2,1)} %get-tuple-element.72.refs_0_), channel_id=1, source_target_pairs={{8,0},{16,8},{24,16},{0,24},{9,1},{17,9},{25,17},{1,25},{10,2},{18... | collective-permute-start | bytes 3145736 | tf_op jit(solution)/shard_map/ppermute | solution.py:121
  16.5 69.3 %collective-permute-start.4 = (bf16[512,1024]{1,0:T(8,128)(2,1)}, bf16[512,1024]{1,0:T(8,128)(2,1)}, u32[]{:S(2)}, u32[]{:S(2)}) collective-permute-start(bf16[512,1024]{1,0:T(8,128)(2,1)} %get-tuple-element.71.refs_0_), channel_id=1, source_target_pairs={{0,8},{8,16},{16,24},{24,0},{1,9},{9,17},{17,25},{25,1},{2,10},{10... | collective-permute-start | bytes 3145736 | tf_op jit(solution)/shard_map/ppermute | solution.py:120
  16.5 124.7 %collective-permute-start.5 = (bf16[512,1024]{1,0:T(8,128)(2,1)}, bf16[512,1024]{1,0:T(8,128)(2,1)}, u32[]{:S(2)}, u32[]{:S(2)}) collective-permute-start(bf16[512,1024]{1,0:T(8,128)(2,1)} %get-tuple-element.71.refs_0_), channel_id=1, source_target_pairs={{8,0},{16,8},{24,16},{0,24},{9,1},{17,9},{25,17},{1,25},{10,2},{18... | collective-permute-start | bytes 3145736 | tf_op jit(solution)/shard_map/ppermute | solution.py:121
  75.9 119.6 %collective-permute-start.8 = (bf16[512,1024]{1,0:T(8,128)(2,1)S(1)}, bf16[512,1024]{1,0:T(8,128)(2,1)}, u32[]{:S(2)}, u32[]{:S(2)}) collective-permute-start(bf16[512,1024]{1,0:T(8,128)(2,1)S(1)} %get-tuple-element.29.refs_0_), channel_id=1, source_target_pairs={{0,8},{8,16},{16,24},{24,0},{1,9},{9,17},{17,25},{25,1},{2,10},{10... | collective-permute-start | bytes 3145736 | tf_op jit(solution)/shard_map/ppermute | solution.py:120
  76.0 124.4 %collective-permute-start.9 = (bf16[512,1024]{1,0:T(8,128)(2,1)S(1)}, bf16[512,1024]{1,0:T(8,128)(2,1)}, u32[]{:S(2)}, u32[]{:S(2)}) collective-permute-start(bf16[512,1024]{1,0:T(8,128)(2,1)S(1)} %get-tuple-element.29.refs_0_), channel_id=1, source_target_pairs={{8,0},{16,8},{24,16},{0,24},{9,1},{17,9},{25,17},{1,25},{10,2},{18... | collective-permute-start | bytes 3145736 | tf_op jit(solution)/shard_map/ppermute | solution.py:121
  85.8 78.6 %collective-permute-start.12 = (bf16[512,512]{1,0:T(8,128)(2,1)S(1)}, bf16[512,512]{1,0:T(8,128)(2,1)S(1)}, u32[]{:S(2)}, u32[]{:S(2)}) collective-permute-start(bf16[512,512]{1,0:T(8,128)(2,1)S(1)} %slice.58.refs_0_), channel_id=1, source_target_pairs={{0,8},{8,16},{16,24},{24,0},{1,9},{9,17},{17,25},{25,1},{2,10},{10... | collective-permute-start | bytes 1572872 | tf_op jit(solution)/shard_map/ppermute | solution.py:120
  135.9 58.7 %collective-permute-start.13 = (bf16[512,512]{1,0:T(8,128)(2,1)S(1)}, bf16[512,512]{1,0:T(8,128)(2,1)S(1)}, u32[]{:S(2)}, u32[]{:S(2)}) collective-permute-start(bf16[512,512]{1,0:T(8,128)(2,1)S(1)} %slice.58.refs_0_), channel_id=1, source_target_pairs={{8,0},{16,8},{24,16},{0,24},{9,1},{17,9},{25,17},{1,25},{10,2},{18... | collective-permute-start | bytes 1572872 | tf_op jit(solution)/shard_map/ppermute | solution.py:121
  141.2 72.3 %collective-permute-start.2 = (bf16[256,1024]{1,0:T(8,128)(2,1)}, bf16[256,1024]{1,0:T(8,128)(2,1)}, u32[]{:S(2)}, u32[]{:S(2)}) collective-permute-start(bf16[256,1024]{1,0:T(8,128)(2,1)} %slice.65), channel_id=1, source_target_pairs={{0,8},{8,16},{16,24},{24,0},{1,9},{9,17},{17,25},{25,1},{2,10},{10... | collective-permute-start | bytes 1572872 | tf_op jit(solution)/shard_map/ppermute | solution.py:125
  164.5 53.0 %collective-permute-start.3 = (bf16[256,1024]{1,0:T(8,128)(2,1)}, bf16[256,1024]{1,0:T(8,128)(2,1)}, u32[]{:S(2)}, u32[]{:S(2)}) collective-permute-start(bf16[256,1024]{1,0:T(8,128)(2,1)} %slice.66), channel_id=1, source_target_pairs={{8,0},{16,8},{24,16},{0,24},{9,1},{17,9},{25,17},{1,25},{10,2},{18... | collective-permute-start | bytes 1572872 | tf_op jit(solution)/shard_map/ppermute | solution.py:126
  194.6 55.9 %collective-permute-start.6 = (bf16[256,1024]{1,0:T(8,128)(2,1)}, bf16[256,1024]{1,0:T(8,128)(2,1)}, u32[]{:S(2)}, u32[]{:S(2)}) collective-permute-start(bf16[256,1024]{1,0:T(8,128)(2,1)} %slice.67), channel_id=1, source_target_pairs={{0,8},{8,16},{16,24},{24,0},{1,9},{9,17},{17,25},{25,1},{2,10},{10... | collective-permute-start | bytes 1572872 | tf_op jit(solution)/shard_map/ppermute | solution.py:125
  195.5 59.1 %collective-permute-start.7 = (bf16[256,1024]{1,0:T(8,128)(2,1)S(1)}, bf16[256,1024]{1,0:T(8,128)(2,1)}, u32[]{:S(2)}, u32[]{:S(2)}) collective-permute-start(bf16[256,1024]{1,0:T(8,128)(2,1)S(1)} %slice.68), channel_id=1, source_target_pairs={{8,0},{16,8},{24,16},{0,24},{9,1},{17,9},{25,17},{1,25},{10,2},{18... | collective-permute-start | bytes 1572872 | tf_op jit(solution)/shard_map/ppermute | solution.py:126
  200.3 156.3 %collective-permute-start.14 = (bf16[256,512]{1,0:T(8,128)(2,1)S(1)}, bf16[256,512]{1,0:T(8,128)(2,1)S(1)}, u32[]{:S(2)}, u32[]{:S(2)}) collective-permute-start(bf16[256,512]{1,0:T(8,128)(2,1)S(1)} %slice.71), channel_id=1, source_target_pairs={{0,8},{8,16},{16,24},{24,0},{1,9},{9,17},{17,25},{25,1},{2,10},{10... | collective-permute-start | bytes 786440 | tf_op jit(solution)/shard_map/ppermute | solution.py:125
  213.6 143.1 %collective-permute-start.15 = (bf16[256,512]{1,0:T(8,128)(2,1)S(1)}, bf16[256,512]{1,0:T(8,128)(2,1)S(1)}, u32[]{:S(2)}, u32[]{:S(2)}) collective-permute-start(bf16[256,512]{1,0:T(8,128)(2,1)S(1)} %copy-done.10), channel_id=1, source_target_pairs={{8,0},{16,8},{24,16},{0,24},{9,1},{17,9},{25,17},{1,25},{10,2},{18... | collective-permute-start | bytes 786440 | tf_op jit(solution)/shard_map/ppermute | solution.py:126
  217.4 70.3 %collective-permute-start.10 = (bf16[256,1024]{1,0:T(8,128)(2,1)S(1)}, bf16[256,1024]{1,0:T(8,128)(2,1)S(1)}, u32[]{:S(2)}, u32[]{:S(2)}) collective-permute-start(bf16[256,1024]{1,0:T(8,128)(2,1)S(1)} %slice.69), channel_id=1, source_target_pairs={{0,8},{8,16},{16,24},{24,0},{1,9},{9,17},{17,25},{25,1},{2,10},{10... | collective-permute-start | bytes 1572872 | tf_op jit(solution)/shard_map/ppermute | solution.py:125
  250.6 37.2 %collective-permute-start.11 = (bf16[256,1024]{1,0:T(8,128)(2,1)S(1)}, bf16[256,1024]{1,0:T(8,128)(2,1)S(1)}, u32[]{:S(2)}, u32[]{:S(2)}) collective-permute-start(bf16[256,1024]{1,0:T(8,128)(2,1)S(1)} %slice.70), channel_id=1, source_target_pairs={{8,0},{16,8},{24,16},{0,24},{9,1},{17,9},{25,17},{1,25},{10,2},{18... | collective-permute-start | bytes 1572872 | tf_op jit(solution)/shard_map/ppermute | solution.py:126
  367.4 31.3 %collective-permute-start.16 = (bf16[1024,2048]{1,0:T(8,128)(2,1)}, bf16[1024,2048]{1,0:T(8,128)(2,1)}, u32[]{:S(2)}, u32[]{:S(2)}) collective-permute-start(bf16[1024,2048]{1,0:T(8,128)(2,1)} %last_input_gradient.3), channel_id=1, source_target_pairs={{0,1},{1,0},{2,3},{3,2},{4,5},{5,4},{6,7},{7,6},{8,9},{9,8},{10,11... | collective-permute-start | bytes 12582920 | tf_op jit(solution)/shard_map/ppermute | solution.py:394
  409.6 27.6 %collective-permute-start.17 = (bf16[2,256,1024]{2,1,0:T(8,128)(2,1)S(1)}, bf16[2,256,1024]{2,1,0:T(8,128)(2,1)}, u32[]{:S(2)}, u32[]{:S(2)}) collective-permute-start(bf16[2,256,1024]{2,1,0:T(8,128)(2,1)S(1)} %fusion), channel_id=1, source_target_pairs={{0,2},{1,3},{2,0},{3,1},{4,6},{5,7},{6,4},{7,5},{8,10},{9,11},{10,... | collective-permute-start | bytes 3145736 | tf_op jit(solution)/shard_map/ppermute | solution.py:325
  413.7 27.2 %collective-permute-start.19 = (bf16[2,256,1024]{2,1,0:T(8,128)(2,1)S(1)}, bf16[2,256,1024]{2,1,0:T(8,128)(2,1)}, u32[]{:S(2)}, u32[]{:S(2)}) collective-permute-start(bf16[2,256,1024]{2,1,0:T(8,128)(2,1)S(1)} %fusion.1), channel_id=1, source_target_pairs={{0,4},{1,5},{2,6},{3,7},{4,0},{5,1},{6,2},{7,3},{8,12},{9,13},{10,... | collective-permute-start | bytes 3145736 | tf_op jit(solution)/shard_map/ppermute | solution.py:325
  422.0 13.7 %collective-permute-start.24 = (f32[4096]{0:T(1024)S(1)}, f32[4096]{0:T(1024)S(1)}, u32[]{:S(2)}, u32[]{:S(2)}) collective-permute-start(f32[4096]{0:T(1024)S(1)} %slice_add_fusion), channel_id=1, source_target_pairs={{0,2},{1,3},{2,0},{3,1},{4,6},{5,7},{6,4},{7,5},{8,10},{9,11},{10,... | collective-permute-start | bytes 49160 | tf_op jit(solution)/shard_map/ppermute | solution.py:345
  435.7 9.8 %collective-permute-start.25 = (f32[4096]{0:T(1024)S(1)}, f32[4096]{0:T(1024)S(1)}, u32[]{:S(2)}, u32[]{:S(2)}) collective-permute-start(f32[4096]{0:T(1024)S(1)} %add.99), channel_id=1, source_target_pairs={{0,4},{1,5},{2,6},{3,7},{4,0},{5,1},{6,2},{7,3},{8,12},{9,13},{10,... | collective-permute-start | bytes 49160 | tf_op jit(solution)/shard_map/ppermute | solution.py:345
  440.4 13.8 %collective-permute-start.18 = (bf16[256,1024]{1,0:T(8,128)(2,1)}, bf16[256,1024]{1,0:T(8,128)(2,1)}, u32[]{:S(2)}, u32[]{:S(2)}) collective-permute-start(bf16[256,1024]{1,0:T(8,128)(2,1)} %fusion.4), channel_id=1, source_target_pairs={{0,4},{1,5},{2,6},{3,7},{4,0},{5,1},{6,2},{7,3},{8,12},{9,13},{10,... | collective-permute-start | bytes 1572872 | tf_op jit(solution)/shard_map/ppermute | solution.py:325
  444.0 13.3 %collective-permute-start.20 = (bf16[256,1024]{1,0:T(8,128)(2,1)S(1)}, bf16[256,1024]{1,0:T(8,128)(2,1)S(1)}, u32[]{:S(2)}, u32[]{:S(2)}) collective-permute-start(bf16[256,1024]{1,0:T(8,128)(2,1)S(1)} %fusion.5), channel_id=1, source_target_pairs={{0,2},{1,3},{2,0},{3,1},{4,6},{5,7},{6,4},{7,5},{8,10},{9,11},{10,... | collective-permute-start | bytes 1572872 | tf_op jit(solution)/shard_map/ppermute | solution.py:325
  (32 other events, 454.3 us)
Sparse Core Ops, SparseCore 0:
  9.9 57.0 all-gather.2

commit v2 on v1

v2 whole, which is shorter than its diff:
```python
import functools
import math

import jax
import jax.numpy as jnp
from jax import lax
from jax.experimental import pallas as pl
from jax.experimental.pallas import tpu as pltpu
from jax.sharding import PartitionSpec as P

DIN = 8192
DOUT = 28672
KCODE = 256
BOOKS = 2
GROUP = 8
TOKENS = 2048

LANES = 128
LOW = 8
HIGH = KCODE // LOW
VMEM = 56 * 1024 * 1024

beta_one = 0.9
beta_two = 0.999
adam_rate = 0.01
adam_eps = 1e-08
corr_one = 1.0 - 0.9**10
corr_two = 1.0 - 0.999**10


def adam_step(param, mean_old, var_old, gradient):
    mean_new = beta_one * mean_old + (1.0 - beta_one) * gradient
    var_new = beta_two * var_old + (1.0 - beta_two) * gradient * gradient
    update = mean_new / corr_one / (jnp.sqrt(var_new / corr_two) + adam_eps)
    return (param - adam_rate * update, mean_new, var_new)


def split_columns(outs):
    unit = next((u for u in (4 * LANES, 2 * LANES) if outs % u == 0), LANES)
    units = outs // unit
    shares = (2, 2, 2, 1)
    ends = [round(units * sum(shares[: i + 1]) / sum(shares)) for i in range(len(shares))]
    widths = [(end - start) * unit for start, end in zip([0] + ends, ends)]
    return [width for width in widths if width]


def largest_tile(size, limit):
    for tile in range(min(size, limit), 0, -1):
        if size % tile == 0 and tile % 8 == 0:
            return tile
    return size


def packed_table(codebooks):
    rounded = codebooks.astype(jnp.bfloat16).astype(jnp.float32).transpose(0, 2, 1)
    unit = jnp.maximum(jnp.max(jnp.abs(rounded)), 1e-30) / 32767.0
    fixed = jnp.round(rounded / unit).astype(jnp.int32)
    return fixed[..., :LANES] * 65536 + (fixed[..., LANES:] & 65535), unit


def decode_kernel(tile_groups, width, codes_ref, table_ref, coef_ref, _, weight_ref):
    @pl.loop(0, tile_groups // 8)
    def _(i):
        start = pl.multiple_of(i * 8, 8)
        for q in range(width // LANES):
            cols = pl.ds(q * LANES, LANES)
            code = [codes_ref[b, pl.ds(start, 8), cols] for b in range(BOOKS)]
            coef = jnp.broadcast_to(coef_ref[:, cols], (8, LANES))
            rows = []
            for g in range(8):
                total = None
                for b in range(BOOKS):
                    c = jnp.broadcast_to(code[b][g : g + 1], (8, LANES))
                    word = jnp.take_along_axis(table_ref[b], c & (LANES - 1), axis=1, mode="promise_in_bounds")
                    value = (word << ((c & LANES) >> 3)) >> 16
                    total = value if total is None else total + value
                rows.append(total.astype(jnp.float32) * coef)
            weight_ref[pl.ds(pl.multiple_of(i * 64, 64), 64), cols] = jnp.concatenate(
                rows, axis=0
            ).astype(jnp.bfloat16)


def decode(codes, table, coef, after, first, width):
    groups = codes.shape[1]
    tile_groups = largest_tile(groups, 64)
    unit = math.gcd(math.gcd(first, width), 512)
    return pl.pallas_call(
        functools.partial(decode_kernel, tile_groups, unit),
        grid=(width // unit, groups // tile_groups),
        in_specs=[
            pl.BlockSpec((BOOKS, tile_groups, unit), lambda o, f: (0, f, first // unit + o)),
            pl.BlockSpec(table.shape, lambda o, f: (0, 0, 0)),
            pl.BlockSpec((1, unit), lambda o, f: (0, first // unit + o)),
            pl.BlockSpec(memory_space=pl.ANY),
        ],
        out_specs=pl.BlockSpec((tile_groups * GROUP, unit), lambda o, f: (f, o)),
        out_shape=jax.ShapeDtypeStruct((groups * GROUP, width), jnp.bfloat16),
        compiler_params=pltpu.CompilerParams(vmem_limit_bytes=VMEM),
        cost_estimate=pl.CostEstimate(
            flops=groups * GROUP * width * 9000, bytes_accessed=groups * width * 24, transcendentals=0
        ),
        name="decode_weights",
    )(codes, table, coef, after)


def piece_places(n, rows):
    places = []
    for d in range(1, (n - 1) // 2 + 1):
        places += [(-d, 0, rows), (d, 0, rows)]
    if n % 2 == 0:
        places += [(-(n // 2), 0, rows // 2), (n // 2, rows // 2, rows - rows // 2)]
    return places


class Ring:
    def __init__(self, n, rows):
        self.n, self.rows = n, rows
        self.forward = [(a, (a + 1) % n) for a in range(n)]
        self.backward = [((a + 1) % n, a) for a in range(n)]

    def begin(self, own):
        self.pieces = [own]
        self.left = self.right = own
        for _ in range(1, (self.n - 1) // 2 + 1):
            self.left = lax.ppermute(self.left, "din", self.forward)
            self.right = lax.ppermute(self.right, "din", self.backward)
            self.pieces += [self.left, self.right]

    def hold(self, gate):
        first = len(self.pieces) > 1
        held, gate = lax.optimization_barrier((self.pieces, gate))
        self.pieces = list(held)
        if first:
            self.left, self.right = self.pieces[-2:]
        return gate

    def finish(self, following):
        if self.n % 2 == 0:
            half = self.rows // 2
            halves, following = lax.optimization_barrier(((self.left[:half], self.right[half:]), following))
            self.pieces += [
                lax.ppermute(halves[0], "din", self.forward),
                lax.ppermute(halves[1], "din", self.backward),
            ]
        return following


def transpose_kernel(in_ref, out_ref):
    out_ref[...] = in_ref[...].T


def transpose(block):
    rows, columns = block.shape
    tile = largest_tile(columns, 512)
    return pl.pallas_call(
        transpose_kernel,
        grid=(columns // tile,),
        in_specs=[pl.BlockSpec((rows, tile), lambda c: (0, c))],
        out_specs=pl.BlockSpec((tile, rows), lambda c: (c, 0)),
        out_shape=jax.ShapeDtypeStruct((columns, rows), block.dtype),
        name="transpose_inputs",
    )(block)


def place_pieces(me, n, rows, pieces, out_ref):
    for piece, (shift, skip, count) in zip(pieces, [(0, 0, rows)] + piece_places(n, rows)):
        chunk = lax.rem(me + shift + 2 * n, n)
        out_ref[pl.ds(pl.multiple_of(chunk * rows + skip, 16), count), :] = piece[...]


def histogram_terms(codes, scaled, width):
    spread = jnp.broadcast_to(codes[:, None, :], (8, GROUP, width)).reshape(8 * GROUP, width)
    low = (spread & (LOW - 1)).astype(jnp.bfloat16)
    zero = jnp.bfloat16(0)
    left = jnp.concatenate([jnp.where(low == jnp.bfloat16(v), scaled, zero) for v in range(LOW)], axis=0)
    iota = lax.broadcasted_iota(jnp.int32, (HIGH, width), 0).astype(jnp.bfloat16)
    hits = []
    for g in range(8):
        high = jnp.broadcast_to(codes[g : g + 1] >> 3, (16, width)).astype(jnp.bfloat16)
        for m in range(HIGH // 16):
            hits.append(jnp.where(high == iota[m * 16 : (m + 1) * 16], jnp.bfloat16(1), zero))
    return left, jnp.concatenate(hits, axis=0)


def gradient_kernel(n, tile, width, blocks, count, parts, me_ref, x_ref, weight_ref, _, *refs):
    code_refs, coef_refs, refs = refs[:parts], refs[parts : 2 * parts], refs[2 * parts :]
    pieces, (cot_ref, book_ref, scale_ref, total_ref) = refs[:count], refs[count:]
    step = pl.program_id(0)

    @pl.when(step == 0)
    def _():
        total_ref[...] = jnp.zeros_like(total_ref)
        scale_ref[...] = jnp.zeros_like(scale_ref)
        place_pieces(me_ref[0], n, pieces[0].shape[0], pieces, cot_ref)

    x = jnp.concatenate([x_ref[e] for e in range(blocks)], axis=1) if blocks > 1 else x_ref[0]
    grads = jnp.dot(x, cot_ref[...], preferred_element_type=jnp.float32)
    coef = jnp.concatenate([ref[...] for ref in coef_refs], axis=1)
    scale = jnp.zeros((GROUP, width), jnp.float32)
    left, right = [[] for _ in range(BOOKS)], [[] for _ in range(BOOKS)]
    for i in range(tile // 64):
        grad = grads[i * 64 : (i + 1) * 64]
        scaled = (grad * coef).astype(jnp.bfloat16)
        product = grad * weight_ref[i * 64 : (i + 1) * 64, :].astype(jnp.float32)
        scale = scale + jnp.sum(product.reshape(8, GROUP, width), axis=0)
        for b in range(BOOKS):
            codes = jnp.concatenate([ref[b, i * 8 : (i + 1) * 8, :] for ref in code_refs], axis=1)
            masked, hits = histogram_terms(codes, scaled, width)
            left[b].append(masked)
            right[b].append(hits)
    scale_ref[...] += scale
    for b in range(BOOKS):
        total_ref[b] += lax.dot_general(
            jnp.concatenate(left[b], axis=1),
            jnp.concatenate(right[b], axis=1),
            (((1,), (1,)), ((), ())),
            preferred_element_type=jnp.float32,
        )

    @pl.when(step == pl.num_programs(0) - 1)
    def _():
        shape = (GROUP, 8 * HIGH)
        column = lax.broadcasted_iota(jnp.int32, shape, 1) // HIGH
        for b in range(BOOKS):
            for v in range(LOW):
                part = jnp.zeros(shape, jnp.float32)
                for g in range(8):
                    block = total_ref[b, pl.ds((v * 8 + g) * GROUP, GROUP), :]
                    part = part + jnp.where(column == g, block, 0.0)
                book_ref[b, pl.ds(v * GROUP, GROUP), :] = part


def gradients(me, n, codes, x, pieces, weights, coef, after, first, width):
    groups = codes.shape[1]
    blocks, features, tokens_block = x.shape
    tile_groups = largest_tile(groups, 32)
    tile = tile_groups * GROUP
    tokens = blocks * tokens_block
    unit = math.gcd(first, width)
    parts = width // unit
    places = [first // unit + p for p in range(parts)]
    once = pl.Buffered(1)
    return pl.pallas_call(
        functools.partial(gradient_kernel, n, tile, width, blocks, len(pieces), parts),
        grid=(groups // tile_groups,),
        in_specs=[
            pl.BlockSpec(memory_space=pltpu.SMEM),
            pl.BlockSpec((blocks, tile, tokens_block), lambda f: (0, f, 0)),
            pl.BlockSpec((tile, width), lambda f: (f, 0)),
            pl.BlockSpec(memory_space=pl.ANY),
        ]
        + [pl.BlockSpec((BOOKS, tile_groups, unit), lambda f, p=p: (0, f, p)) for p in places]
        + [pl.BlockSpec((1, unit), lambda f, p=p: (0, p)) for p in places]
        + [pl.BlockSpec(p.shape, lambda f: (0, 0), pipeline_mode=once) for p in pieces],
        out_specs=[
            pl.BlockSpec((tokens, width), lambda f: (0, 0), pipeline_mode=once),
            pl.BlockSpec((BOOKS, LOW * GROUP, 8 * HIGH), lambda f: (0, 0, 0)),
            pl.BlockSpec((GROUP, width), lambda f: (0, 0)),
        ],
        out_shape=[
            jax.ShapeDtypeStruct((tokens, width), jnp.bfloat16),
            jax.ShapeDtypeStruct((BOOKS, LOW * GROUP, 8 * HIGH), jnp.float32),
            jax.ShapeDtypeStruct((GROUP, width), jnp.float32),
        ],
        scratch_shapes=[pltpu.VMEM((BOOKS, LOW * 8 * GROUP, 8 * HIGH), jnp.float32)],
        compiler_params=pltpu.CompilerParams(vmem_limit_bytes=VMEM),
        cost_estimate=pl.CostEstimate(
            flops=9 * tokens * features * width,
            bytes_accessed=2 * (tokens + 2 * features) * width,
            transcendentals=0,
        ),
        name="weight_gradients",
    )(me, x, weights, after, *([codes] * parts), *([coef] * parts), *pieces)


def input_gradient_kernel(count, refs):
    left = jnp.concatenate([refs[s][...] for s in range(count)], axis=1)
    right = jnp.concatenate([refs[count + s][...] for s in range(count)], axis=1)
    return lax.dot_general(left, right, (((1,), (1,)), ((), ())), preferred_element_type=jnp.float32)


def early_kernel(count, added, *refs):
    total = input_gradient_kernel(count, refs)
    refs[-1][...] = refs[2 * count][...] + total if added else total


def early_input_gradient(cots, weights, total, after):
    tokens, features = cots[0].shape[0], weights[0].shape[0]
    tile_t, tile_f = largest_tile(tokens, 512), largest_tile(features, 1024)
    width = sum(c.shape[1] for c in cots)
    out_spec = pl.BlockSpec((tile_t, tile_f), lambda f, t: (t, f))
    args = [*cots, *weights] + ([] if total is None else [total]) + [after]
    return pl.pallas_call(
        functools.partial(early_kernel, len(cots), total is not None),
        grid=(features // tile_f, tokens // tile_t),
        in_specs=[pl.BlockSpec((tile_t, c.shape[1]), lambda f, t: (t, 0)) for c in cots]
        + [pl.BlockSpec((tile_f, w.shape[1]), lambda f, t: (f, 0)) for w in weights]
        + ([] if total is None else [out_spec])
        + [pl.BlockSpec(memory_space=pl.ANY)],
        out_specs=out_spec,
        out_shape=jax.ShapeDtypeStruct((tokens, features), jnp.float32),
        input_output_aliases={} if total is None else {2 * len(cots): 0},
        compiler_params=pltpu.CompilerParams(vmem_limit_bytes=VMEM),
        cost_estimate=pl.CostEstimate(
            flops=3 * tokens * features * width,
            bytes_accessed=4 * tokens * features + 2 * (tokens + features) * width,
            transcendentals=0,
        ),
        name="early_input_gradient",
    )(*args)


def last_kernel(n, rows, block, fulls, count, me_ref, early_ref, *refs):
    cots, weights, refs = refs[:fulls], refs[fulls : 2 * fulls + 1], refs[2 * fulls + 1 :]
    pieces, (one_ref, two_ref, cot_ref) = refs[:count], refs[count:]

    @pl.when(pl.program_id(0) == 0)
    def _():
        place_pieces(me_ref[0], n, rows, pieces, cot_ref)

    start = pl.multiple_of((2 * pl.program_id(0) + me_ref[1]) * block, 16)
    left = jnp.concatenate([ref[...] for ref in cots] + [cot_ref[pl.ds(start, block), :]], axis=1)
    half = one_ref.shape[1]
    for out_ref, columns in ((one_ref, slice(0, half)), (two_ref, slice(half, 2 * half))):
        right = jnp.concatenate([ref[columns, :] for ref in weights], axis=1)
        part = lax.dot_general(left, right, (((1,), (1,)), ((), ())), preferred_element_type=jnp.float32)
        out_ref[...] = (early_ref[:, columns] + part).astype(out_ref.dtype)


def last_input_gradient(me, n, block, cots, pieces, weights, early, dtype):
    rows = pieces[0].shape[0]
    tokens, features = early.shape
    once = pl.Buffered(1)
    half = tokens // (2 * block)
    width = sum(w.shape[1] for w in weights)
    return pl.pallas_call(
        functools.partial(last_kernel, n, rows, block, len(cots), len(pieces)),
        grid_spec=pltpu.PrefetchScalarGridSpec(
            num_scalar_prefetch=1,
            grid=(half,),
            in_specs=[pl.BlockSpec((block, features), lambda t, who: (2 * t + who[1], 0))]
            + [pl.BlockSpec((block, c.shape[1]), lambda t, who: (2 * t + who[1], 0)) for c in cots]
            + [pl.BlockSpec(w.shape, lambda t, who: (0, 0), pipeline_mode=once) for w in weights]
            + [pl.BlockSpec(p.shape, lambda t, who: (0, 0), pipeline_mode=once) for p in pieces],
            out_specs=[pl.BlockSpec((block, features // 2), lambda t, who: (t, 0))] * 2,
            scratch_shapes=[pltpu.VMEM((tokens, pieces[0].shape[1]), jnp.bfloat16)],
        ),
        out_shape=[jax.ShapeDtypeStruct((tokens // 2, features // 2), dtype)] * 2,
        compiler_params=pltpu.CompilerParams(vmem_limit_bytes=VMEM),
        cost_estimate=pl.CostEstimate(
            flops=2 * tokens * features * width, bytes_accessed=3 * tokens * features, transcendentals=0
        ),
        name="last_input_gradient",
    )(me, early, *cots, *weights, *pieces)


class HalvingScatter:
    def __init__(self, terms, size):
        self.size = size
        self.me = lax.axis_index("dout")
        self.order = list(range(1, size.bit_length() - 1))
        self.step = 0
        rows = 2 * terms[0][0].shape[0] // size
        shape = (2,) * len(self.order) + (rows, terms[0][0].shape[1])
        self.terms = [[t.reshape(shape) for t in half] for half in terms]

    @staticmethod
    def total(terms):
        return sum((t.astype(jnp.float32) for t in terms[1:]), terms[0].astype(jnp.float32))

    def exchange(self, gate=None):
        gives, helds = [], []
        for which in range(2):
            axis, bit = self.place(which)
            mine = (self.me >> bit) & 1
            terms = self.terms[which]
            helds.append([lax.dynamic_index_in_dim(t, mine, axis, keepdims=False) for t in terms])
            give = self.total([lax.dynamic_index_in_dim(t, 1 - mine, axis, keepdims=False) for t in terms])
            gives.append(give.astype(jnp.bfloat16))
        if gate is not None:
            gives, gate = lax.optimization_barrier((gives, gate))
        for which in range(2):
            bit = self.place(which)[1]
            came = lax.ppermute(gives[which], "dout", [(a, a ^ (1 << bit)) for a in range(self.size)])
            self.terms[which] = helds[which] + [came]
        self.step += 1
        return gives if gate is None else gate

    def place(self, which):
        order = self.order if which == 0 else self.order[::-1]
        left = [b for b in reversed(self.order) if b not in order[: self.step]]
        return left.index(order[self.step]), order[self.step]

    def finish(self, gate):
        while self.step < len(self.order):
            gate = self.exchange(gate)
        return jnp.concatenate([self.total(t) for t in self.terms], axis=-1).astype(jnp.bfloat16), gate


def butterfly_sum(value, axis, size):
    if size & (size - 1):
        return lax.psum(value, axis)

    def other(bits):
        return lax.ppermute(value, axis, [(a, a ^ bits) for a in range(size)])

    bit = 1
    while bit < size:
        if 2 * bit < size:
            near, far, both = other(bit), other(2 * bit), other(3 * bit)
            value = (value + near) + (far + both)
            bit *= 4
        else:
            value = value + other(bit)
            bit *= 2
    return value


def local(n_din, n_dout, inputs, cotangent, codes, codebooks, scales, book_mean, book_var, scale_mean, scale_var):
    norm_factor = 1.0 / (2.0 * DOUT) ** 0.5
    loss_scale = (TOKENS * DIN / 4096.0) ** 0.5
    coef = scales * norm_factor
    outs = codes.shape[2]
    me = lax.axis_index("din").astype(jnp.int32).reshape(1)

    if inputs.shape[0] % LANES == 0:
        x = lax.all_gather(transpose(inputs), "dout", axis=0, tiled=True).reshape(n_dout, inputs.shape[1], inputs.shape[0])
    else:
        x = lax.all_gather(inputs, "dout", axis=0, tiled=True).T[None]

    table, unit = packed_table(codebooks)
    coef_row = coef.reshape(1, outs)
    unit_row = coef_row * unit

    widths = split_columns(outs)
    firsts = [sum(widths[:i]) for i in range(len(widths))]
    final = len(widths) - 1
    owns = [lax.slice_in_dim(cotangent, f, f + w, axis=1) for f, w in zip(firsts, widths)]
    rings = [Ring(n_din, own.shape[0]) for own in owns]
    weights = [None] * len(widths)
    books, scale_parts, cots = [], [], []

    def run_decode(s, after):
        weights[s] = decode(codes, table, unit_row, after, firsts[s], widths[s])

    def run_gradients(s, after):
        cot, book, scale = gradients(
            me, n_din, codes, x, rings[s].pieces, weights[s], coef_row, after, firsts[s], widths[s]
        )
        cots.append(cot)
        books.append(book)
        scale_parts.append(scale)
        return scale

    rings[0].begin(owns[0])
    for s in range(min(2, final + 1)):
        run_decode(s, coef_row)
    early, summed, gate = None, 0, weights[min(1, final)]
    for s in range(final + 1):
        gate = rings[s].hold(gate)
        if s == 0:
            weights[min(1, final)] = gate
        gate = rings[s].finish(gate)
        if s == 0 and final >= 2:
            run_decode(2, gate)
            gate = weights[2]
        if 0 < s < max(2, final):
            early = early_input_gradient(cots[summed:], weights[summed:s], early, gate)
            summed, gate = s, early
        if s < final:
            gate = rings[s].hold(gate)
            owns[s + 1], gate = lax.optimization_barrier((owns[s + 1], gate))
            if s > 0:
                early = gate
            elif final >= 2:
                weights[2] = gate
            rings[s + 1].begin(owns[s + 1])
            gate = run_gradients(s, gate)
            if s == 0:
                for later in range(3, final + 1):
                    run_decode(later, gate)
                    gate = weights[later]

    block = inputs.shape[0]
    if early is not None and n_dout > 1 and n_dout & (n_dout - 1) == 0:
        core = lax.axis_index("dout").astype(jnp.int32) & 1
        both_me = [jnp.stack([me[0], 1 - core]), jnp.stack([me[0], core])]
        pieces = rings[final].pieces
        rest = (n_din, block, cots[summed:], pieces, weights[summed:], early)
        give = last_input_gradient(both_me[0], *rest, jnp.bfloat16)
        got = [lax.ppermute(half, "dout", [(a, a ^ 1) for a in range(n_dout)]) for half in give]
        keep = last_input_gradient(both_me[1], *rest, jnp.float32)
        scatter = HalvingScatter([[k, g] for k, g in zip(keep, got)], n_dout)
        gate = keep[0]
        if n_dout > 2:
            gate = lax.optimization_barrier(scatter.exchange())[0]
        run_gradients(final, gate)
        grad_input, books[-1] = scatter.finish(books[-1])
    else:
        run_gradients(final, gate)
        rows = early_input_gradient(cots, weights, None, gate)
        grad_input = lax.psum_scatter(rows, "dout", scatter_dimension=0, tiled=True).astype(jnp.bfloat16)

    book = sum(books[1:], books[0]).reshape(BOOKS, LOW, GROUP, 8, HIGH).sum(axis=3)
    book = book.transpose(0, 3, 1, 2).reshape(BOOKS * KCODE * GROUP)
    scale_total = jnp.concatenate([jnp.sum(part, axis=0) for part in scale_parts]) / coef
    both = butterfly_sum(jnp.concatenate([book, scale_total]), "din", n_din)
    grad_sums = butterfly_sum(both[: book.shape[0]], "dout", n_dout).reshape(BOOKS, KCODE, GROUP)
    scale_sums = both[book.shape[0] :]

    book_grad = grad_sums / loss_scale
    scale_grad = scale_sums * norm_factor / loss_scale
    new_books, new_book_mean, new_book_var = adam_step(codebooks, book_mean, book_var, book_grad)
    new_scales, new_scale_mean, new_scale_var = adam_step(scales, scale_mean, scale_var, scale_grad)
    return (
        grad_input,
        book_grad,
        new_books,
        new_book_mean,
        new_book_var,
        new_scales,
        new_scale_mean,
        new_scale_var,
    )


def solution(mesh):
    in_specs = (
        P("dout", "din"),
        P("din", "dout"),
        P(None, "din", "dout"),
        P(),
        P("dout"),
        P(),
        P(),
        P("dout"),
        P("dout"),
    )
    out_specs = (P("dout", "din"), P(), P(), P(), P(), P("dout"), P("dout"), P("dout"))
    body = functools.partial(local, mesh.shape["din"], mesh.shape["dout"])
    return jax.shard_map(body, mesh=mesh, in_specs=in_specs, out_specs=out_specs, check_vma=False)
```

time: 468 us -> 390 us (0.83)
  local copies, waits for them, and re-layouts: 40.5 us -> 11.2 us
  starting transfers between devices: 69.6 us -> 45.1 us
  Pallas kernels: 266 us -> 253 us
  waiting for transfers between devices: 58.1 us -> 46.1 us
    ppermute x26 -> x29, starting transfers between devices: 69.5 us -> 45 us  [the longest x4 13.5 us: finish(): lax.ppermute(halves[1], 'din', self.backward)]
    pallas_call x7 -> x9, Pallas kernels: 148 us -> 134 us  [the longest x4 64.8 us: decode(): pl.pallas_call(functools.partial(decode_kernel, tile_groups, unit), grid=...]
    all_gather x1 -> x0, local copies, waits for them, and re-layouts: 12 us -> none  [local(): x = lax.all_gather(inputs.T, 'dout', axis=0)]
    ppermute x26 -> x29, waiting for transfers between devices: 57.4 us -> 46.1 us  [the longest x4 15 us: begin(): self.right = lax.ppermute(self.right, 'din', self.backward)]
    slice x11 -> x10, local copies, waits for them, and re-layouts: 17.2 us -> 7.42 us  [the longest x2 4.05 us: local(): lax.slice_in_dim(cotangent, f, f + w, axis=1)]
    convert_element_type x0 -> x5, other arithmetic: none -> 9.73 us  [the longest x4 9.73 us: exchange(): gives.append(give.astype(jnp.bfloat16))]
    add x7 -> x3, other arithmetic: 9.75 us -> 0.63 us  [the longest x1 0.61 us: packed_table(): return (fixed[..., :LANES] * 65536 + (fixed[..., LANES:] & 65535), unit)]
    unnamed x59 -> x69, local copies, waits for them, and re-layouts: 6.53 us -> 1.38 us
  transfers between devices with their start and end apart: 27 -> 30, of which waited for: 8 -> 13; matrix products, arithmetic and copies ran while one was open for 9% -> 5% of each run, Pallas kernels for 55% -> 61%
where the time goes in v2:
time: 390 us; the launch traced here: 389 us
  Pallas kernels  253 us (65%)
  waiting for transfers between devices  46.1 us (12%)
  starting transfers between devices  45.1 us (12%)
  other arithmetic  18.4 us (5%)
  between operations  15.2 us (4%)
  local copies, waits for them, and re-layouts  11.2 us (3%)
    pallas_call x4, Pallas kernels, gradients(): pl.pallas_call(functools.partial(gradient_kernel, n, tile, width, blocks,...  119 us
    pallas_call x4, Pallas kernels, decode(): pl.pallas_call(functools.partial(decode_kernel, tile_groups, unit), grid=...  64.8 us
    pallas_call x2, Pallas kernels, early_input_gradient(): pl.pallas_call(functools.partial(early_kernel, len(cots), total is not No...  38.7 us
    pallas_call x2, Pallas kernels, last_input_gradient(): pl.pallas_call(functools.partial(last_kernel, n, rows, block, len(cots),...  27.1 us
    ppermute x4, waiting for transfers between devices, begin(): self.right = lax.ppermute(self.right, 'din', self.backward)  15 us
    ppermute x7, waiting for transfers between devices, other(): return lax.ppermute(value, axis, [(a, a ^ bits) for a in range(size)])  14.6 us
    ppermute x4, starting transfers between devices, finish(): lax.ppermute(halves[1], 'din', self.backward)  13.5 us
    ppermute x4, starting transfers between devices, begin(): self.right = lax.ppermute(self.right, 'din', self.backward)  10.6 us
  transfers between devices with their start and end apart: 30, of which 13 were waited for; matrix products, arithmetic and copies ran while one was open for 5% of the time, Pallas kernels for 61%

profile of v2, /device:TPU:0, one launch (start us, length us, event | category | flops | bytes accessed | tf_op | source)
XLA Modules:
  0.0 388.8 jit_solution(8051183112096652172)
XLA Ops:
  7.2 3.6 transpose_inputs.1
  13.0 3.1 collective-permute-start
  23.2 18.3 %decode_weights.4._.weight_ref.refs_1_ = bf16[2048,1024]{1,0:T(8,128)(2,1)} custom-call(s32[2,256,3584]{2,1,0:T(8,128)} %refs_0_.7, s32[2,8,128]{2,1,0:T(8,128)} %fusion.12.table_ref, f32[1,3584]{1,0:T(1,128)} %mul.97.coef_ref, f32[1,3584]{1,0:T(1,128)} %reshape.87._.refs_1_), custom_call_target="tpu_custom_call" | custom-call | flops 18874368000 | bytes 6291456 | tf_op jit(solution)/shard_map/decode_weights/pallas_call | solution.py:87
  41.5 18.4 %decode_weights.6.weight_ref.refs_1_ = bf16[2048,1024]{1,0:T(8,128)(2,1)} custom-call(s32[2,256,3584]{2,1,0:T(8,128)} %refs_0_.7, s32[2,8,128]{2,1,0:T(8,128)} %fusion.12.table_ref, f32[1,3584]{1,0:T(1,128)} %mul.97.coef_ref, f32[1,3584]{1,0:T(1,128)} %reshape.87._.refs_1_), custom_call_target="tpu_custom_call" | custom-call | flops 18874368000 | bytes 6291456 | tf_op jit(solution)/shard_map/decode_weights/pallas_call | solution.py:87
  59.9 3.5 collective-permute-done.1.refs_4_
  69.4 18.2 %decode_weights.5._.weight_ref.refs_1_ = bf16[2048,1024]{1,0:T(8,128)(2,1)} custom-call(s32[2,256,3584]{2,1,0:T(8,128)} %refs_0_.7, s32[2,8,128]{2,1,0:T(8,128)} %fusion.12.table_ref, f32[1,3584]{1,0:T(1,128)} %mul.97.coef_ref, bf16[2048,1024]{1,0:T(8,128)(2,1)} %decode_weights.4._.weight_ref.refs_1_), custom_call_target="tpu_custom_call" | custom-call | flops 18874368000 | bytes 6291456 | tf_op jit(solution)/shard_map/decode_weights/pallas_call | solution.py:87
  87.6 3.9 collective-permute-done.3.refs_6_
  92.3 3.0 collective-permute-start.5
  95.3 33.2 %weight_gradients.4 = (bf16[2048,1024]{1,0:T(8,128)(2,1)}, f32[2,64,256]{2,1,0:T(8,128)}, f32[8,1024]{1,0:T(8,128)}) custom-call(s32[1]{0:T(128)} %bitcast.me_ref, bf16[8,2048,256]{2,1,0:T(8,128)(2,1)} %bitcast.47, bf16[2048,1024]{1,0:T(8,128)(2,1)} %decode_weights.6.weight_ref.refs_1_, bf16[2048,1024]{1,0:T(8,128)(2,1)} %decode_weights.5._.weight_ref.refs_1_, ...), custom_call_target="tpu_custom_call" | custom-call | flops 38654705664 | bytes 12582912 | tf_op jit(solution)/shard_map/weight_gradients/pallas_call | solution.py:243
  128.5 9.9 %decode_weights.7.refs_2_.weight_ref = bf16[2048,512]{1,0:T(8,128)(2,1)} custom-call(s32[2,256,3584]{2,1,0:T(8,128)} %refs_0_.7, s32[2,8,128]{2,1,0:T(8,128)} %fusion.12.table_ref, f32[1,3584]{1,0:T(1,128)} %mul.97.coef_ref, f32[8,1024]{1,0:T(8,128)} %get-tuple-element.92._), custom_call_target="tpu_custom_call" | custom-call | flops 9437184000 | bytes 3145728 | tf_op jit(solution)/shard_map/decode_weights/pallas_call | solution.py:87
  140.8 3.7 collective-permute-start.7
  144.5 17.3 %early_input_gradient.2._.refs_2_ = f32[2048,2048]{1,0:T(8,128)} custom-call(bf16[2048,1024]{1,0:T(8,128)(2,1)} %get-tuple-element.99.refs_0_, bf16[2048,1024]{1,0:T(8,128)(2,1)} %decode_weights.6.weight_ref.refs_1_, bf16[2048,512]{1,0:T(8,128)(2,1)} %decode_weights.7.refs_2_.weight_ref), custom_call_target="tpu_custom_call" | custom-call | flops 12884901888 | bytes 25165824 | tf_op jit(solution)/shard_map/early_input_gradient/pallas_call | solution.py:293
  168.6 33.1 %weight_gradients.5 = (bf16[2048,1024]{1,0:T(8,128)(2,1)}, f32[2,64,256]{2,1,0:T(8,128)}, f32[8,1024]{1,0:T(8,128)}) custom-call(s32[1]{0:T(128)} %bitcast.me_ref, bf16[8,2048,256]{2,1,0:T(8,128)(2,1)} %bitcast.48, bf16[2048,1024]{1,0:T(8,128)(2,1)} %decode_weights.4._.weight_ref.refs_1_, f32[2048,2048]{1,0:T(8,128)} %early_input_gradient.2._.refs_2_, ...), custom_call_target="tpu_custom_call" | custom-call | flops 38654705664 | bytes 12582912 | tf_op jit(solution)/shard_map/weight_gradients/pallas_call | solution.py:243
  201.7 10.5 %collective-permute-done.9.refs_4_ = bf16[512,1024]{1,0:T(8,128)(2,1)S(1)} collective-permute-done((bf16[512,1024]{1,0:T(8,128)(2,1)S(1)}, bf16[512,1024]{1,0:T(8,128)(2,1)S(1)}, u32[]{:S(2)}, u32[]{:S(2)}) %collective-permute-start.9) | collective-permute-done | bytes 1048608 | tf_op jit(solution)/shard_map/ppermute | solution.py:126
  213.0 3.3 collective-permute-start.11
  216.3 21.4 %early_input_gradient.3._.early_ref = f32[2048,2048]{1,0:T(8,128)} custom-call(bf16[2048,1024]{1,0:T(8,128)(2,1)} %get-tuple-element.116.refs_0_, bf16[2048,1024]{1,0:T(8,128)(2,1)} %decode_weights.4._.weight_ref.refs_1_, f32[2048,2048]{1,0:T(8,128)} %early_input_gradient.2._.refs_2_, ...), custom_call_target="tpu_custom_call", output_to_operand_aliasing={{}: (2, {})} | custom-call | flops 12884901888 | bytes 25165824 | tf_op jit(solution)/shard_map/early_input_gradient/pallas_call | solution.py:293
  238.3 3.3 collective-permute-start.13
  241.6 33.2 %weight_gradients.6 = (bf16[2048,1024]{1,0:T(8,128)(2,1)}, f32[2,64,256]{2,1,0:T(8,128)}, f32[8,1024]{1,0:T(8,128)}) custom-call(s32[1]{0:T(128)} %bitcast.me_ref, bf16[8,2048,256]{2,1,0:T(8,128)(2,1)} %bitcast.49, bf16[2048,1024]{1,0:T(8,128)(2,1)} %decode_weights.5._.weight_ref.refs_1_, f32[2048,2048]{1,0:T(8,128)} %early_input_gradient.3._.early_ref, ...), custom_call_target="tpu_custom_call" | custom-call | flops 38654705664 | bytes 12582912 | tf_op jit(solution)/shard_map/weight_gradients/pallas_call | solution.py:243
  274.9 3.8 collective-permute-start.15
  279.3 6.6 %collective-permute-done.14.refs_6_.refs_5_ = bf16[256,512]{1,0:T(8,128)(2,1)S(1)} collective-permute-done((bf16[256,512]{1,0:T(8,128)(2,1)S(1)}, bf16[256,512]{1,0:T(8,128)(2,1)S(1)}, u32[]{:S(2)}, u32[]{:S(2)}) %collective-permute-start.14) | collective-permute-done | bytes 262176 | tf_op jit(solution)/shard_map/ppermute | solution.py:142
  288.4 13.3 %last_input_gradient.3 = (bf16[1024,1024]{1,0:T(8,128)(2,1)}, bf16[1024,1024]{1,0:T(8,128)(2,1)}) custom-call(s32[2]{0:T(128)} %get-tuple-element.185.me_ref, f32[2048,2048]{1,0:T(8,128)} %early_input_gradient.3._.early_ref, bf16[2048,1024]{1,0:T(8,128)(2,1)} %get-tuple-element.125.refs_0_, bf16[2048,1024]{1,0:T(8,128)(2,1)} %decode_weights.5._.weight_ref.refs_1_, ...), custom_call_target="tpu_custom_call" | custom-call | flops 12884901888 | bytes 12582912 | tf_op jit(solution)/shard_map/last_input_gradient/pallas_call | solution.py:336
  302.3 13.8 %last_input_gradient.2 = (f32[1024,1024]{1,0:T(8,128)}, f32[1024,1024]{1,0:T(8,128)}) custom-call(s32[2]{0:T(128)} %get-tuple-element.184.me_ref, f32[2048,2048]{1,0:T(8,128)} %early_input_gradient.3._.early_ref, bf16[2048,1024]{1,0:T(8,128)(2,1)} %get-tuple-element.125.refs_0_, bf16[2048,1024]{1,0:T(8,128)(2,1)} %decode_weights.5._.weight_ref.refs_1_, ...), custom_call_target="tpu_custom_call" | custom-call | flops 12884901888 | bytes 12582912 | tf_op jit(solution)/shard_map/last_input_gradient/pallas_call | solution.py:336
  323.9 19.2 %weight_gradients.7 = (bf16[2048,512]{1,0:T(8,128)(2,1)}, f32[2,64,256]{2,1,0:T(8,128)}, f32[8,512]{1,0:T(8,128)}) custom-call(s32[1]{0:T(128)} %bitcast.me_ref, bf16[8,2048,256]{2,1,0:T(8,128)(2,1)} %bitcast.50, bf16[2048,512]{1,0:T(8,128)(2,1)} %decode_weights.7.refs_2_.weight_ref, bf16[2,256,1024]{2,1,0:T(8,128)(2,1)} %fusion._, s32[2,256,3584]{2,1,0:T(8,128)} %refs_0_.7, ...), custom_call_target="tpu_custom_call" | custom-call | flops 19327352832 | bytes 6291456 | tf_op jit(solution)/shard_map/weight_gradients/pallas_call | solution.py:243
  365.6 10.3 %collective-permute-done.28 = f32[4096]{0:T(1024)S(1)} collective-permute-done((f32[4096]{0:T(1024)S(1)}, f32[4096]{0:T(1024)S(1)}, u32[]{:S(2)}, u32[]{:S(2)}) %collective-permute-start.28) | collective-permute-done | bytes 16416 | tf_op jit(solution)/shard_map/ppermute | solution.py:405
  (165 shorter events, 65.8 us)
Async XLA Ops:
  7.2 88.1 %all-gather.2.cloned.1.call-start = ((), (), s32[]{:S(2)}) async-start(), calls=%async_computation | async-start | bytes 9437184 | tf_op jit(solution)/shard_map/all_gather | solution.py:427
  13.0 46.8 %collective-permute-start = (bf16[512,1024]{1,0:T(8,128)(2,1)S(1)}, bf16[512,1024]{1,0:T(8,128)(2,1)}, u32[]{:S(2)}, u32[]{:S(2)}) collective-permute-start(bf16[512,1024]{1,0:T(8,128)(2,1)S(1)} %get-tuple-element.87.refs_2_), channel_id=1, source_target_pairs={{0,8},{8,16},{16,24},{24,0},{1,9},{9,17},{17,25},{25,1},{2,10},{10... | collective-permute-start | bytes 3145736 | tf_op jit(solution)/shard_map/ppermute | solution.py:125
  16.1 47.2 %collective-permute-start.1 = (bf16[512,1024]{1,0:T(8,128)(2,1)S(1)}, bf16[512,1024]{1,0:T(8,128)(2,1)}, u32[]{:S(2)}, u32[]{:S(2)}) collective-permute-start(bf16[512,1024]{1,0:T(8,128)(2,1)S(1)} %get-tuple-element.87.refs_2_), channel_id=1, source_target_pairs={{8,0},{16,8},{24,16},{0,24},{9,1},{17,9},{25,17},{1,25},{10,2},{18... | collective-permute-start | bytes 3145736 | tf_op jit(solution)/shard_map/ppermute | solution.py:126
  65.5 22.1 %collective-permute-start.2 = (bf16[256,1024]{1,0:T(8,128)(2,1)S(1)}, bf16[256,1024]{1,0:T(8,128)(2,1)S(1)}, u32[]{:S(2)}, u32[]{:S(2)}) collective-permute-start(bf16[256,1024]{1,0:T(8,128)(2,1)S(1)} %slice.54), channel_id=1, source_target_pairs={{0,8},{8,16},{16,24},{24,0},{1,9},{9,17},{17,25},{25,1},{2,10},{10... | collective-permute-start | bytes 1572872 | tf_op jit(solution)/shard_map/ppermute | solution.py:142
  66.7 24.8 %collective-permute-start.3 = (bf16[256,1024]{1,0:T(8,128)(2,1)S(1)}, bf16[256,1024]{1,0:T(8,128)(2,1)S(1)}, u32[]{:S(2)}, u32[]{:S(2)}) collective-permute-start(bf16[256,1024]{1,0:T(8,128)(2,1)S(1)} %slice.55), channel_id=1, source_target_pairs={{8,0},{16,8},{24,16},{0,24},{9,1},{17,9},{25,17},{1,25},{10,2},{18... | collective-permute-start | bytes 1572872 | tf_op jit(solution)/shard_map/ppermute | solution.py:143
  91.5 47.0 %collective-permute-start.4 = (bf16[512,1024]{1,0:T(8,128)(2,1)S(1)}, bf16[512,1024]{1,0:T(8,128)(2,1)S(1)}, u32[]{:S(2)}, u32[]{:S(2)}) collective-permute-start(bf16[512,1024]{1,0:T(8,128)(2,1)S(1)} %get-tuple-element.104.refs_2_), channel_id=1, source_target_pairs={{0,8},{8,16},{16,24},{24,0},{1,9},{9,17},{17,25},{25,1},{2,10},{10... | collective-permute-start | bytes 3145736 | tf_op jit(solution)/shard_map/ppermute | solution.py:125
  92.3 47.2 %collective-permute-start.5 = (bf16[512,1024]{1,0:T(8,128)(2,1)S(1)}, bf16[512,1024]{1,0:T(8,128)(2,1)}, u32[]{:S(2)}, u32[]{:S(2)}) collective-permute-start(bf16[512,1024]{1,0:T(8,128)(2,1)S(1)} %get-tuple-element.104.refs_2_), channel_id=1, source_target_pairs={{8,0},{16,8},{24,16},{0,24},{9,1},{17,9},{25,17},{1,25},{10,2},{18... | collective-permute-start | bytes 3145736 | tf_op jit(solution)/shard_map/ppermute | solution.py:126
  140.6 21.2 %collective-permute-start.6 = (bf16[256,1024]{1,0:T(8,128)(2,1)S(1)}, bf16[256,1024]{1,0:T(8,128)(2,1)S(1)}, u32[]{:S(2)}, u32[]{:S(2)}) collective-permute-start(bf16[256,1024]{1,0:T(8,128)(2,1)S(1)} %slice.56), channel_id=1, source_target_pairs={{0,8},{8,16},{16,24},{24,0},{1,9},{9,17},{17,25},{25,1},{2,10},{10... | collective-permute-start | bytes 1572872 | tf_op jit(solution)/shard_map/ppermute | solution.py:142
  140.8 23.9 %collective-permute-start.7 = (bf16[256,1024]{1,0:T(8,128)(2,1)S(1)}, bf16[256,1024]{1,0:T(8,128)(2,1)S(1)}, u32[]{:S(2)}, u32[]{:S(2)}) collective-permute-start(bf16[256,1024]{1,0:T(8,128)(2,1)S(1)} %slice.57), channel_id=1, source_target_pairs={{8,0},{16,8},{24,16},{0,24},{9,1},{17,9},{25,17},{1,25},{10,2},{18... | collective-permute-start | bytes 1572872 | tf_op jit(solution)/shard_map/ppermute | solution.py:143
  164.7 37.0 %collective-permute-start.8 = (bf16[512,1024]{1,0:T(8,128)(2,1)S(1)}, bf16[512,1024]{1,0:T(8,128)(2,1)S(1)}, u32[]{:S(2)}, u32[]{:S(2)}) collective-permute-start(bf16[512,1024]{1,0:T(8,128)(2,1)S(1)} %get-tuple-element.120.refs_2_), channel_id=1, source_target_pairs={{0,8},{8,16},{16,24},{24,0},{1,9},{9,17},{17,25},{25,1},{2,10},{10... | collective-permute-start | bytes 3145736 | tf_op jit(solution)/shard_map/ppermute | solution.py:125
  166.4 45.9 %collective-permute-start.9 = (bf16[512,1024]{1,0:T(8,128)(2,1)S(1)}, bf16[512,1024]{1,0:T(8,128)(2,1)S(1)}, u32[]{:S(2)}, u32[]{:S(2)}) collective-permute-start(bf16[512,1024]{1,0:T(8,128)(2,1)S(1)} %get-tuple-element.120.refs_2_), channel_id=1, source_target_pairs={{8,0},{16,8},{24,16},{0,24},{9,1},{17,9},{25,17},{1,25},{10,2},{18... | collective-permute-start | bytes 3145736 | tf_op jit(solution)/shard_map/ppermute | solution.py:126
  212.4 25.3 %collective-permute-start.10 = (bf16[256,1024]{1,0:T(8,128)(2,1)S(1)}, bf16[256,1024]{1,0:T(8,128)(2,1)S(1)}, u32[]{:S(2)}, u32[]{:S(2)}) collective-permute-start(bf16[256,1024]{1,0:T(8,128)(2,1)S(1)} %slice.58), channel_id=1, source_target_pairs={{0,8},{8,16},{16,24},{24,0},{1,9},{9,17},{17,25},{25,1},{2,10},{10... | collective-permute-start | bytes 1572872 | tf_op jit(solution)/shard_map/ppermute | solution.py:142
  213.0 24.8 %collective-permute-start.11 = (bf16[256,1024]{1,0:T(8,128)(2,1)S(1)}, bf16[256,1024]{1,0:T(8,128)(2,1)S(1)}, u32[]{:S(2)}, u32[]{:S(2)}) collective-permute-start(bf16[256,1024]{1,0:T(8,128)(2,1)S(1)} %slice.59), channel_id=1, source_target_pairs={{8,0},{16,8},{24,16},{0,24},{9,1},{17,9},{25,17},{1,25},{10,2},{18... | collective-permute-start | bytes 1572872 | tf_op jit(solution)/shard_map/ppermute | solution.py:143
  237.8 37.0 %collective-permute-start.12 = (bf16[512,512]{1,0:T(8,128)(2,1)S(1)}, bf16[512,512]{1,0:T(8,128)(2,1)S(1)}, u32[]{:S(2)}, u32[]{:S(2)}) collective-permute-start(bf16[512,512]{1,0:T(8,128)(2,1)S(1)} %copy-done.4), channel_id=1, source_target_pairs={{0,8},{8,16},{16,24},{24,0},{1,9},{9,17},{17,25},{25,1},{2,10},{10... | collective-permute-start | bytes 1572872 | tf_op jit(solution)/shard_map/ppermute | solution.py:125
  238.3 36.5 %collective-permute-start.13 = (bf16[512,512]{1,0:T(8,128)(2,1)S(1)}, bf16[512,512]{1,0:T(8,128)(2,1)S(1)}, u32[]{:S(2)}, u32[]{:S(2)}) collective-permute-start(bf16[512,512]{1,0:T(8,128)(2,1)S(1)} %copy-done.4), channel_id=1, source_target_pairs={{8,0},{16,8},{24,16},{0,24},{9,1},{17,9},{25,17},{1,25},{10,2},{18... | collective-permute-start | bytes 1572872 | tf_op jit(solution)/shard_map/ppermute | solution.py:126
  274.9 11.1 %collective-permute-start.14 = (bf16[256,512]{1,0:T(8,128)(2,1)S(1)}, bf16[256,512]{1,0:T(8,128)(2,1)S(1)}, u32[]{:S(2)}, u32[]{:S(2)}) collective-permute-start(bf16[256,512]{1,0:T(8,128)(2,1)S(1)} %slice.60), channel_id=1, source_target_pairs={{0,8},{8,16},{16,24},{24,0},{1,9},{9,17},{17,25},{25,1},{2,10},{10... | collective-permute-start | bytes 786440 | tf_op jit(solution)/shard_map/ppermute | solution.py:142
  274.9 12.7 %collective-permute-start.15 = (bf16[256,512]{1,0:T(8,128)(2,1)S(1)}, bf16[256,512]{1,0:T(8,128)(2,1)S(1)}, u32[]{:S(2)}, u32[]{:S(2)}) collective-permute-start(bf16[256,512]{1,0:T(8,128)(2,1)S(1)} %slice.61), channel_id=1, source_target_pairs={{8,0},{16,8},{24,16},{0,24},{9,1},{17,9},{25,17},{1,25},{10,2},{18... | collective-permute-start | bytes 786440 | tf_op jit(solution)/shard_map/ppermute | solution.py:143
  301.7 14.4 %collective-permute-start.18 = (bf16[1024,1024]{1,0:T(8,128)(2,1)}, bf16[1024,1024]{1,0:T(8,128)(2,1)S(1)}, u32[]{:S(2)}, u32[]{:S(2)}) collective-permute-start(bf16[1024,1024]{1,0:T(8,128)(2,1)} %get-tuple-element.136), channel_id=1, source_target_pairs={{0,1},{1,0},{2,3},{3,2},{4,5},{5,4},{6,7},{7,6},{8,9},{9,8},{10,11... | collective-permute-start | bytes 6291464 | tf_op jit(solution)/shard_map/ppermute | solution.py:491
  301.7 18.1 %collective-permute-start.16 = (bf16[1024,1024]{1,0:T(8,128)(2,1)}, bf16[1024,1024]{1,0:T(8,128)(2,1)}, u32[]{:S(2)}, u32[]{:S(2)}) collective-permute-start(bf16[1024,1024]{1,0:T(8,128)(2,1)} %get-tuple-element.134), channel_id=1, source_target_pairs={{0,1},{1,0},{2,3},{3,2},{4,5},{5,4},{6,7},{7,6},{8,9},{9,8},{10,11... | collective-permute-start | bytes 6291464 | tf_op jit(solution)/shard_map/ppermute | solution.py:491
  318.2 25.6 %collective-permute-start.19 = (bf16[2,256,1024]{2,1,0:T(8,128)(2,1)S(1)}, bf16[2,256,1024]{2,1,0:T(8,128)(2,1)}, u32[]{:S(2)}, u32[]{:S(2)}) collective-permute-start(bf16[2,256,1024]{2,1,0:T(8,128)(2,1)S(1)} %fusion.1), channel_id=1, source_target_pairs={{0,4},{1,5},{2,6},{3,7},{4,0},{5,1},{6,2},{7,3},{8,12},{9,13},{10,... | collective-permute-start | bytes 3145736 | tf_op jit(solution)/shard_map/ppermute | solution.py:384
  322.4 25.2 %collective-permute-start.17 = (bf16[2,256,1024]{2,1,0:T(8,128)(2,1)}, bf16[2,256,1024]{2,1,0:T(8,128)(2,1)}, u32[]{:S(2)}, u32[]{:S(2)}) collective-permute-start(bf16[2,256,1024]{2,1,0:T(8,128)(2,1)} %fusion._), channel_id=1, source_target_pairs={{0,2},{1,3},{2,0},{3,1},{4,6},{5,7},{6,4},{7,5},{8,10},{9,11},{10,... | collective-permute-start | bytes 3145736 | tf_op jit(solution)/shard_map/ppermute | solution.py:384
  361.1 16.2 %collective-permute-start.20 = (bf16[256,1024]{1,0:T(8,128)(2,1)}, bf16[256,1024]{1,0:T(8,128)(2,1)S(1)}, u32[]{:S(2)}, u32[]{:S(2)}) collective-permute-start(bf16[256,1024]{1,0:T(8,128)(2,1)} %fusion.5), channel_id=1, source_target_pairs={{0,4},{1,5},{2,6},{3,7},{4,0},{5,1},{6,2},{7,3},{8,12},{9,13},{10,... | collective-permute-start | bytes 1572872 | tf_op jit(solution)/shard_map/ppermute | solution.py:384
  362.1 17.1 %collective-permute-start.21 = (bf16[256,1024]{1,0:T(8,128)(2,1)}, bf16[256,1024]{1,0:T(8,128)(2,1)S(1)}, u32[]{:S(2)}, u32[]{:S(2)}) collective-permute-start(bf16[256,1024]{1,0:T(8,128)(2,1)} %fusion.4), channel_id=1, source_target_pairs={{0,2},{1,3},{2,0},{3,1},{4,6},{5,7},{6,4},{7,5},{8,10},{9,11},{10,... | collective-permute-start | bytes 1572872 | tf_op jit(solution)/shard_map/ppermute | solution.py:384
  364.0 11.9 %collective-permute-start.28 = (f32[4096]{0:T(1024)S(1)}, f32[4096]{0:T(1024)S(1)}, u32[]{:S(2)}, u32[]{:S(2)}) collective-permute-start(f32[4096]{0:T(1024)S(1)} %add_add_fusion.2), channel_id=1, source_target_pairs={{0,4},{1,5},{2,6},{3,7},{4,0},{5,1},{6,2},{7,3},{8,12},{9,13},{10,... | collective-permute-start | bytes 49160 | tf_op jit(solution)/shard_map/ppermute | solution.py:405
  (40 other events, 677.9 us)
Sparse Core Ops, SparseCore 0:
  10.9 57.0 all-gather.1

commit v3 on v2

--- a/solution.py
+++ b/solution.py
@@ -36,9 +36,9 @@
 
 
 def split_columns(outs):
-    unit = next((u for u in (4 * LANES, 2 * LANES) if outs % u == 0), LANES)
+    unit = next((u for u in (2 * LANES,) if outs % u == 0), LANES)
     units = outs // unit
-    shares = (2, 2, 2, 1)
+    shares = (5, 5, 4)
     ends = [round(units * sum(shares[: i + 1]) / sum(shares)) for i in range(len(shares))]
     widths = [(end - start) * unit for start, end in zip([0] + ends, ends)]
     return [width for width in widths if width]
@@ -83,7 +83,9 @@
 def decode(codes, table, coef, after, first, width):
     groups = codes.shape[1]
     tile_groups = largest_tile(groups, 64)
-    unit = math.gcd(math.gcd(first, width), 512)
+    unit = math.gcd(first, width)
+    if unit > 12 * LANES:
+        unit = math.gcd(unit, 4 * LANES)
     return pl.pallas_call(
         functools.partial(decode_kernel, tile_groups, unit),
         grid=(width // unit, groups // tile_groups),
@@ -108,7 +110,7 @@
     for d in range(1, (n - 1) // 2 + 1):
         places += [(-d, 0, rows), (d, 0, rows)]
     if n % 2 == 0:
-        places += [(-(n // 2), 0, rows // 2), (n // 2, rows // 2, rows - rows // 2)]
+        places += [(-(n // 2), 0, rows)]
     return places
 
 
@@ -131,18 +133,12 @@
         held, gate = lax.optimization_barrier((self.pieces, gate))
         self.pieces = list(held)
         if first:
-            self.left, self.right = self.pieces[-2:]
+            self.left = self.pieces[-2]
         return gate
 
-    def finish(self, following):
+    def finish(self):
         if self.n % 2 == 0:
-            half = self.rows // 2
-            halves, following = lax.optimization_barrier(((self.left[:half], self.right[half:]), following))
-            self.pieces += [
-                lax.ppermute(halves[0], "din", self.forward),
-                lax.ppermute(halves[1], "din", self.backward),
-            ]
-        return following
+            self.pieces.append(lax.ppermute(self.left, "din", self.forward))
 
 
 def transpose_kernel(in_ref, out_ref):
@@ -184,14 +180,17 @@
 
 def gradient_kernel(n, tile, width, blocks, count, parts, me_ref, x_ref, weight_ref, _, *refs):
     code_refs, coef_refs, refs = refs[:parts], refs[parts : 2 * parts], refs[2 * parts :]
-    pieces, (cot_ref, book_ref, scale_ref, total_ref) = refs[:count], refs[count:]
+    pieces, refs = refs[:count], refs[count:]
+    cot_ref = refs[0] if count > 1 else pieces[0]
+    book_ref, scale_ref, total_ref = refs[-3:]
     step = pl.program_id(0)
 
     @pl.when(step == 0)
     def _():
         total_ref[...] = jnp.zeros_like(total_ref)
         scale_ref[...] = jnp.zeros_like(scale_ref)
-        place_pieces(me_ref[0], n, pieces[0].shape[0], pieces, cot_ref)
+        if count > 1:
+            place_pieces(me_ref[0], n, pieces[0].shape[0], pieces, cot_ref)
 
     x = jnp.concatenate([x_ref[e] for e in range(blocks)], axis=1) if blocks > 1 else x_ref[0]
     grads = jnp.dot(x, cot_ref[...], preferred_element_type=jnp.float32)
@@ -230,47 +229,53 @@
                 book_ref[b, pl.ds(v * GROUP, GROUP), :] = part
 
 
-def gradients(me, n, codes, x, pieces, weights, coef, after, first, width):
+def gradients(me, n, codes, x, pieces, weights, coef, after, first, width, span=(0, 1)):
     groups = codes.shape[1]
     blocks, features, tokens_block = x.shape
     tile_groups = largest_tile(groups, 32)
     tile = tile_groups * GROUP
     tokens = blocks * tokens_block
+    tiles = groups // tile_groups
+    start, end = [round(tiles * at) for at in span]
     unit = math.gcd(first, width)
     parts = width // unit
     places = [first // unit + p for p in range(parts)]
     once = pl.Buffered(1)
-    return pl.pallas_call(
+    out_specs = [
+        pl.BlockSpec((BOOKS, LOW * GROUP, 8 * HIGH), lambda f: (0, 0, 0)),
+        pl.BlockSpec((GROUP, width), lambda f: (0, 0)),
+    ]
+    out_shape = [
+        jax.ShapeDtypeStruct((BOOKS, LOW * GROUP, 8 * HIGH), jnp.float32),
+        jax.ShapeDtypeStruct((GROUP, width), jnp.float32),
+    ]
+    if len(pieces) > 1:
+        out_specs.insert(0, pl.BlockSpec((tokens, width), lambda f: (0, 0), pipeline_mode=once))
+        out_shape.insert(0, jax.ShapeDtypeStruct((tokens, width), jnp.bfloat16))
+    result = pl.pallas_call(
         functools.partial(gradient_kernel, n, tile, width, blocks, len(pieces), parts),
-        grid=(groups // tile_groups,),
+        grid=(end - start,),
         in_specs=[
             pl.BlockSpec(memory_space=pltpu.SMEM),
-            pl.BlockSpec((blocks, tile, tokens_block), lambda f: (0, f, 0)),
-            pl.BlockSpec((tile, width), lambda f: (f, 0)),
+            pl.BlockSpec((blocks, tile, tokens_block), lambda f: (0, start + f, 0)),
+            pl.BlockSpec((tile, width), lambda f: (start + f, 0)),
             pl.BlockSpec(memory_space=pl.ANY),
         ]
-        + [pl.BlockSpec((BOOKS, tile_groups, unit), lambda f, p=p: (0, f, p)) for p in places]
+        + [pl.BlockSpec((BOOKS, tile_groups, unit), lambda f, p=p: (0, start + f, p)) for p in places]
         + [pl.BlockSpec((1, unit), lambda f, p=p: (0, p)) for p in places]
         + [pl.BlockSpec(p.shape, lambda f: (0, 0), pipeline_mode=once) for p in pieces],
-        out_specs=[
-            pl.BlockSpec((tokens, width), lambda f: (0, 0), pipeline_mode=once),
-            pl.BlockSpec((BOOKS, LOW * GROUP, 8 * HIGH), lambda f: (0, 0, 0)),
-            pl.BlockSpec((GROUP, width), lambda f: (0, 0)),
-        ],
-        out_shape=[
-            jax.ShapeDtypeStruct((tokens, width), jnp.bfloat16),
-            jax.ShapeDtypeStruct((BOOKS, LOW * GROUP, 8 * HIGH), jnp.float32),
-            jax.ShapeDtypeStruct((GROUP, width), jnp.float32),
-        ],
+        out_specs=out_specs,
+        out_shape=out_shape,
         scratch_shapes=[pltpu.VMEM((BOOKS, LOW * 8 * GROUP, 8 * HIGH), jnp.float32)],
         compiler_params=pltpu.CompilerParams(vmem_limit_bytes=VMEM),
         cost_estimate=pl.CostEstimate(
-            flops=9 * tokens * features * width,
-            bytes_accessed=2 * (tokens + 2 * features) * width,
+            flops=9 * tokens * features * width * (end - start) // tiles,
+            bytes_accessed=2 * (tokens + 2 * features) * width * (end - start) // tiles,
             transcendentals=0,
         ),
         name="weight_gradients",
     )(me, x, weights, after, *([codes] * parts), *([coef] * parts), *pieces)
+    return result if len(pieces) > 1 else [pieces[0], *result]
 
 
 def input_gradient_kernel(count, refs):
@@ -423,11 +428,6 @@
     outs = codes.shape[2]
     me = lax.axis_index("din").astype(jnp.int32).reshape(1)
 
-    if inputs.shape[0] % LANES == 0:
-        x = lax.all_gather(transpose(inputs), "dout", axis=0, tiled=True).reshape(n_dout, inputs.shape[1], inputs.shape[0])
-    else:
-        x = lax.all_gather(inputs, "dout", axis=0, tiled=True).T[None]
-
     table, unit = packed_table(codebooks)
     coef_row = coef.reshape(1, outs)
     unit_row = coef_row * unit
@@ -443,28 +443,39 @@
     def run_decode(s, after):
         weights[s] = decode(codes, table, unit_row, after, firsts[s], widths[s])
 
-    def run_gradients(s, after):
+    def run_gradients(s, after, span=(0, 1)):
+        pieces = rings[s].pieces if span[0] == 0 else [cots[s]]
         cot, book, scale = gradients(
-            me, n_din, codes, x, rings[s].pieces, weights[s], coef_row, after, firsts[s], widths[s]
+            me, n_din, codes, x, pieces, weights[s], coef_row, after, firsts[s], widths[s], span
         )
-        cots.append(cot)
+        if span[0] == 0:
+            cots.append(cot)
+            scale_parts.append(jnp.sum(scale, axis=0))
+        else:
+            scale_parts[s] += jnp.sum(scale, axis=0)
         books.append(book)
-        scale_parts.append(scale)
         return scale
 
+    blocks, owns[0] = lax.optimization_barrier((inputs, owns[0]))
+    if inputs.shape[0] % LANES == 0:
+        x = lax.all_gather(transpose(blocks), "dout", axis=0, tiled=True)
+        x = x.reshape(n_dout, inputs.shape[1], inputs.shape[0])
+    else:
+        x = lax.all_gather(blocks, "dout", axis=0, tiled=True).T[None]
     rings[0].begin(owns[0])
-    for s in range(min(2, final + 1)):
-        run_decode(s, coef_row)
+    run_decode(0, coef_row)
+    if final > 0:
+        run_decode(1, coef_row)
     early, summed, gate = None, 0, weights[min(1, final)]
     for s in range(final + 1):
         gate = rings[s].hold(gate)
         if s == 0:
             weights[min(1, final)] = gate
-        gate = rings[s].finish(gate)
+        rings[s].finish()
         if s == 0 and final >= 2:
             run_decode(2, gate)
             gate = weights[2]
-        if 0 < s < max(2, final):
+        if 0 < s < final + 1:
             early = early_input_gradient(cots[summed:], weights[summed:s], early, gate)
             summed, gate = s, early
         if s < final:
@@ -494,8 +505,12 @@
         gate = keep[0]
         if n_dout > 2:
             gate = lax.optimization_barrier(scatter.exchange())[0]
-        run_gradients(final, gate)
-        grad_input, books[-1] = scatter.finish(books[-1])
+        cut = 5 / 8 if codes.shape[1] >= 256 else 1
+        gate = run_gradients(final, gate, (0, cut))
+        grad_input, gate = scatter.finish(gate)
+        if cut < 1:
+            run_gradients(final, gate, (cut, 1))
+        grad_input, books[-1] = lax.optimization_barrier((grad_input, books[-1]))
     else:
         run_gradients(final, gate)
         rows = early_input_gradient(cots, weights, None, gate)
@@ -503,7 +518,7 @@
 
     book = sum(books[1:], books[0]).reshape(BOOKS, LOW, GROUP, 8, HIGH).sum(axis=3)
     book = book.transpose(0, 3, 1, 2).reshape(BOOKS * KCODE * GROUP)
-    scale_total = jnp.concatenate([jnp.sum(part, axis=0) for part in scale_parts]) / coef
+    scale_total = jnp.concatenate(scale_parts) / coef
     both = butterfly_sum(jnp.concatenate([book, scale_total]), "din", n_din)
     grad_sums = butterfly_sum(both[: book.shape[0]], "dout", n_dout).reshape(BOOKS, KCODE, GROUP)
     scale_sums = both[book.shape[0] :]

time: 390 us -> 375 us (0.962)
  starting transfers between devices: 45.1 us -> 23.8 us
  waiting for transfers between devices: 46.1 us -> 62.9 us
  Pallas kernels: 253 us -> 244 us
    ppermute x4 -> x3, waiting for transfers between devices: 0.01 us -> 18.7 us  [begin(): self.left = lax.ppermute(self.left, 'din', self.forward)]
    ppermute x8 -> x3, starting transfers between devices: 15.5 us -> 2.15 us  [finish(): self.pieces.append(lax.ppermute(self.left, 'din', self.forward))]
    pallas_call x4 -> x3, Pallas kernels: 64.8 us -> 56.3 us  [decode(): pl.pallas_call(functools.partial(decode_kernel, tile_groups, unit), grid=...]
    ppermute x8 -> x3, waiting for transfers between devices: 15.2 us -> 23.3 us  [finish(): self.pieces.append(lax.ppermute(self.left, 'din', self.forward))]
    ppermute x7, waiting for transfers between devices: 14.6 us -> 6.8 us  [other(): return lax.ppermute(value, axis, [(a, a ^ bits) for a in range(size)])]
    ppermute x4 -> x3, starting transfers between devices: 10.6 us -> 7.43 us  [begin(): self.right = lax.ppermute(self.right, 'din', self.backward)]
    ppermute x4 -> x3, waiting for transfers between devices: 15 us -> 14.1 us  [begin(): self.right = lax.ppermute(self.right, 'din', self.backward)]
  transfers between devices with their start and end apart: 30 -> 23, of which waited for: 13 -> 11; matrix products, arithmetic and copies ran while one was open for 5% -> 4% of each run, Pallas kernels for 61% -> 61%
where the time goes in v3:
time: 375 us; the launch traced here: 374 us
  Pallas kernels  244 us (65%)
  waiting for transfers between devices  62.9 us (17%)
  starting transfers between devices  23.8 us (6%)
  other arithmetic  18.2 us (5%)
  between operations  15 us (4%)
  local copies, waits for them, and re-layouts  9.43 us (3%)
    pallas_call x4, Pallas kernels, gradients(): pl.pallas_call(functools.partial(gradient_kernel, n, tile, width, blocks,...  118 us
    pallas_call x3, Pallas kernels, decode(): pl.pallas_call(functools.partial(decode_kernel, tile_groups, unit), grid=...  56.3 us
    pallas_call x2, Pallas kernels, early_input_gradient(): pl.pallas_call(functools.partial(early_kernel, len(cots), total is not No...  42 us
    pallas_call x2, Pallas kernels, last_input_gradient(): pl.pallas_call(functools.partial(last_kernel, n, rows, block, len(cots),...  24.1 us
    ppermute x3, waiting for transfers between devices, finish(): self.pieces.append(lax.ppermute(self.left, 'din', self.forward))  23.3 us
    ppermute x3, waiting for transfers between devices, begin(): self.left = lax.ppermute(self.left, 'din', self.forward)  18.7 us
    ppermute x3, waiting for transfers between devices, begin(): self.right = lax.ppermute(self.right, 'din', self.backward)  14.1 us
    convert_element_type x4, other arithmetic, exchange(): gives.append(give.astype(jnp.bfloat16))  8.69 us
  transfers between devices with their start and end apart: 23, of which 11 were waited for; matrix products, arithmetic and copies ran while one was open for 4% of the time, Pallas kernels for 61%

profile of v3, /device:TPU:0, one launch (start us, length us, event | category | flops | bytes accessed | tf_op | source)
XLA Modules:
  0.0 373.8 jit_solution(7018756768850549645)
XLA Ops:
  9.1 3.8 %transpose_inputs.1 = bf16[2048,256]{1,0:T(8,128)(2,1)} custom-call(bf16[256,2048]{1,0:T(8,128)(2,1)} %in_ref), custom_call_target="tpu_custom_call" | custom-call | tf_op jit(solution)/shard_map/transpose_inputs/pallas_call | solution.py:151
  12.9 5.1 %collective-permute-start.1 = (bf16[512,1280]{1,0:T(8,128)(2,1)S(1)}, bf16[512,1280]{1,0:T(8,128)(2,1)}, u32[]{:S(2)}, u32[]{:S(2)}) collective-permute-start(bf16[512,1280]{1,0:T(8,128)(2,1)S(1)} %get-tuple-element.66.refs_2_), channel_id=1, source_target_pairs={{8,0},{16,8},{24,16},{0,24},{9,1},{17,9},{25,17},{1,25},{10,2},{18... | collective-permute-start | bytes 3932168 | tf_op jit(solution)/shard_map/ppermute | solution.py:128
  18.0 2.3 slice.24.refs_1_.refs_4_
  24.0 18.9 %decode_weights.5.weight_ref.refs_1_ = bf16[2048,1280]{1,0:T(8,128)(2,1)} custom-call(s32[2,256,3584]{2,1,0:T(8,128)} %refs_1_.3, s32[2,8,128]{2,1,0:T(8,128)} %fusion.12.table_ref, f32[1,3584]{1,0:T(1,128)} %mul.97.coef_ref, f32[1,3584]{1,0:T(1,128)} %reshape.88._.refs_1_.refs_2_.refs_3_), custom_call_target="tpu_custom_call" | custom-call | flops 23592960000 | bytes 7864320 | tf_op jit(solution)/shard_map/decode_weights/pallas_call | solution.py:89
  43.0 19.1 %decode_weights.3._.weight_ref.refs_1_ = bf16[2048,1280]{1,0:T(8,128)(2,1)} custom-call(s32[2,256,3584]{2,1,0:T(8,128)} %refs_1_.3, s32[2,8,128]{2,1,0:T(8,128)} %fusion.12.table_ref, f32[1,3584]{1,0:T(1,128)} %mul.97.coef_ref, f32[1,3584]{1,0:T(1,128)} %reshape.88._.refs_1_.refs_2_.refs_3_), custom_call_target="tpu_custom_call" | custom-call | flops 23592960000 | bytes 7864320 | tf_op jit(solution)/shard_map/decode_weights/pallas_call | solution.py:89
  62.1 13.0 %collective-permute-done.refs_3_ = bf16[512,1280]{1,0:T(8,128)(2,1)} collective-permute-done((bf16[512,1280]{1,0:T(8,128)(2,1)S(1)}, bf16[512,1280]{1,0:T(8,128)(2,1)}, u32[]{:S(2)}, u32[]{:S(2)}) %collective-permute-start) | collective-permute-done | bytes 1310752 | tf_op jit(solution)/shard_map/ppermute | solution.py:127
  76.8 18.2 %decode_weights.4._.refs_0_.weight_ref = bf16[2048,1024]{1,0:T(8,128)(2,1)} custom-call(s32[2,256,3584]{2,1,0:T(8,128)} %refs_1_.3, s32[2,8,128]{2,1,0:T(8,128)} %fusion.12.table_ref, f32[1,3584]{1,0:T(1,128)} %mul.97.coef_ref, bf16[2048,1280]{1,0:T(8,128)(2,1)} %decode_weights.3._.weight_ref.refs_1_), custom_call_target="tpu_custom_call" | custom-call | flops 18874368000 | bytes 6291456 | tf_op jit(solution)/shard_map/decode_weights/pallas_call | solution.py:89
  95.0 11.8 %collective-permute-done.2.refs_5_ = bf16[512,1280]{1,0:T(8,128)(2,1)S(1)} collective-permute-done((bf16[512,1280]{1,0:T(8,128)(2,1)}, bf16[512,1280]{1,0:T(8,128)(2,1)S(1)}, u32[]{:S(2)}, u32[]{:S(2)}) %collective-permute-start.2) | collective-permute-done | bytes 1310752 | tf_op jit(solution)/shard_map/ppermute | solution.py:141
  110.0 40.7 %weight_gradients.4 = (bf16[2048,1280]{1,0:T(8,128)(2,1)}, f32[2,64,256]{2,1,0:T(8,128)}, f32[8,1280]{1,0:T(8,128)}) custom-call(s32[1]{0:T(128)} %bitcast.me_ref, bf16[8,2048,256]{2,1,0:T(8,128)(2,1)} %bitcast.47, bf16[2048,1280]{1,0:T(8,128)(2,1)} %decode_weights.5.weight_ref.refs_1_, bf16[2048,1024]{1,0:T(8,128)(2,1)} %decode_weights.4._.refs_0_.weight_ref, ...), custom_call_target="tpu_custom_call" | custom-call | flops 48318382080 | bytes 15728640 | tf_op jit(solution)/shard_map/weight_gradients/pallas_call | solution.py:255
  150.7 14.1 %collective-permute-done.4.refs_4_ = bf16[512,1280]{1,0:T(8,128)(2,1)S(1)} collective-permute-done((bf16[512,1280]{1,0:T(8,128)(2,1)S(1)}, bf16[512,1280]{1,0:T(8,128)(2,1)S(1)}, u32[]{:S(2)}, u32[]{:S(2)}) %collective-permute-start.4) | collective-permute-done | bytes 1310752 | tf_op jit(solution)/shard_map/ppermute | solution.py:128
  165.8 19.1 %early_input_gradient.2._.refs_2_ = f32[2048,2048]{1,0:T(8,128)} custom-call(bf16[2048,1280]{1,0:T(8,128)(2,1)} %get-tuple-element.74.refs_0_, bf16[2048,1280]{1,0:T(8,128)(2,1)} %decode_weights.5.weight_ref.refs_1_, f32[8,1280]{1,0:T(8,128)} %get-tuple-element.75.refs_2_), custom_call_target="tpu_custom_call" | custom-call | flops 16106127360 | bytes 27262976 | tf_op jit(solution)/shard_map/early_input_gradient/pallas_call | solution.py:298
  184.9 9.4 %collective-permute-done.5.refs_5_ = bf16[512,1280]{1,0:T(8,128)(2,1)S(1)} collective-permute-done((bf16[512,1280]{1,0:T(8,128)(2,1)}, bf16[512,1280]{1,0:T(8,128)(2,1)S(1)}, u32[]{:S(2)}, u32[]{:S(2)}) %collective-permute-start.5) | collective-permute-done | bytes 1310752 | tf_op jit(solution)/shard_map/ppermute | solution.py:141
  194.3 2.3 collective-permute-start.7
  196.7 40.8 %weight_gradients.5 = (bf16[2048,1280]{1,0:T(8,128)(2,1)}, f32[2,64,256]{2,1,0:T(8,128)}, f32[8,1280]{1,0:T(8,128)}) custom-call(s32[1]{0:T(128)} %bitcast.me_ref, bf16[8,2048,256]{2,1,0:T(8,128)(2,1)} %bitcast.48, bf16[2048,1280]{1,0:T(8,128)(2,1)} %decode_weights.3._.weight_ref.refs_1_, f32[2048,2048]{1,0:T(8,128)} %early_input_gradient.2._.refs_2_, ...), custom_call_target="tpu_custom_call" | custom-call | flops 48318382080 | bytes 15728640 | tf_op jit(solution)/shard_map/weight_gradients/pallas_call | solution.py:255
  237.5 5.6 %collective-permute-done.6.refs_2_.refs_5_ = bf16[512,1024]{1,0:T(8,128)(2,1)S(1)} collective-permute-done((bf16[512,1024]{1,0:T(8,128)(2,1)S(1)}, bf16[512,1024]{1,0:T(8,128)(2,1)S(1)}, u32[]{:S(2)}, u32[]{:S(2)}) %collective-permute-start.6) | collective-permute-done | bytes 1048608 | tf_op jit(solution)/shard_map/ppermute | solution.py:127
  243.2 22.9 %early_input_gradient.3.early_ref = f32[2048,2048]{1,0:T(8,128)} custom-call(bf16[2048,1280]{1,0:T(8,128)(2,1)} %get-tuple-element.82.refs_0_, bf16[2048,1280]{1,0:T(8,128)(2,1)} %decode_weights.3._.weight_ref.refs_1_, f32[2048,2048]{1,0:T(8,128)} %early_input_gradient.2._.refs_2_, f32[8,1280]{1,0:T(8,128)} %get-tuple-element.85.refs_3_), custom_call_target="tpu_custom_call", output_to_operand_aliasing={{}: (2, {})} | custom-call | flops 16106127360 | bytes 27262976 | tf_op jit(solution)/shard_map/early_input_gradient/pallas_call | solution.py:298
  266.1 2.1 collective-permute-done.8.refs_4_.refs_7_
  269.2 11.7 %last_input_gradient.3 = (bf16[1024,1024]{1,0:T(8,128)(2,1)}, bf16[1024,1024]{1,0:T(8,128)(2,1)}) custom-call(s32[2]{0:T(128)} %get-tuple-element.144.me_ref, f32[2048,2048]{1,0:T(8,128)} %early_input_gradient.3.early_ref, bf16[2048,1024]{1,0:T(8,128)(2,1)} %decode_weights.4._.refs_0_.weight_ref, bf16[512,1024]{1,0:T(8,128)(2,1)} %slice.24.refs_1_.refs_4_, ...), custom_call_target="tpu_custom_call" | custom-call | flops 8589934592 | bytes 12582912 | tf_op jit(solution)/shard_map/last_input_gradient/pallas_call | solution.py:341
  281.5 12.4 %last_input_gradient.2 = (f32[1024,1024]{1,0:T(8,128)}, f32[1024,1024]{1,0:T(8,128)}) custom-call(s32[2]{0:T(128)} %get-tuple-element.143.me_ref, f32[2048,2048]{1,0:T(8,128)} %early_input_gradient.3.early_ref, bf16[2048,1024]{1,0:T(8,128)(2,1)} %decode_weights.4._.refs_0_.weight_ref, bf16[512,1024]{1,0:T(8,128)(2,1)} %slice.24.refs_1_.refs_4_, ...), custom_call_target="tpu_custom_call" | custom-call | flops 8589934592 | bytes 12582912 | tf_op jit(solution)/shard_map/last_input_gradient/pallas_call | solution.py:341
  293.9 2.4 fusion._
  300.7 22.7 %weight_gradients.6 = (bf16[2048,1024]{1,0:T(8,128)(2,1)}, f32[2,64,256]{2,1,0:T(8,128)}, f32[8,1024]{1,0:T(8,128)}) custom-call(s32[1]{0:T(128)} %bitcast.me_ref, bf16[8,2048,256]{2,1,0:T(8,128)(2,1)} %bitcast.49, bf16[2048,1024]{1,0:T(8,128)(2,1)} %decode_weights.4._.refs_0_.weight_ref, bf16[2,256,1024]{2,1,0:T(8,128)(2,1)} %copy-done.3, ...), custom_call_target="tpu_custom_call" | custom-call | flops 24159191040 | bytes 7864320 | tf_op jit(solution)/shard_map/weight_gradients/pallas_call | solution.py:255
  324.2 2.6 fusion.5
  326.8 2.4 fusion.4
  330.4 14.0 %weight_gradients.7 = (f32[2,64,256]{2,1,0:T(8,128)}, f32[8,1024]{1,0:T(8,128)}) custom-call(s32[1]{0:T(128)} %bitcast.me_ref, bf16[8,2048,256]{2,1,0:T(8,128)(2,1)} %bitcast.50, bf16[2048,1024]{1,0:T(8,128)(2,1)} %decode_weights.4._.refs_0_.weight_ref, f32[8,1024]{1,0:T(8,128)} %get-tuple-element.97._, s32[2,256,3584]{2,1,0:T(8,128)} %refs_1_.3, ...), custom_call_target="tpu_custom_call" | custom-call | flops 14495514624 | bytes 4718592 | tf_op jit(solution)/shard_map/weight_gradients/pallas_call | solution.py:255
  (127 shorter events, 41.2 us)
Async XLA Ops:
  7.2 102.8 %all-gather.2.cloned.1.call-start = ((), (), s32[]{:S(2)}) async-start(), calls=%async_computation | async-start | bytes 9437184 | tf_op jit(solution)/shard_map/all_gather | solution.py:461
  9.1 98.8 %copy-start.1 = (bf16[512,1280]{1,0:T(8,128)(2,1)}, bf16[512,1280]{1,0:T(8,128)(2,1)S(1)}, u32[]{:S(2)}) copy-start(bf16[512,1280]{1,0:T(8,128)(2,1)S(1)} %get-tuple-element.78.refs_2_) | copy-start | bytes 3932164
  12.9 49.2 %collective-permute-start.1 = (bf16[512,1280]{1,0:T(8,128)(2,1)S(1)}, bf16[512,1280]{1,0:T(8,128)(2,1)}, u32[]{:S(2)}, u32[]{:S(2)}) collective-permute-start(bf16[512,1280]{1,0:T(8,128)(2,1)S(1)} %get-tuple-element.66.refs_2_), channel_id=1, source_target_pairs={{8,0},{16,8},{24,16},{0,24},{9,1},{17,9},{25,17},{1,25},{10,2},{18... | collective-permute-start | bytes 3932168 | tf_op jit(solution)/shard_map/ppermute | solution.py:128
  18.0 57.1 %collective-permute-start = (bf16[512,1280]{1,0:T(8,128)(2,1)S(1)}, bf16[512,1280]{1,0:T(8,128)(2,1)}, u32[]{:S(2)}, u32[]{:S(2)}) collective-permute-start(bf16[512,1280]{1,0:T(8,128)(2,1)S(1)} %get-tuple-element.66.refs_2_), channel_id=1, source_target_pairs={{0,8},{8,16},{16,24},{24,0},{1,9},{9,17},{17,25},{25,1},{2,10},{10... | collective-permute-start | bytes 3932168 | tf_op jit(solution)/shard_map/ppermute | solution.py:127
  75.2 31.7 %collective-permute-start.2 = (bf16[512,1280]{1,0:T(8,128)(2,1)}, bf16[512,1280]{1,0:T(8,128)(2,1)S(1)}, u32[]{:S(2)}, u32[]{:S(2)}) collective-permute-start(bf16[512,1280]{1,0:T(8,128)(2,1)} %collective-permute-done.refs_3_), channel_id=1, source_target_pairs={{0,8},{8,16},{16,24},{24,0},{1,9},{9,17},{17,25},{25,1},{2,10},{10... | collective-permute-start | bytes 3932168 | tf_op jit(solution)/shard_map/ppermute | solution.py:141
  107.9 56.8 %collective-permute-start.4 = (bf16[512,1280]{1,0:T(8,128)(2,1)S(1)}, bf16[512,1280]{1,0:T(8,128)(2,1)S(1)}, u32[]{:S(2)}, u32[]{:S(2)}) collective-permute-start(bf16[512,1280]{1,0:T(8,128)(2,1)S(1)} %get-tuple-element.78.refs_2_), channel_id=1, source_target_pairs={{8,0},{16,8},{24,16},{0,24},{9,1},{17,9},{25,17},{1,25},{10,2},{18... | collective-permute-start | bytes 3932168 | tf_op jit(solution)/shard_map/ppermute | solution.py:128
  107.9 56.8 %collective-permute-start.3 = (bf16[512,1280]{1,0:T(8,128)(2,1)S(1)}, bf16[512,1280]{1,0:T(8,128)(2,1)}, u32[]{:S(2)}, u32[]{:S(2)}) collective-permute-start(bf16[512,1280]{1,0:T(8,128)(2,1)S(1)} %get-tuple-element.78.refs_2_), channel_id=1, source_target_pairs={{0,8},{8,16},{16,24},{24,0},{1,9},{9,17},{17,25},{25,1},{2,10},{10... | collective-permute-start | bytes 3932168 | tf_op jit(solution)/shard_map/ppermute | solution.py:127
  164.7 29.6 %collective-permute-start.5 = (bf16[512,1280]{1,0:T(8,128)(2,1)}, bf16[512,1280]{1,0:T(8,128)(2,1)S(1)}, u32[]{:S(2)}, u32[]{:S(2)}) collective-permute-start(bf16[512,1280]{1,0:T(8,128)(2,1)} %collective-permute-done.3.refs_3_), channel_id=1, source_target_pairs={{0,8},{8,16},{16,24},{24,0},{1,9},{9,17},{17,25},{25,1},{2,10},{10... | collective-permute-start | bytes 3932168 | tf_op jit(solution)/shard_map/ppermute | solution.py:141
  194.3 43.1 %collective-permute-start.7 = (bf16[512,1024]{1,0:T(8,128)(2,1)S(1)}, bf16[512,1024]{1,0:T(8,128)(2,1)S(1)}, u32[]{:S(2)}, u32[]{:S(2)}) collective-permute-start(bf16[512,1024]{1,0:T(8,128)(2,1)S(1)} %copy-done.4), channel_id=1, source_target_pairs={{8,0},{16,8},{24,16},{0,24},{9,1},{17,9},{25,17},{1,25},{10,2},{18... | collective-permute-start | bytes 3145736 | tf_op jit(solution)/shard_map/ppermute | solution.py:128
  196.7 46.4 %collective-permute-start.6 = (bf16[512,1024]{1,0:T(8,128)(2,1)S(1)}, bf16[512,1024]{1,0:T(8,128)(2,1)S(1)}, u32[]{:S(2)}, u32[]{:S(2)}) collective-permute-start(bf16[512,1024]{1,0:T(8,128)(2,1)S(1)} %copy-done.4), channel_id=1, source_target_pairs={{0,8},{8,16},{16,24},{24,0},{1,9},{9,17},{17,25},{25,1},{2,10},{10... | collective-permute-start | bytes 3145736 | tf_op jit(solution)/shard_map/ppermute | solution.py:127
  243.1 25.1 %collective-permute-start.8 = (bf16[512,1024]{1,0:T(8,128)(2,1)S(1)}, bf16[512,1024]{1,0:T(8,128)(2,1)S(1)}, u32[]{:S(2)}, u32[]{:S(2)}) collective-permute-start(bf16[512,1024]{1,0:T(8,128)(2,1)S(1)} %collective-permute-done.6.refs_2_.refs_5_), channel_id=1, source_target_pairs={{0,8},{8,16},{16,24},{24,0},{1,9},{9,17},{17,25},{25,1},{2,10},{10... | collective-permute-start | bytes 3145736 | tf_op jit(solution)/shard_map/ppermute | solution.py:141
  280.9 13.0 %collective-permute-start.9 = (bf16[1024,1024]{1,0:T(8,128)(2,1)}, bf16[1024,1024]{1,0:T(8,128)(2,1)}, u32[]{:S(2)}, u32[]{:S(2)}) collective-permute-start(bf16[1024,1024]{1,0:T(8,128)(2,1)} %get-tuple-element.90), channel_id=1, source_target_pairs={{0,1},{1,0},{2,3},{3,2},{4,5},{5,4},{6,7},{7,6},{8,9},{9,8},{10,11... | collective-permute-start | bytes 6291464 | tf_op jit(solution)/shard_map/ppermute | solution.py:502
  280.9 16.9 %collective-permute-start.11 = (bf16[1024,1024]{1,0:T(8,128)(2,1)}, bf16[1024,1024]{1,0:T(8,128)(2,1)S(1)}, u32[]{:S(2)}, u32[]{:S(2)}) collective-permute-start(bf16[1024,1024]{1,0:T(8,128)(2,1)} %get-tuple-element.92), channel_id=1, source_target_pairs={{0,1},{1,0},{2,3},{3,2},{4,5},{5,4},{6,7},{7,6},{8,9},{9,8},{10,11... | collective-permute-start | bytes 6291464 | tf_op jit(solution)/shard_map/ppermute | solution.py:502
  296.2 28.0 %collective-permute-start.10 = (bf16[2,256,1024]{2,1,0:T(8,128)(2,1)S(1)}, bf16[2,256,1024]{2,1,0:T(8,128)(2,1)}, u32[]{:S(2)}, u32[]{:S(2)}) collective-permute-start(bf16[2,256,1024]{2,1,0:T(8,128)(2,1)S(1)} %fusion._), channel_id=1, source_target_pairs={{0,2},{1,3},{2,0},{3,1},{4,6},{5,7},{6,4},{7,5},{8,10},{9,11},{10,... | collective-permute-start | bytes 3145736 | tf_op jit(solution)/shard_map/ppermute | solution.py:389
  299.2 27.6 %collective-permute-start.12 = (bf16[2,256,1024]{2,1,0:T(8,128)(2,1)}, bf16[2,256,1024]{2,1,0:T(8,128)(2,1)}, u32[]{:S(2)}, u32[]{:S(2)}) collective-permute-start(bf16[2,256,1024]{2,1,0:T(8,128)(2,1)} %fusion.1), channel_id=1, source_target_pairs={{0,4},{1,5},{2,6},{3,7},{4,0},{5,1},{6,2},{7,3},{8,12},{9,13},{10,... | collective-permute-start | bytes 3145736 | tf_op jit(solution)/shard_map/ppermute | solution.py:389
  329.2 16.0 %collective-permute-start.13 = (bf16[256,1024]{1,0:T(8,128)(2,1)}, bf16[256,1024]{1,0:T(8,128)(2,1)S(1)}, u32[]{:S(2)}, u32[]{:S(2)}) collective-permute-start(bf16[256,1024]{1,0:T(8,128)(2,1)} %fusion.5), channel_id=1, source_target_pairs={{0,4},{1,5},{2,6},{3,7},{4,0},{5,1},{6,2},{7,3},{8,12},{9,13},{10,... | collective-permute-start | bytes 1572872 | tf_op jit(solution)/shard_map/ppermute | solution.py:389
  329.7 17.4 %collective-permute-start.14 = (bf16[256,1024]{1,0:T(8,128)(2,1)}, bf16[256,1024]{1,0:T(8,128)(2,1)S(1)}, u32[]{:S(2)}, u32[]{:S(2)}) collective-permute-start(bf16[256,1024]{1,0:T(8,128)(2,1)} %fusion.4), channel_id=1, source_target_pairs={{0,2},{1,3},{2,0},{3,1},{4,6},{5,7},{6,4},{7,5},{8,10},{9,11},{10,... | collective-permute-start | bytes 1572872 | tf_op jit(solution)/shard_map/ppermute | solution.py:389
  350.6 4.9 %collective-permute-start.16 = (f32[7680]{0:T(1024)S(1)}, f32[7680]{0:T(1024)S(1)}, u32[]{:S(2)}, u32[]{:S(2)}) collective-permute-start(f32[7680]{0:T(1024)S(1)} %pad_maximum_fusion.1), channel_id=1, source_target_pairs={{0,16},{8,24},{16,0},{24,8},{1,17},{9,25},{17,1},{25,9},{2,18},{10... | collective-permute-start | bytes 92168 | tf_op jit(solution)/shard_map/ppermute | solution.py:410
  351.3 5.7 %collective-permute-start.17 = (f32[7680]{0:T(1024)S(1)}, f32[7680]{0:T(1024)S(1)}, u32[]{:S(2)}, u32[]{:S(2)}) collective-permute-start(f32[7680]{0:T(1024)S(1)} %pad_maximum_fusion.1), channel_id=1, source_target_pairs={{0,24},{8,16},{16,8},{24,0},{1,25},{9,17},{17,9},{25,1},{2,26},{10... | collective-permute-start | bytes 92168 | tf_op jit(solution)/shard_map/ppermute | solution.py:410
  352.3 4.7 %collective-permute-start.15 = (f32[7680]{0:T(1024)S(1)}, f32[7680]{0:T(1024)S(1)}, u32[]{:S(2)}, u32[]{:S(2)}) collective-permute-start(f32[7680]{0:T(1024)S(1)} %pad_maximum_fusion.1), channel_id=1, source_target_pairs={{0,8},{8,0},{16,24},{24,16},{1,9},{9,1},{17,25},{25,17},{2,10},{10... | collective-permute-start | bytes 92168 | tf_op jit(solution)/shard_map/ppermute | solution.py:410
  357.1 3.8 %collective-permute-start.19 = (f32[4096]{0:T(1024)S(1)}, f32[4096]{0:T(1024)S(1)}, u32[]{:S(2)}, u32[]{:S(2)}) collective-permute-start(f32[4096]{0:T(1024)S(1)} %slice.30), channel_id=1, source_target_pairs={{0,2},{1,3},{2,0},{3,1},{4,6},{5,7},{6,4},{7,5},{8,10},{9,11},{10,... | collective-permute-start | bytes 49160 | tf_op jit(solution)/shard_map/ppermute | solution.py:410
  358.5 3.2 collective-permute-start.20
  358.5 3.2 collective-permute-start.18
  361.7 3.8 %collective-permute-start.21 = (f32[4096]{0:T(1024)S(1)}, f32[4096]{0:T(1024)S(1)}, u32[]{:S(2)}, u32[]{:S(2)}) collective-permute-start(f32[4096]{0:T(1024)S(1)} %add_add_fusion.2), channel_id=1, source_target_pairs={{0,4},{1,5},{2,6},{3,7},{4,0},{5,1},{6,2},{7,3},{8,12},{9,13},{10,... | collective-permute-start | bytes 49160 | tf_op jit(solution)/shard_map/ppermute | solution.py:410
  (25 other events, 249.1 us)
Sparse Core Ops, SparseCore 0:
  13.1 57.0 all-gather.1

commit v4 on v3

--- a/solution.py
+++ b/solution.py
@@ -315,40 +315,52 @@
     )(*args)
 
 
-def last_kernel(n, rows, block, fulls, count, me_ref, early_ref, *refs):
-    cots, weights, refs = refs[:fulls], refs[fulls : 2 * fulls + 1], refs[2 * fulls + 1 :]
+def last_kernel(n, rows, count, me_ref, early_ref, weight_ref, *refs):
     pieces, (one_ref, two_ref, cot_ref) = refs[:count], refs[count:]
-
-    @pl.when(pl.program_id(0) == 0)
+    step, half = pl.program_id(0), pl.num_programs(0) // 2
+    width = cot_ref.shape[1]
+
+    @pl.when(step == 0)
     def _():
-        place_pieces(me_ref[0], n, rows, pieces, cot_ref)
-
-    start = pl.multiple_of((2 * pl.program_id(0) + me_ref[1]) * block, 16)
-    left = jnp.concatenate([ref[...] for ref in cots] + [cot_ref[pl.ds(start, block), :]], axis=1)
-    half = one_ref.shape[1]
-    for out_ref, columns in ((one_ref, slice(0, half)), (two_ref, slice(half, 2 * half))):
-        right = jnp.concatenate([ref[columns, :] for ref in weights], axis=1)
-        part = lax.dot_general(left, right, (((1,), (1,)), ((), ())), preferred_element_type=jnp.float32)
-        out_ref[...] = (early_ref[:, columns] + part).astype(out_ref.dtype)
-
-
-def last_input_gradient(me, n, block, cots, pieces, weights, early, dtype):
-    rows = pieces[0].shape[0]
+        for piece, (shift, _, _) in zip(pieces, [(0, 0, rows)] + piece_places(n, rows)):
+            chunk = lax.rem(me_ref[0] + shift + 2 * n, n)
+            start = pl.multiple_of(chunk * (rows // 2), 16)
+            cot_ref[pl.ds(start, rows // 2), :] = piece[...].reshape(rows // 2, width)
+
+    part = lax.dot_general(cot_ref[...], weight_ref[...], (((1,), (1,)), ((), ())), preferred_element_type=jnp.float32)
+    total = (early_ref[...].reshape(part.shape) + part).astype(one_ref.dtype)
+
+    @pl.when(step < half)
+    def _():
+        one_ref[...] = total
+
+    @pl.when(step >= half)
+    def _():
+        two_ref[...] = total
+
+
+def last_input_gradient(me, n, block, pieces, weights, early, dtype):
+    rows, width = pieces[0].shape
     tokens, features = early.shape
     once = pl.Buffered(1)
-    half = tokens // (2 * block)
-    width = sum(w.shape[1] for w in weights)
+    tile = largest_tile(features // 2, 512)
+    half = features // 2 // tile
+    pairs = rows // (2 * block)
     return pl.pallas_call(
-        functools.partial(last_kernel, n, rows, block, len(cots), len(pieces)),
+        functools.partial(last_kernel, n, rows, len(pieces)),
         grid_spec=pltpu.PrefetchScalarGridSpec(
             num_scalar_prefetch=1,
-            grid=(half,),
-            in_specs=[pl.BlockSpec((block, features), lambda t, who: (2 * t + who[1], 0))]
-            + [pl.BlockSpec((block, c.shape[1]), lambda t, who: (2 * t + who[1], 0)) for c in cots]
-            + [pl.BlockSpec(w.shape, lambda t, who: (0, 0), pipeline_mode=once) for w in weights]
-            + [pl.BlockSpec(p.shape, lambda t, who: (0, 0), pipeline_mode=once) for p in pieces],
-            out_specs=[pl.BlockSpec((block, features // 2), lambda t, who: (t, 0))] * 2,
-            scratch_shapes=[pltpu.VMEM((tokens, pieces[0].shape[1]), jnp.bfloat16)],
+            grid=(2 * half,),
+            in_specs=[
+                pl.BlockSpec((tokens // (2 * block), 1, block, tile), lambda f, who: (0, who[1], 0, f)),
+                pl.BlockSpec((tile, width), lambda f, who: (f, 0)),
+            ]
+            + [pl.BlockSpec((pairs, 1, block, width), lambda f, who: (0, who[1], 0, 0), pipeline_mode=once) for _ in pieces],
+            out_specs=[
+                pl.BlockSpec((tokens // 2, tile), lambda f, who: (0, jnp.minimum(f, half - 1))),
+                pl.BlockSpec((tokens // 2, tile), lambda f, who: (0, jnp.maximum(f - half, 0))),
+            ],
+            scratch_shapes=[pltpu.VMEM((tokens // 2, width), jnp.bfloat16)],
         ),
         out_shape=[jax.ShapeDtypeStruct((tokens // 2, features // 2), dtype)] * 2,
         compiler_params=pltpu.CompilerParams(vmem_limit_bytes=VMEM),
@@ -356,7 +368,12 @@
             flops=2 * tokens * features * width, bytes_accessed=3 * tokens * features, transcendentals=0
         ),
         name="last_input_gradient",
-    )(me, early, *cots, *weights, *pieces)
+    )(
+        me,
+        early.reshape(tokens // (2 * block), 2, block, features),
+        weights,
+        *[piece.reshape(pairs, 2, block, width) for piece in pieces],
+    )
 
 
 class HalvingScatter:
@@ -396,10 +413,13 @@
         left = [b for b in reversed(self.order) if b not in order[: self.step]]
         return left.index(order[self.step]), order[self.step]
 
-    def finish(self, gate):
-        while self.step < len(self.order):
-            gate = self.exchange(gate)
-        return jnp.concatenate([self.total(t) for t in self.terms], axis=-1).astype(jnp.bfloat16), gate
+    def hold(self, gate):
+        came, gate = lax.optimization_barrier(([terms[-1] for terms in self.terms], gate))
+        self.terms = [[*terms[:-1], new] for terms, new in zip(self.terms, came)]
+        return gate
+
+    def finish(self):
+        return jnp.concatenate([self.total(t) for t in self.terms], axis=-1).astype(jnp.bfloat16)
 
 
 def butterfly_sum(value, axis, size):
@@ -493,11 +513,11 @@
                     gate = weights[later]
 
     block = inputs.shape[0]
-    if early is not None and n_dout > 1 and n_dout & (n_dout - 1) == 0:
+    if early is not None and n_dout > 1 and n_dout & (n_dout - 1) == 0 and owns[0].shape[0] % (2 * block) == 0:
         core = lax.axis_index("dout").astype(jnp.int32) & 1
         both_me = [jnp.stack([me[0], 1 - core]), jnp.stack([me[0], core])]
         pieces = rings[final].pieces
-        rest = (n_din, block, cots[summed:], pieces, weights[summed:], early)
+        rest = (n_din, block, pieces, weights[final], early)
         give = last_input_gradient(both_me[0], *rest, jnp.bfloat16)
         got = [lax.ppermute(half, "dout", [(a, a ^ 1) for a in range(n_dout)]) for half in give]
         keep = last_input_gradient(both_me[1], *rest, jnp.float32)
@@ -507,10 +527,12 @@
             gate = lax.optimization_barrier(scatter.exchange())[0]
         cut = 5 / 8 if codes.shape[1] >= 256 else 1
         gate = run_gradients(final, gate, (0, cut))
-        grad_input, gate = scatter.finish(gate)
+        while scatter.step < len(scatter.order):
+            gate = scatter.exchange(gate)
         if cut < 1:
             run_gradients(final, gate, (cut, 1))
-        grad_input, books[-1] = lax.optimization_barrier((grad_input, books[-1]))
+            books[-1] = scatter.hold(books[-1])
+        grad_input = scatter.finish()
     else:
         run_gradients(final, gate)
         rows = early_input_gradient(cots, weights, None, gate)

time: 375 us -> 373 us (level)
    ppermute x7, waiting for transfers between devices: 6.8 us -> 2.95 us  [other(): return lax.ppermute(value, axis, [(a, a ^ bits) for a in range(size)])]
  transfers between devices with their start and end apart: 23 -> 23, of which waited for: 11 -> 9; matrix products, arithmetic and copies ran while one was open for 4% -> 5% of each run, Pallas kernels for 61% -> 62%
where the time goes in v4:
time: 373 us; the launch traced here: 372 us
  Pallas kernels  244 us (65%)
  waiting for transfers between devices  59.7 us (16%)
  starting transfers between devices  23.7 us (6%)
  other arithmetic  20.3 us (5%)
  between operations  15 us (4%)
  local copies, waits for them, and re-layouts  9.58 us (3%)
    pallas_call x4, Pallas kernels, gradients(): pl.pallas_call(functools.partial(gradient_kernel, n, tile, width, blocks,...  118 us
    pallas_call x3, Pallas kernels, decode(): pl.pallas_call(functools.partial(decode_kernel, tile_groups, unit), grid=...  56.3 us
    pallas_call x2, Pallas kernels, early_input_gradient(): pl.pallas_call(functools.partial(early_kernel, len(cots), total is not No...  42 us
    ppermute x3, waiting for transfers between devices, finish(): self.pieces.append(lax.ppermute(self.left, 'din', self.forward))  23.9 us
    pallas_call x2, Pallas kernels, last_input_gradient(): pl.pallas_call(functools.partial(last_kernel, n, rows, len(pieces)), grid...  23.7 us
    ppermute x3, waiting for transfers between devices, begin(): self.left = lax.ppermute(self.left, 'din', self.forward)  18.7 us
    ppermute x3, waiting for transfers between devices, begin(): self.right = lax.ppermute(self.right, 'din', self.backward)  14.1 us
    convert_element_type x4, other arithmetic, exchange(): gives.append(give.astype(jnp.bfloat16))  9.63 us
  transfers between devices with their start and end apart: 23, of which 9 were waited for; matrix products, arithmetic and copies ran while one was open for 5% of the time, Pallas kernels for 62%

profile of v4, /device:TPU:0, one launch (start us, length us, event | category | flops | bytes accessed | tf_op | source)
XLA Modules:
  0.0 372.5 jit_solution(10660632536151781378)
XLA Ops:
  9.1 3.8 %transpose_inputs.1 = bf16[2048,256]{1,0:T(8,128)(2,1)} custom-call(bf16[256,2048]{1,0:T(8,128)(2,1)} %in_ref), custom_call_target="tpu_custom_call" | custom-call | tf_op jit(solution)/shard_map/transpose_inputs/pallas_call | solution.py:151
  12.9 5.1 %collective-permute-start.1 = (bf16[512,1280]{1,0:T(8,128)(2,1)S(1)}, bf16[512,1280]{1,0:T(8,128)(2,1)}, u32[]{:S(2)}, u32[]{:S(2)}) collective-permute-start(bf16[512,1280]{1,0:T(8,128)(2,1)S(1)} %get-tuple-element.67.refs_2_), channel_id=1, source_target_pairs={{8,0},{16,8},{24,16},{0,24},{9,1},{17,9},{25,17},{1,25},{10,2},{18... | collective-permute-start | bytes 3932168 | tf_op jit(solution)/shard_map/ppermute | solution.py:128
  18.0 2.3 slice.24.refs_4_
  24.0 18.9 %decode_weights.5.weight_ref.refs_1_ = bf16[2048,1280]{1,0:T(8,128)(2,1)} custom-call(s32[2,256,3584]{2,1,0:T(8,128)} %refs_1_.3, s32[2,8,128]{2,1,0:T(8,128)} %fusion.12.table_ref, f32[1,3584]{1,0:T(1,128)} %mul.97.coef_ref, f32[1,3584]{1,0:T(1,128)} %reshape.108._.refs_1_.refs_2_.refs_3_), custom_call_target="tpu_custom_call" | custom-call | flops 23592960000 | bytes 7864320 | tf_op jit(solution)/shard_map/decode_weights/pallas_call | solution.py:89
  43.0 19.1 %decode_weights.3._.weight_ref.refs_1_ = bf16[2048,1280]{1,0:T(8,128)(2,1)} custom-call(s32[2,256,3584]{2,1,0:T(8,128)} %refs_1_.3, s32[2,8,128]{2,1,0:T(8,128)} %fusion.12.table_ref, f32[1,3584]{1,0:T(1,128)} %mul.97.coef_ref, f32[1,3584]{1,0:T(1,128)} %reshape.108._.refs_1_.refs_2_.refs_3_), custom_call_target="tpu_custom_call" | custom-call | flops 23592960000 | bytes 7864320 | tf_op jit(solution)/shard_map/decode_weights/pallas_call | solution.py:89
  62.1 13.0 %collective-permute-done.refs_3_ = bf16[512,1280]{1,0:T(8,128)(2,1)} collective-permute-done((bf16[512,1280]{1,0:T(8,128)(2,1)S(1)}, bf16[512,1280]{1,0:T(8,128)(2,1)}, u32[]{:S(2)}, u32[]{:S(2)}) %collective-permute-start) | collective-permute-done | bytes 1310752 | tf_op jit(solution)/shard_map/ppermute | solution.py:127
  76.8 18.2 %decode_weights.4._.weight_ref = bf16[2048,1024]{1,0:T(8,128)(2,1)} custom-call(s32[2,256,3584]{2,1,0:T(8,128)} %refs_1_.3, s32[2,8,128]{2,1,0:T(8,128)} %fusion.12.table_ref, f32[1,3584]{1,0:T(1,128)} %mul.97.coef_ref, bf16[2048,1280]{1,0:T(8,128)(2,1)} %decode_weights.3._.weight_ref.refs_1_), custom_call_target="tpu_custom_call" | custom-call | flops 18874368000 | bytes 6291456 | tf_op jit(solution)/shard_map/decode_weights/pallas_call | solution.py:89
  95.0 11.8 %collective-permute-done.2.refs_5_ = bf16[512,1280]{1,0:T(8,128)(2,1)S(1)} collective-permute-done((bf16[512,1280]{1,0:T(8,128)(2,1)}, bf16[512,1280]{1,0:T(8,128)(2,1)S(1)}, u32[]{:S(2)}, u32[]{:S(2)}) %collective-permute-start.2) | collective-permute-done | bytes 1310752 | tf_op jit(solution)/shard_map/ppermute | solution.py:141
  109.9 40.7 %weight_gradients.4 = (bf16[2048,1280]{1,0:T(8,128)(2,1)}, f32[2,64,256]{2,1,0:T(8,128)}, f32[8,1280]{1,0:T(8,128)}) custom-call(s32[1]{0:T(128)} %bitcast.me_ref, bf16[8,2048,256]{2,1,0:T(8,128)(2,1)} %bitcast.54, bf16[2048,1280]{1,0:T(8,128)(2,1)} %decode_weights.5.weight_ref.refs_1_, bf16[2048,1024]{1,0:T(8,128)(2,1)} %decode_weights.4._.weight_ref, ...), custom_call_target="tpu_custom_call" | custom-call | flops 48318382080 | bytes 15728640 | tf_op jit(solution)/shard_map/weight_gradients/pallas_call | solution.py:255
  150.6 14.1 %collective-permute-done.4.refs_4_ = bf16[512,1280]{1,0:T(8,128)(2,1)S(1)} collective-permute-done((bf16[512,1280]{1,0:T(8,128)(2,1)S(1)}, bf16[512,1280]{1,0:T(8,128)(2,1)S(1)}, u32[]{:S(2)}, u32[]{:S(2)}) %collective-permute-start.4) | collective-permute-done | bytes 1310752 | tf_op jit(solution)/shard_map/ppermute | solution.py:128
  165.2 19.1 %early_input_gradient.2._.refs_2_ = f32[2048,2048]{1,0:T(8,128)} custom-call(bf16[2048,1280]{1,0:T(8,128)(2,1)} %get-tuple-element.75.refs_0_, bf16[2048,1280]{1,0:T(8,128)(2,1)} %decode_weights.5.weight_ref.refs_1_, f32[8,1280]{1,0:T(8,128)} %get-tuple-element.76.refs_2_), custom_call_target="tpu_custom_call" | custom-call | flops 16106127360 | bytes 27262976 | tf_op jit(solution)/shard_map/early_input_gradient/pallas_call | solution.py:298
  184.3 10.0 %collective-permute-done.5.refs_5_ = bf16[512,1280]{1,0:T(8,128)(2,1)S(1)} collective-permute-done((bf16[512,1280]{1,0:T(8,128)(2,1)}, bf16[512,1280]{1,0:T(8,128)(2,1)S(1)}, u32[]{:S(2)}, u32[]{:S(2)}) %collective-permute-start.5) | collective-permute-done | bytes 1310752 | tf_op jit(solution)/shard_map/ppermute | solution.py:141
  194.3 2.3 collective-permute-start.7
  196.7 40.8 %weight_gradients.5 = (bf16[2048,1280]{1,0:T(8,128)(2,1)}, f32[2,64,256]{2,1,0:T(8,128)}, f32[8,1280]{1,0:T(8,128)}) custom-call(s32[1]{0:T(128)} %bitcast.me_ref, bf16[8,2048,256]{2,1,0:T(8,128)(2,1)} %bitcast.55, bf16[2048,1280]{1,0:T(8,128)(2,1)} %decode_weights.3._.weight_ref.refs_1_, f32[2048,2048]{1,0:T(8,128)} %early_input_gradient.2._.refs_2_, ...), custom_call_target="tpu_custom_call" | custom-call | flops 48318382080 | bytes 15728640 | tf_op jit(solution)/shard_map/weight_gradients/pallas_call | solution.py:255
  237.4 5.6 %collective-permute-done.6.refs_5_ = bf16[512,1024]{1,0:T(8,128)(2,1)S(1)} collective-permute-done((bf16[512,1024]{1,0:T(8,128)(2,1)S(1)}, bf16[512,1024]{1,0:T(8,128)(2,1)S(1)}, u32[]{:S(2)}, u32[]{:S(2)}) %collective-permute-start.6) | collective-permute-done | bytes 1048608 | tf_op jit(solution)/shard_map/ppermute | solution.py:127
  243.2 22.9 %early_input_gradient.3 = f32[2048,2048]{1,0:T(8,128)} custom-call(bf16[2048,1280]{1,0:T(8,128)(2,1)} %get-tuple-element.83.refs_0_, bf16[2048,1280]{1,0:T(8,128)(2,1)} %decode_weights.3._.weight_ref.refs_1_, f32[2048,2048]{1,0:T(8,128)} %early_input_gradient.2._.refs_2_, f32[8,1280]{1,0:T(8,128)} %get-tuple-element.86.refs_3_), custom_call_target="tpu_custom_call", output_to_operand_aliasing={{}: (2, {})} | custom-call | flops 16106127360 | bytes 27262976 | tf_op jit(solution)/shard_map/early_input_gradient/pallas_call | solution.py:298
  269.2 11.3 %last_input_gradient.3 = (bf16[1024,1024]{1,0:T(8,128)(2,1)}, bf16[1024,1024]{1,0:T(8,128)(2,1)}) custom-call(s32[2]{0:T(128)} %get-tuple-element.146.me_ref, f32[4,2,256,2048]{3,2,1,0:T(8,128)} %bitcast.64, bf16[2048,1024]{1,0:T(8,128)(2,1)} %decode_weights.4._.weight_ref, bf16[1,2,256,1024]{3,2,1,0:T(8,128)(2,1)} %bitcast.51, ...), custom_call_target="tpu_custom_call" | custom-call | flops 8589934592 | bytes 12582912 | tf_op jit(solution)/shard_map/last_input_gradient/pallas_call | solution.py:349
  281.1 12.3 %last_input_gradient.2 = (f32[1024,1024]{1,0:T(8,128)}, f32[1024,1024]{1,0:T(8,128)}) custom-call(s32[2]{0:T(128)} %get-tuple-element.145.me_ref, f32[4,2,256,2048]{3,2,1,0:T(8,128)} %bitcast.65, bf16[2048,1024]{1,0:T(8,128)(2,1)} %decode_weights.4._.weight_ref, bf16[1,2,256,1024]{3,2,1,0:T(8,128)(2,1)} %bitcast.52, bf16[1,2,256,1024]{3,2,1,0:T(8,128)(2,1)} %bitcast.61, ...), custom_call_target="tpu_custom_call" | custom-call | flops 8589934592 | bytes 12582912 | tf_op jit(solution)/shard_map/last_input_gradient/pallas_call | solution.py:349
  293.4 2.1 fusion._
  297.1 2.6 fusion.1
  301.2 22.7 %weight_gradients.6 = (bf16[2048,1024]{1,0:T(8,128)(2,1)}, f32[2,64,256]{2,1,0:T(8,128)}, f32[8,1024]{1,0:T(8,128)}) custom-call(s32[1]{0:T(128)} %bitcast.me_ref, bf16[8,2048,256]{2,1,0:T(8,128)(2,1)} %bitcast.56, bf16[2048,1024]{1,0:T(8,128)(2,1)} %decode_weights.4._.weight_ref, bf16[2,256,1024]{2,1,0:T(8,128)(2,1)} %copy-done.3, s32[2,256,3584]{2,1,0:T(8,128)} %refs_1_.3, ...), custom_call_target="tpu_custom_call" | custom-call | flops 24159191040 | bytes 7864320 | tf_op jit(solution)/shard_map/weight_gradients/pallas_call | solution.py:255
  324.7 2.4 fusion.5
  327.1 2.5 fusion.4
  330.8 14.2 %weight_gradients.7 = (f32[2,64,256]{2,1,0:T(8,128)}, f32[8,1024]{1,0:T(8,128)}) custom-call(s32[1]{0:T(128)} %bitcast.me_ref, bf16[8,2048,256]{2,1,0:T(8,128)(2,1)} %bitcast.57, bf16[2048,1024]{1,0:T(8,128)(2,1)} %decode_weights.4._.weight_ref, f32[8,1024]{1,0:T(8,128)} %get-tuple-element.98._, s32[2,256,3584]{2,1,0:T(8,128)} %refs_1_.3, ...), custom_call_target="tpu_custom_call" | custom-call | flops 14495514624 | bytes 4718592 | tf_op jit(solution)/shard_map/weight_gradients/pallas_call | solution.py:255
  (123 shorter events, 39.3 us)
Async XLA Ops:
  7.2 102.8 %all-gather.2.cloned.1.call-start = ((), (), s32[]{:S(2)}) async-start(), calls=%async_computation | async-start | bytes 9437184 | tf_op jit(solution)/shard_map/all_gather | solution.py:481
  9.1 98.8 %copy-start.1 = (bf16[512,1280]{1,0:T(8,128)(2,1)}, bf16[512,1280]{1,0:T(8,128)(2,1)S(1)}, u32[]{:S(2)}) copy-start(bf16[512,1280]{1,0:T(8,128)(2,1)S(1)} %get-tuple-element.79.refs_2_) | copy-start | bytes 3932164
  12.9 49.2 %collective-permute-start.1 = (bf16[512,1280]{1,0:T(8,128)(2,1)S(1)}, bf16[512,1280]{1,0:T(8,128)(2,1)}, u32[]{:S(2)}, u32[]{:S(2)}) collective-permute-start(bf16[512,1280]{1,0:T(8,128)(2,1)S(1)} %get-tuple-element.67.refs_2_), channel_id=1, source_target_pairs={{8,0},{16,8},{24,16},{0,24},{9,1},{17,9},{25,17},{1,25},{10,2},{18... | collective-permute-start | bytes 3932168 | tf_op jit(solution)/shard_map/ppermute | solution.py:128
  18.0 57.1 %collective-permute-start = (bf16[512,1280]{1,0:T(8,128)(2,1)S(1)}, bf16[512,1280]{1,0:T(8,128)(2,1)}, u32[]{:S(2)}, u32[]{:S(2)}) collective-permute-start(bf16[512,1280]{1,0:T(8,128)(2,1)S(1)} %get-tuple-element.67.refs_2_), channel_id=1, source_target_pairs={{0,8},{8,16},{16,24},{24,0},{1,9},{9,17},{17,25},{25,1},{2,10},{10... | collective-permute-start | bytes 3932168 | tf_op jit(solution)/shard_map/ppermute | solution.py:127
  75.2 31.7 %collective-permute-start.2 = (bf16[512,1280]{1,0:T(8,128)(2,1)}, bf16[512,1280]{1,0:T(8,128)(2,1)S(1)}, u32[]{:S(2)}, u32[]{:S(2)}) collective-permute-start(bf16[512,1280]{1,0:T(8,128)(2,1)} %collective-permute-done.refs_3_), channel_id=1, source_target_pairs={{0,8},{8,16},{16,24},{24,0},{1,9},{9,17},{17,25},{25,1},{2,10},{10... | collective-permute-start | bytes 3932168 | tf_op jit(solution)/shard_map/ppermute | solution.py:141
  107.9 56.8 %collective-permute-start.4 = (bf16[512,1280]{1,0:T(8,128)(2,1)S(1)}, bf16[512,1280]{1,0:T(8,128)(2,1)S(1)}, u32[]{:S(2)}, u32[]{:S(2)}) collective-permute-start(bf16[512,1280]{1,0:T(8,128)(2,1)S(1)} %get-tuple-element.79.refs_2_), channel_id=1, source_target_pairs={{8,0},{16,8},{24,16},{0,24},{9,1},{17,9},{25,17},{1,25},{10,2},{18... | collective-permute-start | bytes 3932168 | tf_op jit(solution)/shard_map/ppermute | solution.py:128
  107.9 56.8 %collective-permute-start.3 = (bf16[512,1280]{1,0:T(8,128)(2,1)S(1)}, bf16[512,1280]{1,0:T(8,128)(2,1)}, u32[]{:S(2)}, u32[]{:S(2)}) collective-permute-start(bf16[512,1280]{1,0:T(8,128)(2,1)S(1)} %get-tuple-element.79.refs_2_), channel_id=1, source_target_pairs={{0,8},{8,16},{16,24},{24,0},{1,9},{9,17},{17,25},{25,1},{2,10},{10... | collective-permute-start | bytes 3932168 | tf_op jit(solution)/shard_map/ppermute | solution.py:127
  164.7 29.6 %collective-permute-start.5 = (bf16[512,1280]{1,0:T(8,128)(2,1)}, bf16[512,1280]{1,0:T(8,128)(2,1)S(1)}, u32[]{:S(2)}, u32[]{:S(2)}) collective-permute-start(bf16[512,1280]{1,0:T(8,128)(2,1)} %collective-permute-done.3.refs_3_), channel_id=1, source_target_pairs={{0,8},{8,16},{16,24},{24,0},{1,9},{9,17},{17,25},{25,1},{2,10},{10... | collective-permute-start | bytes 3932168 | tf_op jit(solution)/shard_map/ppermute | solution.py:141
  194.3 43.1 %collective-permute-start.7 = (bf16[512,1024]{1,0:T(8,128)(2,1)S(1)}, bf16[512,1024]{1,0:T(8,128)(2,1)S(1)}, u32[]{:S(2)}, u32[]{:S(2)}) collective-permute-start(bf16[512,1024]{1,0:T(8,128)(2,1)S(1)} %copy-done.4), channel_id=1, source_target_pairs={{8,0},{16,8},{24,16},{0,24},{9,1},{17,9},{25,17},{1,25},{10,2},{18... | collective-permute-start | bytes 3145736 | tf_op jit(solution)/shard_map/ppermute | solution.py:128
  196.6 46.4 %collective-permute-start.6 = (bf16[512,1024]{1,0:T(8,128)(2,1)S(1)}, bf16[512,1024]{1,0:T(8,128)(2,1)S(1)}, u32[]{:S(2)}, u32[]{:S(2)}) collective-permute-start(bf16[512,1024]{1,0:T(8,128)(2,1)S(1)} %copy-done.4), channel_id=1, source_target_pairs={{0,8},{8,16},{16,24},{24,0},{1,9},{9,17},{17,25},{25,1},{2,10},{10... | collective-permute-start | bytes 3145736 | tf_op jit(solution)/shard_map/ppermute | solution.py:127
  243.1 25.1 %collective-permute-start.8 = (bf16[512,1024]{1,0:T(8,128)(2,1)S(1)}, bf16[512,1024]{1,0:T(8,128)(2,1)S(1)}, u32[]{:S(2)}, u32[]{:S(2)}) collective-permute-start(bf16[512,1024]{1,0:T(8,128)(2,1)S(1)} %collective-permute-done.6.refs_5_), channel_id=1, source_target_pairs={{0,8},{8,16},{16,24},{24,0},{1,9},{9,17},{17,25},{25,1},{2,10},{10... | collective-permute-start | bytes 3145736 | tf_op jit(solution)/shard_map/ppermute | solution.py:141
  280.5 12.9 %collective-permute-start.9 = (bf16[1024,1024]{1,0:T(8,128)(2,1)}, bf16[1024,1024]{1,0:T(8,128)(2,1)S(1)}, u32[]{:S(2)}, u32[]{:S(2)}) collective-permute-start(bf16[1024,1024]{1,0:T(8,128)(2,1)} %get-tuple-element.91), channel_id=1, source_target_pairs={{0,1},{1,0},{2,3},{3,2},{4,5},{5,4},{6,7},{7,6},{8,9},{9,8},{10,11... | collective-permute-start | bytes 6291464 | tf_op jit(solution)/shard_map/ppermute | solution.py:522
  280.5 16.6 %collective-permute-start.11 = (bf16[1024,1024]{1,0:T(8,128)(2,1)}, bf16[1024,1024]{1,0:T(8,128)(2,1)}, u32[]{:S(2)}, u32[]{:S(2)}) collective-permute-start(bf16[1024,1024]{1,0:T(8,128)(2,1)} %get-tuple-element.93), channel_id=1, source_target_pairs={{0,1},{1,0},{2,3},{3,2},{4,5},{5,4},{6,7},{7,6},{8,9},{9,8},{10,11... | collective-permute-start | bytes 6291464 | tf_op jit(solution)/shard_map/ppermute | solution.py:522
  295.5 29.2 %collective-permute-start.10 = (bf16[2,256,1024]{2,1,0:T(8,128)(2,1)S(1)}, bf16[2,256,1024]{2,1,0:T(8,128)(2,1)}, u32[]{:S(2)}, u32[]{:S(2)}) collective-permute-start(bf16[2,256,1024]{2,1,0:T(8,128)(2,1)S(1)} %fusion._), channel_id=1, source_target_pairs={{0,2},{1,3},{2,0},{3,1},{4,6},{5,7},{6,4},{7,5},{8,10},{9,11},{10,... | collective-permute-start | bytes 3145736 | tf_op jit(solution)/shard_map/ppermute | solution.py:406
  299.7 27.4 %collective-permute-start.12 = (bf16[2,256,1024]{2,1,0:T(8,128)(2,1)}, bf16[2,256,1024]{2,1,0:T(8,128)(2,1)}, u32[]{:S(2)}, u32[]{:S(2)}) collective-permute-start(bf16[2,256,1024]{2,1,0:T(8,128)(2,1)} %fusion.1), channel_id=1, source_target_pairs={{0,4},{1,5},{2,6},{3,7},{4,0},{5,1},{6,2},{7,3},{8,12},{9,13},{10,... | collective-permute-start | bytes 3145736 | tf_op jit(solution)/shard_map/ppermute | solution.py:406
  329.7 16.2 %collective-permute-start.13 = (bf16[256,1024]{1,0:T(8,128)(2,1)}, bf16[256,1024]{1,0:T(8,128)(2,1)S(1)}, u32[]{:S(2)}, u32[]{:S(2)}) collective-permute-start(bf16[256,1024]{1,0:T(8,128)(2,1)} %fusion.5), channel_id=1, source_target_pairs={{0,4},{1,5},{2,6},{3,7},{4,0},{5,1},{6,2},{7,3},{8,12},{9,13},{10,... | collective-permute-start | bytes 1572872 | tf_op jit(solution)/shard_map/ppermute | solution.py:406
  330.2 15.7 %collective-permute-start.14 = (bf16[256,1024]{1,0:T(8,128)(2,1)}, bf16[256,1024]{1,0:T(8,128)(2,1)S(1)}, u32[]{:S(2)}, u32[]{:S(2)}) collective-permute-start(bf16[256,1024]{1,0:T(8,128)(2,1)} %fusion.4), channel_id=1, source_target_pairs={{0,2},{1,3},{2,0},{3,1},{4,6},{5,7},{6,4},{7,5},{8,10},{9,11},{10,... | collective-permute-start | bytes 1572872 | tf_op jit(solution)/shard_map/ppermute | solution.py:406
  348.4 7.3 %collective-permute-start.16 = (f32[7680]{0:T(1024)S(1)}, f32[7680]{0:T(1024)S(1)}, u32[]{:S(2)}, u32[]{:S(2)}) collective-permute-start(f32[7680]{0:T(1024)S(1)} %pad_maximum_fusion.1), channel_id=1, source_target_pairs={{0,16},{8,24},{16,0},{24,8},{1,17},{9,25},{17,1},{25,9},{2,18},{10... | collective-permute-start | bytes 92168 | tf_op jit(solution)/shard_map/ppermute | solution.py:430
  349.1 6.6 %collective-permute-start.17 = (f32[7680]{0:T(1024)S(1)}, f32[7680]{0:T(1024)S(1)}, u32[]{:S(2)}, u32[]{:S(2)}) collective-permute-start(f32[7680]{0:T(1024)S(1)} %pad_maximum_fusion.1), channel_id=1, source_target_pairs={{0,24},{8,16},{16,8},{24,0},{1,25},{9,17},{17,9},{25,1},{2,26},{10... | collective-permute-start | bytes 92168 | tf_op jit(solution)/shard_map/ppermute | solution.py:430
  350.1 5.6 %collective-permute-start.15 = (f32[7680]{0:T(1024)S(1)}, f32[7680]{0:T(1024)S(1)}, u32[]{:S(2)}, u32[]{:S(2)}) collective-permute-start(f32[7680]{0:T(1024)S(1)} %pad_maximum_fusion.1), channel_id=1, source_target_pairs={{0,8},{8,0},{16,24},{24,16},{1,9},{9,1},{17,25},{25,17},{2,10},{10... | collective-permute-start | bytes 92168 | tf_op jit(solution)/shard_map/ppermute | solution.py:430
  355.7 3.8 %collective-permute-start.19 = (f32[4096]{0:T(1024)S(1)}, f32[4096]{0:T(1024)S(1)}, u32[]{:S(2)}, u32[]{:S(2)}) collective-permute-start(f32[4096]{0:T(1024)S(1)} %slice.30), channel_id=1, source_target_pairs={{0,2},{1,3},{2,0},{3,1},{4,6},{5,7},{6,4},{7,5},{8,10},{9,11},{10,... | collective-permute-start | bytes 49160 | tf_op jit(solution)/shard_map/ppermute | solution.py:430
  357.2 3.2 collective-permute-start.20
  357.2 3.2 collective-permute-start.18
  360.4 3.8 %collective-permute-start.21 = (f32[4096]{0:T(1024)S(1)}, f32[4096]{0:T(1024)S(1)}, u32[]{:S(2)}, u32[]{:S(2)}) collective-permute-start(f32[4096]{0:T(1024)S(1)} %add_add_fusion.2), channel_id=1, source_target_pairs={{0,4},{1,5},{2,6},{3,7},{4,0},{5,1},{6,2},{7,3},{8,12},{9,13},{10,... | collective-permute-start | bytes 49160 | tf_op jit(solution)/shard_map/ppermute | solution.py:430
  (23 other events, 240.1 us)
Sparse Core Ops, SparseCore 0:
  13.1 57.0 all-gather.1

commit v5 on v4

--- a/solution.py
+++ b/solution.py
@@ -286,10 +286,11 @@
 
 def early_kernel(count, added, *refs):
     total = input_gradient_kernel(count, refs)
-    refs[-1][...] = refs[2 * count][...] + total if added else total
-
-
-def early_input_gradient(cots, weights, total, after):
+    total = refs[2 * count][...].astype(jnp.float32) + total if added else total
+    refs[-1][...] = total.astype(refs[-1].dtype)
+
+
+def early_input_gradient(cots, weights, total, after, dtype=jnp.float32):
     tokens, features = cots[0].shape[0], weights[0].shape[0]
     tile_t, tile_f = largest_tile(tokens, 512), largest_tile(features, 1024)
     width = sum(c.shape[1] for c in cots)
@@ -303,7 +304,7 @@
         + ([] if total is None else [out_spec])
         + [pl.BlockSpec(memory_space=pl.ANY)],
         out_specs=out_spec,
-        out_shape=jax.ShapeDtypeStruct((tokens, features), jnp.float32),
+        out_shape=jax.ShapeDtypeStruct((tokens, features), dtype),
         input_output_aliases={} if total is None else {2 * len(cots): 0},
         compiler_params=pltpu.CompilerParams(vmem_limit_bytes=VMEM),
         cost_estimate=pl.CostEstimate(
@@ -328,7 +329,7 @@
             cot_ref[pl.ds(start, rows // 2), :] = piece[...].reshape(rows // 2, width)
 
     part = lax.dot_general(cot_ref[...], weight_ref[...], (((1,), (1,)), ((), ())), preferred_element_type=jnp.float32)
-    total = (early_ref[...].reshape(part.shape) + part).astype(one_ref.dtype)
+    total = (early_ref[...].reshape(part.shape).astype(jnp.float32) + part).astype(one_ref.dtype)
 
     @pl.when(step < half)
     def _():
@@ -496,7 +497,7 @@
             run_decode(2, gate)
             gate = weights[2]
         if 0 < s < final + 1:
-            early = early_input_gradient(cots[summed:], weights[summed:s], early, gate)
+            early = early_input_gradient(cots[summed:], weights[summed:s], early, gate, jnp.bfloat16)
             summed, gate = s, early
         if s < final:
             gate = rings[s].hold(gate)

time: 373 us -> 372 us (level)
  Pallas kernels: 244 us -> 237 us
  waiting for transfers between devices: 59.7 us -> 65.6 us
    pallas_call x2, Pallas kernels: 42 us -> 35.9 us  [early_input_gradient(): pl.pallas_call(functools.partial(early_kernel, len(cots), total is not No...]
    ppermute x3, waiting for transfers between devices: 23.9 us -> 30.1 us  [finish(): self.pieces.append(lax.ppermute(self.left, 'din', self.forward))]
  transfers between devices with their start and end apart: 23 -> 23, of which waited for: 9 -> 9; matrix products, arithmetic and copies ran while one was open for 5% -> 5% of each run, Pallas kernels for 62% -> 60%
where the time goes in v5:
time: 372 us; the launch traced here: 371 us
  Pallas kernels  237 us (64%)
  waiting for transfers between devices  65.6 us (18%)
  starting transfers between devices  23.7 us (6%)
  other arithmetic  20.3 us (5%)
  between operations  15 us (4%)
  local copies, waits for them, and re-layouts  9.62 us (3%)
    pallas_call x4, Pallas kernels, gradients(): pl.pallas_call(functools.partial(gradient_kernel, n, tile, width, blocks,...  119 us
    pallas_call x3, Pallas kernels, decode(): pl.pallas_call(functools.partial(decode_kernel, tile_groups, unit), grid=...  56.4 us
    pallas_call x2, Pallas kernels, early_input_gradient(): pl.pallas_call(functools.partial(early_kernel, len(cots), total is not No...  35.9 us
    ppermute x3, waiting for transfers between devices, finish(): self.pieces.append(lax.ppermute(self.left, 'din', self.forward))  30.1 us
    pallas_call x2, Pallas kernels, last_input_gradient(): pl.pallas_call(functools.partial(last_kernel, n, rows, len(pieces)), grid...  22.5 us
    ppermute x3, waiting for transfers between devices, begin(): self.left = lax.ppermute(self.left, 'din', self.forward)  18.5 us
    ppermute x3, waiting for transfers between devices, begin(): self.right = lax.ppermute(self.right, 'din', self.backward)  14.1 us
    convert_element_type x4, other arithmetic, exchange(): gives.append(give.astype(jnp.bfloat16))  9.69 us
  transfers between devices with their start and end apart: 23, of which 9 were waited for; matrix products, arithmetic and copies ran while one was open for 5% of the time, Pallas kernels for 60%

profile of v5, /device:TPU:0, one launch (start us, length us, event | category | flops | bytes accessed | tf_op | source)
XLA Modules:
  0.0 371.3 jit_solution(7163647355791244109)
XLA Ops:
  9.1 3.8 %transpose_inputs.1 = bf16[2048,256]{1,0:T(8,128)(2,1)} custom-call(bf16[256,2048]{1,0:T(8,128)(2,1)} %in_ref), custom_call_target="tpu_custom_call" | custom-call | tf_op jit(solution)/shard_map/transpose_inputs/pallas_call | solution.py:151
  12.9 5.1 %collective-permute-start.1 = (bf16[512,1280]{1,0:T(8,128)(2,1)S(1)}, bf16[512,1280]{1,0:T(8,128)(2,1)}, u32[]{:S(2)}, u32[]{:S(2)}) collective-permute-start(bf16[512,1280]{1,0:T(8,128)(2,1)S(1)} %get-tuple-element.67.refs_2_), channel_id=1, source_target_pairs={{8,0},{16,8},{24,16},{0,24},{9,1},{17,9},{25,17},{1,25},{10,2},{18... | collective-permute-start | bytes 3932168 | tf_op jit(solution)/shard_map/ppermute | solution.py:128
  18.0 2.3 slice.24.refs_4_
  24.1 19.0 %decode_weights.5.weight_ref.refs_1_ = bf16[2048,1280]{1,0:T(8,128)(2,1)} custom-call(s32[2,256,3584]{2,1,0:T(8,128)} %refs_1_.3, s32[2,8,128]{2,1,0:T(8,128)} %fusion.12.table_ref, f32[1,3584]{1,0:T(1,128)} %mul.97.coef_ref, f32[1,3584]{1,0:T(1,128)} %reshape.108._.refs_1_.refs_2_.refs_3_), custom_call_target="tpu_custom_call" | custom-call | flops 23592960000 | bytes 7864320 | tf_op jit(solution)/shard_map/decode_weights/pallas_call | solution.py:89
  43.0 19.2 %decode_weights.3._.weight_ref.refs_1_ = bf16[2048,1280]{1,0:T(8,128)(2,1)} custom-call(s32[2,256,3584]{2,1,0:T(8,128)} %refs_1_.3, s32[2,8,128]{2,1,0:T(8,128)} %fusion.12.table_ref, f32[1,3584]{1,0:T(1,128)} %mul.97.coef_ref, f32[1,3584]{1,0:T(1,128)} %reshape.108._.refs_1_.refs_2_.refs_3_), custom_call_target="tpu_custom_call" | custom-call | flops 23592960000 | bytes 7864320 | tf_op jit(solution)/shard_map/decode_weights/pallas_call | solution.py:89
  62.2 12.9 %collective-permute-done.refs_3_ = bf16[512,1280]{1,0:T(8,128)(2,1)} collective-permute-done((bf16[512,1280]{1,0:T(8,128)(2,1)S(1)}, bf16[512,1280]{1,0:T(8,128)(2,1)}, u32[]{:S(2)}, u32[]{:S(2)}) %collective-permute-start) | collective-permute-done | bytes 1310752 | tf_op jit(solution)/shard_map/ppermute | solution.py:127
  76.8 18.3 %decode_weights.4._.weight_ref = bf16[2048,1024]{1,0:T(8,128)(2,1)} custom-call(s32[2,256,3584]{2,1,0:T(8,128)} %refs_1_.3, s32[2,8,128]{2,1,0:T(8,128)} %fusion.12.table_ref, f32[1,3584]{1,0:T(1,128)} %mul.97.coef_ref, bf16[2048,1280]{1,0:T(8,128)(2,1)} %decode_weights.3._.weight_ref.refs_1_), custom_call_target="tpu_custom_call" | custom-call | flops 18874368000 | bytes 6291456 | tf_op jit(solution)/shard_map/decode_weights/pallas_call | solution.py:89
  95.0 11.8 %collective-permute-done.2.refs_5_ = bf16[512,1280]{1,0:T(8,128)(2,1)S(1)} collective-permute-done((bf16[512,1280]{1,0:T(8,128)(2,1)}, bf16[512,1280]{1,0:T(8,128)(2,1)S(1)}, u32[]{:S(2)}, u32[]{:S(2)}) %collective-permute-start.2) | collective-permute-done | bytes 1310752 | tf_op jit(solution)/shard_map/ppermute | solution.py:141
  109.9 40.7 %weight_gradients.4 = (bf16[2048,1280]{1,0:T(8,128)(2,1)}, f32[2,64,256]{2,1,0:T(8,128)}, f32[8,1280]{1,0:T(8,128)}) custom-call(s32[1]{0:T(128)} %bitcast.me_ref, bf16[8,2048,256]{2,1,0:T(8,128)(2,1)} %bitcast.54, bf16[2048,1280]{1,0:T(8,128)(2,1)} %decode_weights.5.weight_ref.refs_1_, bf16[2048,1024]{1,0:T(8,128)(2,1)} %decode_weights.4._.weight_ref, ...), custom_call_target="tpu_custom_call" | custom-call | flops 48318382080 | bytes 15728640 | tf_op jit(solution)/shard_map/weight_gradients/pallas_call | solution.py:255
  150.6 14.1 %collective-permute-done.4.refs_4_ = bf16[512,1280]{1,0:T(8,128)(2,1)S(1)} collective-permute-done((bf16[512,1280]{1,0:T(8,128)(2,1)S(1)}, bf16[512,1280]{1,0:T(8,128)(2,1)S(1)}, u32[]{:S(2)}, u32[]{:S(2)}) %collective-permute-start.4) | collective-permute-done | bytes 1310752 | tf_op jit(solution)/shard_map/ppermute | solution.py:128
  165.1 17.0 %early_input_gradient.2._.refs_2_ = bf16[2048,2048]{1,0:T(8,128)(2,1)} custom-call(bf16[2048,1280]{1,0:T(8,128)(2,1)} %get-tuple-element.75.refs_0_, bf16[2048,1280]{1,0:T(8,128)(2,1)} %decode_weights.5.weight_ref.refs_1_, f32[8,1280]{1,0:T(8,128)} %get-tuple-element.76.refs_2_), custom_call_target="tpu_custom_call" | custom-call | flops 16106127360 | bytes 27262976 | tf_op jit(solution)/shard_map/early_input_gradient/pallas_call | solution.py:299
  182.2 12.1 %collective-permute-done.5.refs_5_ = bf16[512,1280]{1,0:T(8,128)(2,1)S(1)} collective-permute-done((bf16[512,1280]{1,0:T(8,128)(2,1)}, bf16[512,1280]{1,0:T(8,128)(2,1)S(1)}, u32[]{:S(2)}, u32[]{:S(2)}) %collective-permute-start.5) | collective-permute-done | bytes 1310752 | tf_op jit(solution)/shard_map/ppermute | solution.py:141
  194.3 2.3 collective-permute-start.7
  196.6 40.9 %weight_gradients.5 = (bf16[2048,1280]{1,0:T(8,128)(2,1)}, f32[2,64,256]{2,1,0:T(8,128)}, f32[8,1280]{1,0:T(8,128)}) custom-call(s32[1]{0:T(128)} %bitcast.me_ref, bf16[8,2048,256]{2,1,0:T(8,128)(2,1)} %bitcast.55, bf16[2048,1280]{1,0:T(8,128)(2,1)} %decode_weights.3._.weight_ref.refs_1_, bf16[2048,2048]{1,0:T(8,128)(2,1)} %early_input_gradient.2._.refs_2_, ...), custom_call_target="tpu_custom_call" | custom-call | flops 48318382080 | bytes 15728640 | tf_op jit(solution)/shard_map/weight_gradients/pallas_call | solution.py:255
  237.5 5.6 %collective-permute-done.6.refs_5_ = bf16[512,1024]{1,0:T(8,128)(2,1)S(1)} collective-permute-done((bf16[512,1024]{1,0:T(8,128)(2,1)S(1)}, bf16[512,1024]{1,0:T(8,128)(2,1)S(1)}, u32[]{:S(2)}, u32[]{:S(2)}) %collective-permute-start.6) | collective-permute-done | bytes 1048608 | tf_op jit(solution)/shard_map/ppermute | solution.py:127
  243.2 18.9 %early_input_gradient.3 = bf16[2048,2048]{1,0:T(8,128)(2,1)} custom-call(bf16[2048,1280]{1,0:T(8,128)(2,1)} %get-tuple-element.83.refs_0_, bf16[2048,1280]{1,0:T(8,128)(2,1)} %decode_weights.3._.weight_ref.refs_1_, bf16[2048,2048]{1,0:T(8,128)(2,1)} %early_input_gradient.2._.refs_2_, f32[8,1280]{1,0:T(8,128)} %get-tuple-element.86.refs_3_), custom_call_target="tpu_custom_call", output_to_operand_aliasing={{}: (2, {})} | custom-call | flops 16106127360 | bytes 27262976 | tf_op jit(solution)/shard_map/early_input_gradient/pallas_call | solution.py:299
  262.0 6.1 %collective-permute-done.8.refs_7_ = bf16[512,1024]{1,0:T(8,128)(2,1)S(1)} collective-permute-done((bf16[512,1024]{1,0:T(8,128)(2,1)S(1)}, bf16[512,1024]{1,0:T(8,128)(2,1)S(1)}, u32[]{:S(2)}, u32[]{:S(2)}) %collective-permute-start.8) | collective-permute-done | bytes 1048608 | tf_op jit(solution)/shard_map/ppermute | solution.py:141
  269.1 10.7 %last_input_gradient.3 = (bf16[1024,1024]{1,0:T(8,128)(2,1)}, bf16[1024,1024]{1,0:T(8,128)(2,1)}) custom-call(s32[2]{0:T(128)} %get-tuple-element.146.me_ref, bf16[4,2,256,2048]{3,2,1,0:T(8,128)(2,1)} %bitcast.64, bf16[2048,1024]{1,0:T(8,128)(2,1)} %decode_weights.4._.weight_ref, bf16[1,2,256,1024]{3,2,1,0:T(8,128)(2,1)} %bitcast.51, ...), custom_call_target="tpu_custom_call" | custom-call | flops 8589934592 | bytes 12582912 | tf_op jit(solution)/shard_map/last_input_gradient/pallas_call | solution.py:350
  280.4 11.8 %last_input_gradient.2 = (f32[1024,1024]{1,0:T(8,128)}, f32[1024,1024]{1,0:T(8,128)}) custom-call(s32[2]{0:T(128)} %get-tuple-element.145.me_ref, bf16[4,2,256,2048]{3,2,1,0:T(8,128)(2,1)} %bitcast.65, bf16[2048,1024]{1,0:T(8,128)(2,1)} %decode_weights.4._.weight_ref, bf16[1,2,256,1024]{3,2,1,0:T(8,128)(2,1)} %bitcast.52, ...), custom_call_target="tpu_custom_call" | custom-call | flops 8589934592 | bytes 12582912 | tf_op jit(solution)/shard_map/last_input_gradient/pallas_call | solution.py:350
  295.9 2.6 fusion.1
  300.0 22.7 %weight_gradients.6 = (bf16[2048,1024]{1,0:T(8,128)(2,1)}, f32[2,64,256]{2,1,0:T(8,128)}, f32[8,1024]{1,0:T(8,128)}) custom-call(s32[1]{0:T(128)} %bitcast.me_ref, bf16[8,2048,256]{2,1,0:T(8,128)(2,1)} %bitcast.56, bf16[2048,1024]{1,0:T(8,128)(2,1)} %decode_weights.4._.weight_ref, bf16[2,256,1024]{2,1,0:T(8,128)(2,1)} %copy-done.3, s32[2,256,3584]{2,1,0:T(8,128)} %refs_1_.3, ...), custom_call_target="tpu_custom_call" | custom-call | flops 24159191040 | bytes 7864320 | tf_op jit(solution)/shard_map/weight_gradients/pallas_call | solution.py:255
  323.5 2.4 fusion.5
  325.9 2.5 fusion.4
  329.6 14.2 %weight_gradients.7 = (f32[2,64,256]{2,1,0:T(8,128)}, f32[8,1024]{1,0:T(8,128)}) custom-call(s32[1]{0:T(128)} %bitcast.me_ref, bf16[8,2048,256]{2,1,0:T(8,128)(2,1)} %bitcast.57, bf16[2048,1024]{1,0:T(8,128)(2,1)} %decode_weights.4._.weight_ref, f32[8,1024]{1,0:T(8,128)} %get-tuple-element.98._, s32[2,256,3584]{2,1,0:T(8,128)} %refs_1_.3, ...), custom_call_target="tpu_custom_call" | custom-call | flops 14495514624 | bytes 4718592 | tf_op jit(solution)/shard_map/weight_gradients/pallas_call | solution.py:255
  (123 shorter events, 39.3 us)
Async XLA Ops:
  7.2 102.7 %all-gather.2.cloned.1.call-start = ((), (), s32[]{:S(2)}) async-start(), calls=%async_computation | async-start | bytes 9437184 | tf_op jit(solution)/shard_map/all_gather | solution.py:482
  9.1 98.8 %copy-start.1 = (bf16[512,1280]{1,0:T(8,128)(2,1)}, bf16[512,1280]{1,0:T(8,128)(2,1)S(1)}, u32[]{:S(2)}) copy-start(bf16[512,1280]{1,0:T(8,128)(2,1)S(1)} %get-tuple-element.79.refs_2_) | copy-start | bytes 3932164
  12.9 49.3 %collective-permute-start.1 = (bf16[512,1280]{1,0:T(8,128)(2,1)S(1)}, bf16[512,1280]{1,0:T(8,128)(2,1)}, u32[]{:S(2)}, u32[]{:S(2)}) collective-permute-start(bf16[512,1280]{1,0:T(8,128)(2,1)S(1)} %get-tuple-element.67.refs_2_), channel_id=1, source_target_pairs={{8,0},{16,8},{24,16},{0,24},{9,1},{17,9},{25,17},{1,25},{10,2},{18... | collective-permute-start | bytes 3932168 | tf_op jit(solution)/shard_map/ppermute | solution.py:128
  18.0 57.1 %collective-permute-start = (bf16[512,1280]{1,0:T(8,128)(2,1)S(1)}, bf16[512,1280]{1,0:T(8,128)(2,1)}, u32[]{:S(2)}, u32[]{:S(2)}) collective-permute-start(bf16[512,1280]{1,0:T(8,128)(2,1)S(1)} %get-tuple-element.67.refs_2_), channel_id=1, source_target_pairs={{0,8},{8,16},{16,24},{24,0},{1,9},{9,17},{17,25},{25,1},{2,10},{10... | collective-permute-start | bytes 3932168 | tf_op jit(solution)/shard_map/ppermute | solution.py:127
  75.2 31.7 %collective-permute-start.2 = (bf16[512,1280]{1,0:T(8,128)(2,1)}, bf16[512,1280]{1,0:T(8,128)(2,1)S(1)}, u32[]{:S(2)}, u32[]{:S(2)}) collective-permute-start(bf16[512,1280]{1,0:T(8,128)(2,1)} %collective-permute-done.refs_3_), channel_id=1, source_target_pairs={{0,8},{8,16},{16,24},{24,0},{1,9},{9,17},{17,25},{25,1},{2,10},{10... | collective-permute-start | bytes 3932168 | tf_op jit(solution)/shard_map/ppermute | solution.py:141
  107.9 56.8 %collective-permute-start.4 = (bf16[512,1280]{1,0:T(8,128)(2,1)S(1)}, bf16[512,1280]{1,0:T(8,128)(2,1)S(1)}, u32[]{:S(2)}, u32[]{:S(2)}) collective-permute-start(bf16[512,1280]{1,0:T(8,128)(2,1)S(1)} %get-tuple-element.79.refs_2_), channel_id=1, source_target_pairs={{8,0},{16,8},{24,16},{0,24},{9,1},{17,9},{25,17},{1,25},{10,2},{18... | collective-permute-start | bytes 3932168 | tf_op jit(solution)/shard_map/ppermute | solution.py:128
  107.9 56.8 %collective-permute-start.3 = (bf16[512,1280]{1,0:T(8,128)(2,1)S(1)}, bf16[512,1280]{1,0:T(8,128)(2,1)}, u32[]{:S(2)}, u32[]{:S(2)}) collective-permute-start(bf16[512,1280]{1,0:T(8,128)(2,1)S(1)} %get-tuple-element.79.refs_2_), channel_id=1, source_target_pairs={{0,8},{8,16},{16,24},{24,0},{1,9},{9,17},{17,25},{25,1},{2,10},{10... | collective-permute-start | bytes 3932168 | tf_op jit(solution)/shard_map/ppermute | solution.py:127
  164.7 29.6 %collective-permute-start.5 = (bf16[512,1280]{1,0:T(8,128)(2,1)}, bf16[512,1280]{1,0:T(8,128)(2,1)S(1)}, u32[]{:S(2)}, u32[]{:S(2)}) collective-permute-start(bf16[512,1280]{1,0:T(8,128)(2,1)} %collective-permute-done.3.refs_3_), channel_id=1, source_target_pairs={{0,8},{8,16},{16,24},{24,0},{1,9},{9,17},{17,25},{25,1},{2,10},{10... | collective-permute-start | bytes 3932168 | tf_op jit(solution)/shard_map/ppermute | solution.py:141
  194.3 43.2 %collective-permute-start.7 = (bf16[512,1024]{1,0:T(8,128)(2,1)S(1)}, bf16[512,1024]{1,0:T(8,128)(2,1)S(1)}, u32[]{:S(2)}, u32[]{:S(2)}) collective-permute-start(bf16[512,1024]{1,0:T(8,128)(2,1)S(1)} %copy-done.4), channel_id=1, source_target_pairs={{8,0},{16,8},{24,16},{0,24},{9,1},{17,9},{25,17},{1,25},{10,2},{18... | collective-permute-start | bytes 3145736 | tf_op jit(solution)/shard_map/ppermute | solution.py:128
  196.6 46.4 %collective-permute-start.6 = (bf16[512,1024]{1,0:T(8,128)(2,1)S(1)}, bf16[512,1024]{1,0:T(8,128)(2,1)S(1)}, u32[]{:S(2)}, u32[]{:S(2)}) collective-permute-start(bf16[512,1024]{1,0:T(8,128)(2,1)S(1)} %copy-done.4), channel_id=1, source_target_pairs={{0,8},{8,16},{16,24},{24,0},{1,9},{9,17},{17,25},{25,1},{2,10},{10... | collective-permute-start | bytes 3145736 | tf_op jit(solution)/shard_map/ppermute | solution.py:127
  243.0 25.1 %collective-permute-start.8 = (bf16[512,1024]{1,0:T(8,128)(2,1)S(1)}, bf16[512,1024]{1,0:T(8,128)(2,1)S(1)}, u32[]{:S(2)}, u32[]{:S(2)}) collective-permute-start(bf16[512,1024]{1,0:T(8,128)(2,1)S(1)} %collective-permute-done.6.refs_5_), channel_id=1, source_target_pairs={{0,8},{8,16},{16,24},{24,0},{1,9},{9,17},{17,25},{25,1},{2,10},{10... | collective-permute-start | bytes 3145736 | tf_op jit(solution)/shard_map/ppermute | solution.py:141
  279.8 12.4 %collective-permute-start.9 = (bf16[1024,1024]{1,0:T(8,128)(2,1)}, bf16[1024,1024]{1,0:T(8,128)(2,1)S(1)}, u32[]{:S(2)}, u32[]{:S(2)}) collective-permute-start(bf16[1024,1024]{1,0:T(8,128)(2,1)} %get-tuple-element.91), channel_id=1, source_target_pairs={{0,1},{1,0},{2,3},{3,2},{4,5},{5,4},{6,7},{7,6},{8,9},{9,8},{10,11... | collective-permute-start | bytes 6291464 | tf_op jit(solution)/shard_map/ppermute | solution.py:523
  279.8 16.1 %collective-permute-start.11 = (bf16[1024,1024]{1,0:T(8,128)(2,1)}, bf16[1024,1024]{1,0:T(8,128)(2,1)}, u32[]{:S(2)}, u32[]{:S(2)}) collective-permute-start(bf16[1024,1024]{1,0:T(8,128)(2,1)} %get-tuple-element.93), channel_id=1, source_target_pairs={{0,1},{1,0},{2,3},{3,2},{4,5},{5,4},{6,7},{7,6},{8,9},{9,8},{10,11... | collective-permute-start | bytes 6291464 | tf_op jit(solution)/shard_map/ppermute | solution.py:523
  294.3 29.2 %collective-permute-start.10 = (bf16[2,256,1024]{2,1,0:T(8,128)(2,1)S(1)}, bf16[2,256,1024]{2,1,0:T(8,128)(2,1)}, u32[]{:S(2)}, u32[]{:S(2)}) collective-permute-start(bf16[2,256,1024]{2,1,0:T(8,128)(2,1)S(1)} %fusion._), channel_id=1, source_target_pairs={{0,2},{1,3},{2,0},{3,1},{4,6},{5,7},{6,4},{7,5},{8,10},{9,11},{10,... | collective-permute-start | bytes 3145736 | tf_op jit(solution)/shard_map/ppermute | solution.py:407
  298.5 27.4 %collective-permute-start.12 = (bf16[2,256,1024]{2,1,0:T(8,128)(2,1)}, bf16[2,256,1024]{2,1,0:T(8,128)(2,1)}, u32[]{:S(2)}, u32[]{:S(2)}) collective-permute-start(bf16[2,256,1024]{2,1,0:T(8,128)(2,1)} %fusion.1), channel_id=1, source_target_pairs={{0,4},{1,5},{2,6},{3,7},{4,0},{5,1},{6,2},{7,3},{8,12},{9,13},{10,... | collective-permute-start | bytes 3145736 | tf_op jit(solution)/shard_map/ppermute | solution.py:407
  328.5 16.2 %collective-permute-start.13 = (bf16[256,1024]{1,0:T(8,128)(2,1)}, bf16[256,1024]{1,0:T(8,128)(2,1)S(1)}, u32[]{:S(2)}, u32[]{:S(2)}) collective-permute-start(bf16[256,1024]{1,0:T(8,128)(2,1)} %fusion.5), channel_id=1, source_target_pairs={{0,4},{1,5},{2,6},{3,7},{4,0},{5,1},{6,2},{7,3},{8,12},{9,13},{10,... | collective-permute-start | bytes 1572872 | tf_op jit(solution)/shard_map/ppermute | solution.py:407
  329.0 15.7 %collective-permute-start.14 = (bf16[256,1024]{1,0:T(8,128)(2,1)}, bf16[256,1024]{1,0:T(8,128)(2,1)S(1)}, u32[]{:S(2)}, u32[]{:S(2)}) collective-permute-start(bf16[256,1024]{1,0:T(8,128)(2,1)} %fusion.4), channel_id=1, source_target_pairs={{0,2},{1,3},{2,0},{3,1},{4,6},{5,7},{6,4},{7,5},{8,10},{9,11},{10,... | collective-permute-start | bytes 1572872 | tf_op jit(solution)/shard_map/ppermute | solution.py:407
  347.2 7.3 %collective-permute-start.16 = (f32[7680]{0:T(1024)S(1)}, f32[7680]{0:T(1024)S(1)}, u32[]{:S(2)}, u32[]{:S(2)}) collective-permute-start(f32[7680]{0:T(1024)S(1)} %pad_maximum_fusion.1), channel_id=1, source_target_pairs={{0,16},{8,24},{16,0},{24,8},{1,17},{9,25},{17,1},{25,9},{2,18},{10... | collective-permute-start | bytes 92168 | tf_op jit(solution)/shard_map/ppermute | solution.py:431
  347.9 6.6 %collective-permute-start.17 = (f32[7680]{0:T(1024)S(1)}, f32[7680]{0:T(1024)S(1)}, u32[]{:S(2)}, u32[]{:S(2)}) collective-permute-start(f32[7680]{0:T(1024)S(1)} %pad_maximum_fusion.1), channel_id=1, source_target_pairs={{0,24},{8,16},{16,8},{24,0},{1,25},{9,17},{17,9},{25,1},{2,26},{10... | collective-permute-start | bytes 92168 | tf_op jit(solution)/shard_map/ppermute | solution.py:431
  348.9 5.6 %collective-permute-start.15 = (f32[7680]{0:T(1024)S(1)}, f32[7680]{0:T(1024)S(1)}, u32[]{:S(2)}, u32[]{:S(2)}) collective-permute-start(f32[7680]{0:T(1024)S(1)} %pad_maximum_fusion.1), channel_id=1, source_target_pairs={{0,8},{8,0},{16,24},{24,16},{1,9},{9,1},{17,25},{25,17},{2,10},{10... | collective-permute-start | bytes 92168 | tf_op jit(solution)/shard_map/ppermute | solution.py:431
  354.5 3.8 %collective-permute-start.19 = (f32[4096]{0:T(1024)S(1)}, f32[4096]{0:T(1024)S(1)}, u32[]{:S(2)}, u32[]{:S(2)}) collective-permute-start(f32[4096]{0:T(1024)S(1)} %slice.30), channel_id=1, source_target_pairs={{0,2},{1,3},{2,0},{3,1},{4,6},{5,7},{6,4},{7,5},{8,10},{9,11},{10,... | collective-permute-start | bytes 49160 | tf_op jit(solution)/shard_map/ppermute | solution.py:431
  356.0 3.2 collective-permute-start.20
  356.0 3.2 collective-permute-start.18
  359.2 3.8 %collective-permute-start.21 = (f32[4096]{0:T(1024)S(1)}, f32[4096]{0:T(1024)S(1)}, u32[]{:S(2)}, u32[]{:S(2)}) collective-permute-start(f32[4096]{0:T(1024)S(1)} %add_add_fusion.2), channel_id=1, source_target_pairs={{0,4},{1,5},{2,6},{3,7},{4,0},{5,1},{6,2},{7,3},{8,12},{9,13},{10,... | collective-permute-start | bytes 49160 | tf_op jit(solution)/shard_map/ppermute | solution.py:431
  (23 other events, 228.7 us)
Sparse Core Ops, SparseCore 0:
  13.1 57.0 all-gather.1
